TPU v7x, 32 devices: a whole 2x2x4 slice. The times are simulated.
32 devices in a mesh: dev: 4 (over y, x), gx: 4 (over z), gy: 2 (over core).
Axes of the slice: x: 2, y: 2, z: 4, core: 2. Of those that a mesh axis runs over, the one named last changes fastest.
Arguments:
- tokens: bfloat16 [4096, 1024], P(('dev', 'gy'), 'gx'), may hold values from -6 to 6
- norm_gain: bfloat16 [1024], P('gx'), may hold values from 0.099609375 to 1.8984375
- w_query: bfloat16 [1024, 2048], P('gy', 'gx'), may hold values from -0.1875 to 0.1875
- key_projection: bfloat16 [1024, 1024], P('gy', 'gx'), may hold values from -0.1875 to 0.1875
- value_projection: bfloat16 [1024, 1024], P('gy', 'gx'), may hold values from -0.1875 to 0.1875
- query_gain: bfloat16 [128], replicated, may hold values from 0.099609375 to 1.8984375
- key_gain: bfloat16 [128], replicated, may hold values from 0.099609375 to 1.8984375
- w_out: bfloat16 [2048, 1024], P('gx', 'gy'), may hold values from -0.5 to 0.5
- ffn_gain: bfloat16 [1024], P('gx'), may hold values from 0.099609375 to 1.8984375
- w_gate: bfloat16 [1024, 3072], P('gy', 'gx'), may hold values from -0.1875 to 0.1875
- w_up: bfloat16 [1024, 3072], P('gy', 'gx'), may hold values from -0.1875 to 0.1875
- w_down: bfloat16 [3072, 1024], P('gx', 'gy'), may hold values from -0.109375 to 0.109375
- cotangent: bfloat16 [4096, 1024], P(('dev', 'gy'), 'gx'), may hold values from -6 to 6
- sequence: int32 [4096], P('dev'), may hold values from 0 to 1, as said below
- position: int32 [4096], P('dev'), may hold values from 0 to 959, as said below
Outputs:
- output: bfloat16 [4096, 1024], P(('dev', 'gy'), 'gx')
- grad_tokens: float32 [4096, 1024], P(('dev', 'gy'), 'gx')
- grad_norm_gain: float32 [1024], P('gx')
- grad_query: float32 [1024, 2048], P('gy', 'gx')
- grad_key: float32 [1024, 1024], P('gy', 'gx')
- grad_value: float32 [1024, 1024], P('gy', 'gx')
- grad_query_gain: float32 [128], replicated
- grad_key_gain: float32 [128], replicated
- grad_out: float32 [2048, 1024], P('gx', 'gy')
- grad_ffn_gain: float32 [1024], P('gx')
- grad_gate: float32 [1024, 3072], P('gy', 'gx')
- grad_up: float32 [1024, 3072], P('gy', 'gx')
- grad_down: float32 [3072, 1024], P('gx', 'gy')
Inputs may be any that keep to these rules, and one draw needn't show every extreme that they name: Each index of dev holds a block of 1024 tokens read as a stream: token t of the stream lies in row (t mod g) * 512 + floor(t / g) of the block, g = 2. Along the stream the numbers start at 0 and rise by one at each new sequence. One sequence of each block has 960 tokens; every other one has 64 tokens. `position`: the place of each token in its sequence along the stream, 0 at its first token.
All inputs are finite; a program needn't handle non-finite values.
Results may differ from a plain program's by a relative error of at most 0.024.
Values may be sent and summed in bfloat16 or wider, within the bound.
No kernel may reach another device: no remote copies, remote signals or barrier semaphores. Data moves between devices by JAX's collectives and lax.ppermute only.
A program may use at most 256 MiB of HBM per device.

v0:
```python
import jax
import jax.numpy as jnp
from jax import lax
from jax.sharding import PartitionSpec as P

EPS = 1e-06
THETA = 1000000.0
NEGATIVE = -1e30


def head_norm(value_vectors, gain):
    return (
        value_vectors
        * lax.rsqrt(jnp.mean(value_vectors * value_vectors, axis=-1, keepdims=True) + EPS)
        * gain
    )


def rotate(value_vectors, cosine, sine):
    half = value_vectors.shape[-1] // 2
    turned = jnp.concatenate([-value_vectors[..., half:], value_vectors[..., :half]], axis=-1)
    return value_vectors * cosine + turned * sine


def angles(position, size):
    rates = THETA ** (-(jnp.arange(size // 2, dtype=jnp.float32) * 2.0) / size)
    phase = position.astype(jnp.float32)[:, None] * rates[None, :]
    phase = jnp.concatenate([phase, phase], axis=-1)
    return (jnp.cos(phase)[:, None, :], jnp.sin(phase)[:, None, :])


def contract_rows(left, right):
    return lax.dot_general(
        left, right, (((0,), (0,)), ((), ())), preferred_element_type=jnp.float32
    )


def contract_cols(left, right):
    return lax.dot_general(
        left, right, (((1,), (1,)), ((), ())), preferred_element_type=jnp.float32
    )


def row_stats(parts):
    return lax.psum(parts, "gx")


def row_pieces(block):
    return lax.all_gather(block, "gx", axis=1, tiled=True)


def head_sums(term):
    return lax.psum_scatter(
        term.astype(jnp.bfloat16), "gx", scatter_dimension=1, tiled=True
    ).astype(jnp.float32)


def keys_fold(function, start_value, key_rows, value_rows):
    return function(
        start_value,
        (
            lax.all_gather(key_rows, "gy", axis=0, tiled=True),
            lax.all_gather(value_rows, "gy", axis=0, tiled=True),
        ),
        jnp.int32(0),
    )


def per_device(
    tokens,
    norm_gain,
    w_query,
    key_projection,
    value_projection,
    query_gain,
    key_gain,
    w_out,
    ffn_gain,
    w_gate,
    w_up,
    w_down,
    cotangent,
    sequence,
    position,
):
    rows = tokens.shape[0]
    width = tokens.shape[1] * lax.axis_size("gx")
    head_size = query_gain.shape[0]
    query_heads = w_query.shape[1] // head_size
    kv_heads = key_projection.shape[1] // head_size
    query_group_ratio = query_heads // kv_heads
    factor = head_size ** (-0.5)
    offset = lax.axis_index("gy") * rows
    own_seq = lax.dynamic_slice_in_dim(sequence, offset, rows)
    own_pos = lax.dynamic_slice_in_dim(position, offset, rows)
    cosine, sine = angles(own_pos, head_size)
    full_query, full_key, full_value, full_gate, full_up = (
        lax.all_gather(w_query, "gy", axis=0, tiled=True),
        lax.all_gather(key_projection, "gy", axis=0, tiled=True),
        lax.all_gather(value_projection, "gy", axis=0, tiled=True),
        lax.all_gather(w_gate, "gy", axis=0, tiled=True),
        lax.all_gather(w_up, "gy", axis=0, tiled=True),
    )
    full_out, full_down = (
        lax.all_gather(w_out, "gy", axis=1, tiled=True),
        lax.all_gather(w_down, "gy", axis=1, tiled=True),
    )
    gain_one = norm_gain.astype(jnp.float32)
    gain_two = ffn_gain.astype(jnp.float32)
    query_scale = query_gain.astype(jnp.float32)
    key_scale = key_gain.astype(jnp.float32)
    inputs = tokens.astype(jnp.float32)
    (square_one,) = row_stats((jnp.sum(inputs * inputs, axis=1),))
    scale_one = lax.rsqrt(square_one / width + EPS)[:, None]
    normed_one = row_pieces((inputs * scale_one * gain_one).astype(jnp.bfloat16))
    query_lin = jnp.dot(normed_one, full_query, preferred_element_type=jnp.float32)
    key_lin = jnp.dot(normed_one, full_key, preferred_element_type=jnp.float32)
    value_lin = jnp.dot(normed_one, full_value, preferred_element_type=jnp.float32)

    def positional(query_in, key_in, query_weight, key_matrix):
        query_rot = rotate(
            head_norm(query_in.reshape(rows, query_heads, head_size), query_weight), cosine, sine
        )
        key_rot = rotate(
            head_norm(key_in.reshape(rows, kv_heads, head_size), key_matrix), cosine, sine
        )
        return (query_rot, key_rot)

    (query_rot, key_rot), positional_back = jax.vjp(
        positional, query_lin, key_lin, query_scale, key_scale
    )
    query_bf = query_rot.astype(jnp.bfloat16).reshape(rows, kv_heads, query_group_ratio, head_size)
    key_bf = key_rot.astype(jnp.bfloat16)
    value_bf = value_lin.astype(jnp.bfloat16).reshape(rows, kv_heads, head_size)

    def key_mask():
        return ((own_seq[:, None] == sequence[None, :]) & (position[None, :] <= own_pos[:, None]))[
            None, None
        ]

    def forward_fold(carry, pieces, start):
        running, total, accum = carry
        key_piece, value_piece = pieces
        visible = key_mask()
        scores = (
            jnp.einsum("qkgd,jkd->kgqj", query_bf, key_piece, preferred_element_type=jnp.float32)
            * factor
        )
        scores = jnp.where(visible, scores, NEGATIVE)
        newest = jnp.maximum(running, jnp.max(scores, axis=-1))
        weights = jnp.where(visible, jnp.exp(scores - newest[..., None]), 0.0)
        total = jnp.sum(weights, axis=-1)
        accum = jnp.einsum(
            "kgqj,jkd->kgqd",
            weights.astype(jnp.bfloat16),
            value_piece,
            preferred_element_type=jnp.float32,
        )
        return (newest, total, accum)

    stat_zero = jnp.zeros((kv_heads, query_group_ratio, rows), jnp.float32)
    start_state = (
        jnp.full((kv_heads, query_group_ratio, rows), NEGATIVE, jnp.float32),
        stat_zero,
        jnp.zeros((kv_heads, query_group_ratio, rows, head_size), jnp.float32),
    )
    running, total, accum = keys_fold(forward_fold, start_state, key_bf, value_bf)
    attended = accum / total[..., None]
    log_total = running + jnp.log(total)
    mixed_bf = (
        jnp.transpose(attended, (2, 0, 1, 3))
        .reshape(rows, query_heads * head_size)
        .astype(jnp.bfloat16)
    )
    hidden = inputs + head_sums(jnp.dot(mixed_bf, full_out, preferred_element_type=jnp.float32))
    (square_two,) = row_stats((jnp.sum(hidden * hidden, axis=1),))
    scale_two = lax.rsqrt(square_two / width + EPS)[:, None]
    normed_two = row_pieces((hidden * scale_two * gain_two).astype(jnp.bfloat16))
    gate = jnp.dot(normed_two, full_gate, preferred_element_type=jnp.float32)
    up_lin = jnp.dot(normed_two, full_up, preferred_element_type=jnp.float32)

    def swish(gate_in, up_in):
        return jax.nn.silu(gate_in) * up_in

    product, swish_back = jax.vjp(swish, gate, up_lin)
    product_bf = product.astype(jnp.bfloat16)
    result = hidden + head_sums(jnp.dot(product_bf, full_down, preferred_element_type=jnp.float32))
    grad_result = cotangent.astype(jnp.float32)
    grad_rows = row_pieces(cotangent)
    down_grad = contract_rows(grad_rows, product_bf)
    grad_product = contract_cols(grad_rows, full_down)
    grad_gate_lin, grad_up_lin = swish_back(grad_product)
    gate_bf = grad_gate_lin.astype(jnp.bfloat16)
    up_bf = grad_up_lin.astype(jnp.bfloat16)
    gate_grad = contract_rows(normed_two, gate_bf)
    up_grad = contract_rows(normed_two, up_bf)
    grad_normed_two = head_sums(contract_cols(gate_bf, full_gate) + contract_cols(up_bf, full_up))
    (inner_two,) = row_stats((jnp.sum(hidden * gain_two * grad_normed_two, axis=1),))
    grad_hidden = (
        grad_result
        + scale_two * gain_two * grad_normed_two
        - hidden * scale_two**3 * (inner_two / width)[:, None]
    )
    gain_two_part = jnp.sum(grad_normed_two * hidden * scale_two, axis=0)
    branch_rows = row_pieces(grad_hidden.astype(jnp.bfloat16))
    out_grad = contract_rows(branch_rows, mixed_bf)
    grad_mixed_bf = contract_cols(branch_rows, full_out).astype(jnp.bfloat16)
    grad_heads = grad_mixed_bf.reshape(rows, kv_heads, query_group_ratio, head_size)
    delta = jnp.sum(jnp.transpose(grad_heads.astype(jnp.float32), (1, 2, 0, 3)) * attended, axis=-1)

    def query_fold(grad_query, pieces, start):
        key_piece, value_piece = pieces
        visible = key_mask()
        scores = (
            jnp.einsum("qkgd,jkd->kgqj", query_bf, key_piece, preferred_element_type=jnp.float32)
            * factor
        )
        probs = jnp.where(visible, jnp.exp(scores - log_total[..., None]), 0.0)
        grad_probs = jnp.einsum(
            "qkgd,jkd->kgqj", grad_heads, value_piece, preferred_element_type=jnp.float32
        )
        grad_scores = (probs * (grad_probs - delta[..., None])).astype(jnp.bfloat16)
        return factor * jnp.einsum(
            "kgqj,jkd->kgqd", grad_scores, key_piece, preferred_element_type=jnp.float32
        )

    grad_query_heads = keys_fold(
        query_fold,
        jnp.zeros((kv_heads, query_group_ratio, rows, head_size), jnp.float32),
        key_bf,
        value_bf,
    )
    log_rows = jnp.transpose(log_total, (2, 0, 1)).reshape(rows, query_heads)
    delta_rows = jnp.transpose(delta, (2, 0, 1)).reshape(rows, query_heads)
    all_log, all_delta = (
        lax.all_gather(log_rows, "gy", axis=0, tiled=True),
        lax.all_gather(delta_rows, "gy", axis=0, tiled=True),
    )
    query_piece = lax.all_gather(query_bf, "gy", axis=0, tiled=True)
    grad_piece = lax.all_gather(grad_heads, "gy", axis=0, tiled=True)
    count = query_piece.shape[0]
    visible = ((sequence[:, None] == own_seq[None, :]) & (own_pos[None, :] <= position[:, None]))[
        None, None
    ]
    piece_log = jnp.transpose(all_log.reshape(count, kv_heads, query_group_ratio), (1, 2, 0))
    piece_delta = jnp.transpose(all_delta.reshape(count, kv_heads, query_group_ratio), (1, 2, 0))
    scores = (
        jnp.einsum("qkgd,jkd->kgqj", query_piece, key_bf, preferred_element_type=jnp.float32)
        * factor
    )
    probs = jnp.where(visible, jnp.exp(scores - piece_log[..., None]), 0.0)
    grad_value_rows = jnp.einsum(
        "kgqj,qkgd->jkd", probs.astype(jnp.bfloat16), grad_piece, preferred_element_type=jnp.float32
    )
    grad_probs = jnp.einsum(
        "qkgd,jkd->kgqj", grad_piece, value_bf, preferred_element_type=jnp.float32
    )
    grad_scores = (probs * (grad_probs - piece_delta[..., None])).astype(jnp.bfloat16)
    grad_key_rows = factor * jnp.einsum(
        "kgqj,qkgd->jkd", grad_scores, query_piece, preferred_element_type=jnp.float32
    )
    grad_query_rot = jnp.transpose(grad_query_heads, (2, 0, 1, 3)).reshape(
        rows, query_heads, head_size
    )
    grad_query_lin, grad_key_lin, query_gain_part, key_gain_part = positional_back(
        (grad_query_rot, grad_key_rows)
    )
    query_lin_bf = grad_query_lin.astype(jnp.bfloat16)
    key_lin_bf = grad_key_lin.astype(jnp.bfloat16)
    value_lin_bf = grad_value_rows.reshape(rows, kv_heads * head_size).astype(jnp.bfloat16)
    query_grad = contract_rows(normed_one, query_lin_bf)
    key_grad = contract_rows(normed_one, key_lin_bf)
    value_grad = contract_rows(normed_one, value_lin_bf)
    grad_normed_one = head_sums(
        contract_cols(query_lin_bf, full_query)
        + contract_cols(key_lin_bf, full_key)
        + contract_cols(value_lin_bf, full_value)
    )
    inner_one, query_gain_sum, key_gain_sum = row_stats(
        (jnp.sum(inputs * gain_one * grad_normed_one, axis=1), query_gain_part, key_gain_part)
    )
    grad_inputs = (
        grad_hidden
        + scale_one * gain_one * grad_normed_one
        - inputs * scale_one**3 * (inner_one / width)[:, None]
    )
    gain_one_part = jnp.sum(grad_normed_one * inputs * scale_one, axis=0)
    gain_one_grad, gain_two_grad, query_gain_grad, key_gain_grad = lax.psum(
        (gain_one_part, gain_two_part, query_gain_sum, key_gain_sum), ("dev", "gy")
    )
    narrowed = (
        lax.psum_scatter(
            query_grad.astype(jnp.bfloat16), "gy", scatter_dimension=0, tiled=True
        ).astype(jnp.float32),
        lax.psum_scatter(
            key_grad.astype(jnp.bfloat16), "gy", scatter_dimension=0, tiled=True
        ).astype(jnp.float32),
        lax.psum_scatter(
            value_grad.astype(jnp.bfloat16), "gy", scatter_dimension=0, tiled=True
        ).astype(jnp.float32),
        lax.psum_scatter(
            gate_grad.astype(jnp.bfloat16), "gy", scatter_dimension=0, tiled=True
        ).astype(jnp.float32),
        lax.psum_scatter(
            up_grad.astype(jnp.bfloat16), "gy", scatter_dimension=0, tiled=True
        ).astype(jnp.float32),
        lax.psum_scatter(
            out_grad.astype(jnp.bfloat16), "gy", scatter_dimension=0, tiled=True
        ).astype(jnp.float32),
        lax.psum_scatter(
            down_grad.astype(jnp.bfloat16), "gy", scatter_dimension=0, tiled=True
        ).astype(jnp.float32),
    )
    blocks = (
        lax.psum(narrowed[0].astype(jnp.bfloat16), "dev").astype(jnp.float32),
        lax.psum(narrowed[1].astype(jnp.bfloat16), "dev").astype(jnp.float32),
        lax.psum(narrowed[2].astype(jnp.bfloat16), "dev").astype(jnp.float32),
        lax.psum(narrowed[3].astype(jnp.bfloat16), "dev").astype(jnp.float32),
        lax.psum(narrowed[4].astype(jnp.bfloat16), "dev").astype(jnp.float32),
        lax.psum(narrowed[5].astype(jnp.bfloat16), "dev").astype(jnp.float32),
        lax.psum(narrowed[6].astype(jnp.bfloat16), "dev").astype(jnp.float32),
    )
    return (
        result.astype(jnp.bfloat16),
        grad_inputs,
        gain_one_grad,
        blocks[0],
        blocks[1],
        blocks[2],
        query_gain_grad,
        key_gain_grad,
        jnp.transpose(blocks[5]),
        gain_two_grad,
        blocks[3],
        blocks[4],
        jnp.transpose(blocks[6]),
    )


def solution(mesh):
    return jax.shard_map(
        per_device,
        mesh=mesh,
        in_specs=(
            P(("dev", "gy"), "gx"),
            P("gx"),
            P("gy", "gx"),
            P("gy", "gx"),
            P("gy", "gx"),
            P(),
            P(),
            P("gx", "gy"),
            P("gx"),
            P("gy", "gx"),
            P("gy", "gx"),
            P("gx", "gy"),
            P(("dev", "gy"), "gx"),
            P("dev"),
            P("dev"),
        ),
        out_specs=(
            P(("dev", "gy"), "gx"),
            P(("dev", "gy"), "gx"),
            P("gx"),
            P("gy", "gx"),
            P("gy", "gx"),
            P("gy", "gx"),
            P(),
            P(),
            P("gx", "gy"),
            P("gx"),
            P("gy", "gx"),
            P("gy", "gx"),
            P("gx", "gy"),
        ),
        check_vma=False,
    )
```

profile of v0, /device:TPU:0, one launch (start us, length us, event | category | flops | bytes accessed | tf_op | source)
XLA Modules:
  0.0 578.1 jit_solution(3506545188027675732)
XLA Ops:
  9.8 13.5 %psum.119 = f32[512]{0:T(512)S(1)} all-reduce(f32[512]{0:T(512)S(1)} %fusion.61), channel_id=1, replica_groups=mesh['dev'=4,'gx'=4,'gy'=2] {'gx'}, use_global_device_ids=true, to_apply=%region_1.0 | all-reduce | flops 512 | bytes 4096 | tf_op jit(solution)/shard_map/psum | solution.py:45
  23.3 1.8 fusion.63
  26.2 1.9 broadcast_multiply_fusion.2
  28.2 2.2 all_gather.54
  30.3 2.2 all_gather.57
  32.5 1.5 compare_and_fusion.1
  34.0 20.9 %all-gather.12.cloned.1.call-done = bf16[512,1024]{1,0:T(8,128)(2,1)} async-done(((bf16[512,256]{1,0:T(8,128)(2,1)}), bf16[512,1024]{1,0:T(8,128)(2,1)}) %all-gather.12.cloned.1.call-update) | async-done | bytes 1048592 | tf_op jit(solution)/shard_map/all_gather | solution.py:49
  54.9 2.3 multiply_reduce_fusion.2
  58.5 2.4 copy.47
  60.9 2.5 copy.46
  63.4 1.3 copy.45
  64.7 1.3 multiply_reduce_fusion.6
  69.2 2.3 all_gather.55
  71.5 1.4 fusion.47
  72.9 3.0 fusion.8
  76.0 2.1 fusion.10
  78.6 2.2 all_gather.58
  81.6 3.2 fusion.51
  84.8 3.1 convolution_convert_fusion.6
  88.6 24.9 %reduce-scatter.12.cloned.1.call-done = bf16[512,256]{1,0:T(8,128)(2,1)} async-done(((bf16[512,1024]{1,0:T(8,128)(2,1)}), bf16[512,256]{1,0:T(8,128)(2,1)}) %reduce-scatter.12.cloned.1.call-update) | async-done | bytes 262160 | tf_op jit(solution)/shard_map/reduce_scatter | solution.py:53
  114.6 9.4 %psum.120 = f32[512]{0:T(512)S(1)} all-reduce(f32[512]{0:T(512)S(1)} %multiply_reduce_fusion.5), channel_id=1, replica_groups=mesh['dev'=4,'gx'=4,'gy'=2] {'gx'}, use_global_device_ids=true, to_apply=%region_8.9 | all-reduce | flops 512 | bytes 4096 | tf_op jit(solution)/shard_map/psum | solution.py:45
  124.0 1.8 multiply_convert_fusion.2
  128.3 28.6 %all-gather.18.cloned.1.call-done = bf16[512,1024]{1,0:T(8,128)(2,1)} async-done(((bf16[512,256]{1,0:T(8,128)(2,1)}), bf16[512,1024]{1,0:T(8,128)(2,1)}) %all-gather.18.cloned.1.call-update) | async-done | bytes 1048592 | tf_op jit(solution)/shard_map/all_gather | solution.py:49
  156.9 3.9 fusion.95
  160.8 5.9 %all-gather.22.cloned.1.call-done = bf16[1024,768]{1,0:T(8,128)(2,1)} async-done(((bf16[512,768]{1,0:T(8,128)(2,1)}), bf16[1024,768]{1,0:T(8,128)(2,1)}) %all-gather.22.cloned.1.call-update) | async-done | bytes 1572880 | tf_op jit(solution)/shard_map/all_gather | solution.py:102
  166.7 3.9 fusion.96
  170.5 29.2 %all-gather.26.cloned.1.call-done = bf16[512,1024]{1,0:T(8,128)(2,1)} async-done(((bf16[512,256]{1,0:T(8,128)(2,1)}), bf16[512,1024]{1,0:T(8,128)(2,1)}) %all-gather.26.cloned.1.call-update) | async-done | bytes 1048592 | tf_op jit(solution)/shard_map/all_gather | solution.py:49
  199.7 9.8 %all-gather.24.cloned.1.call-done = bf16[768,1024]{1,0:T(8,128)(2,1)} async-done(((bf16[768,512]{1,0:T(8,128)(2,1)}), bf16[768,1024]{1,0:T(8,128)(2,1)}) %all-gather.24.cloned.1.call-update) | async-done | bytes 1572880 | tf_op jit(solution)/shard_map/all_gather | solution.py:106
  209.5 5.3 multiply_convert_fusion
  216.8 2.0 add_convert_fusion.1
  218.8 28.4 %reduce-scatter.16.cloned.1.call-done = bf16[512,256]{1,0:T(8,128)(2,1)} async-done(((bf16[512,1024]{1,0:T(8,128)(2,1)}), bf16[512,256]{1,0:T(8,128)(2,1)}) %reduce-scatter.16.cloned.1.call-update) | async-done | bytes 262160 | tf_op jit(solution)/shard_map/reduce_scatter | solution.py:53
  248.5 9.4 %psum.121 = f32[512]{0:T(512)S(1)} all-reduce(f32[512]{0:T(512)S(1)} %get-tuple-element.44), channel_id=1, replica_groups=mesh['dev'=4,'gx'=4,'gy'=2] {'gx'}, use_global_device_ids=true, to_apply=%region_12.13 | all-reduce | flops 512 | bytes 4096 | tf_op jit(solution)/shard_map/psum | solution.py:45
  257.9 1.9 fusion.90
  260.5 28.3 %all-gather.28.cloned.1.call-done = bf16[512,1024]{1,0:T(8,128)(2,1)} async-done(((bf16[512,256]{1,0:T(8,128)(2,1)}), bf16[512,1024]{1,0:T(8,128)(2,1)}) %all-gather.28.cloned.1.call-update) | async-done | bytes 1048592 | tf_op jit(solution)/shard_map/all_gather | solution.py:49
  288.8 3.1 convolution_convert_fusion.9
  291.9 3.6 convolution_convert_fusion.2
  295.6 3.7 convolution_convert_fusion.1
  300.7 3.7 fusion.32
  304.4 1.8 all_gather.67
  306.3 5.9 %fusion.75 = f32[2,512,1024,2]{2,1,3,0:T(8,128)} fusion(bf16[1024,2,2,128]{3,0,2,1:T(8,128)(2,1)} %all-gather.30.cloned.1.call-done, bf16[512,2,128]{2,0,1:T(8,128)(2,1)S(1)} %copy-done.17), kind=kOutput, calls=%fused_computation.121 | convolution fusion | flops 536870912 | bytes 9699328 | tf_op jit(solution)/shard_map/qkgd,jkd->kgqj/dot_general | solution.py:248
  312.5 2.0 all_gather.69
  314.5 8.7 %broadcast_multiply_fusion = (f32[512,2,128]{2,0,1:T(8,128)}, f32[512,2,128]{2,0,1:T(8,128)}) fusion(f32[512,128]{1,0:T(8,128)} %get-tuple-element.79, bf16[1024,2,2,128]{3,0,2,1:T(8,128)(2,1)} %all-gather.30.cloned.1.call-done, f32[2,512,1024,2]{2,1,3,0:T(8,128)} %fusion.75, f32[2,2,1024]{2,1,0:T(2,128)S(1)} %bitcast.231, ...), kind=kOutput, calls=%fused_computation.123 | convolution fusion | flops 1086455808 | bytes 12615680 | tf_op jit(solution)/shard_map/kgqj,qkgd->jkd/dot_general | solution.py:259
  323.2 1.5 fusion.94
  327.5 1.3 convolution_convert_fusion.8
  328.9 5.7 fusion.42
  338.4 3.1 convolution_convert_fusion.4
  341.8 8.2 %fusion.33 = f32[2,2,512,128]{2,3,1,0:T(8,128)} fusion(f32[2,1024,512,2]{2,1,3,0:T(8,128)} %copy-done.2, f32[2,2,512]{2,1,0:T(2,128)S(1)} %fusion.50, f32[2,2,512]{2,1,0:T(2,128)S(1)} %log_add_fusion, pred[512,1024]{0,1:T(8,128)(4,1)S(1)} %copy-done.22, bf16[512,2,2,128]{0,3,2,1:T(8,128)(2,1)} %bitcast.216, bf16[1024,2,128]{2,0,1:T(8,128)(2,1)} %all_gather.55, ...), kind=kOutput, calls=%fused_computation.49 | convolution fusion | flops 1086586880 | bytes 11550720 | tf_op jit(solution)/shard_map/kgqj,jkd->kgqd/dot_general | solution.py:223
  350.0 1.5 bitcast_multiply_fusion
  353.3 1.7 convolution_convert_fusion.5
  355.1 2.2 fusion.98
  358.4 1.5 add_convert_fusion
  360.0 3.7 convolution_convert_fusion.3
  363.9 8.7 %reduce-scatter.24.cloned.1.call-done = bf16[512,256]{1,0:T(8,128)(2,1)} async-done(((bf16[1024,256]{1,0:T(8,128)(2,1)}), bf16[512,256]{1,0:T(8,128)(2,1)}) %reduce-scatter.24.cloned.1.call-update) | async-done | bytes 262160 | tf_op jit(solution)/shard_map/reduce_scatter | solution.py:298
  372.6 12.1 %reduce-scatter.26.cloned.1.call-done = bf16[512,512]{1,0:T(8,128)(2,1)} async-done(((bf16[1024,512]{1,0:T(8,128)(2,1)}), bf16[512,512]{1,0:T(8,128)(2,1)}) %reduce-scatter.26.cloned.1.call-update) | async-done | bytes 524304 | tf_op jit(solution)/shard_map/reduce_scatter | solution.py:307
  384.7 11.8 %reduce-scatter.20.cloned.1.call-done = bf16[512,512]{1,0:T(8,128)(2,1)} async-done(((bf16[1024,512]{1,0:T(8,128)(2,1)}), bf16[512,512]{1,0:T(8,128)(2,1)}) %reduce-scatter.20.cloned.1.call-update) | async-done | bytes 524304 | tf_op jit(solution)/shard_map/reduce_scatter | solution.py:292
  396.5 31.3 %reduce-scatter.18.cloned.1.call-done = bf16[512,256]{1,0:T(8,128)(2,1)} async-done(((bf16[512,1024]{1,0:T(8,128)(2,1)}), bf16[512,256]{1,0:T(8,128)(2,1)}) %reduce-scatter.18.cloned.1.call-update) | async-done | bytes 262160 | tf_op jit(solution)/shard_map/reduce_scatter | solution.py:53
  429.0 9.5 %all-reduce.5 = (f32[512]{0:T(512)S(1)}, f32[128]{0:T(128)S(1)}, f32[128]{0:T(128)S(1)}) all-reduce(f32[512]{0:T(512)S(1)} %get-tuple-element.46, f32[128]{0:T(128)S(1)} %get-tuple-element.41, f32[128]{0:T(128)S(1)} %get-tuple-element.39), channel_id=1, replica_groups=mesh['dev'=4,'gx'=4,'gy'=2] {'gx'}, use_global_device_ids=true, to_apply=%region_18.19 | all-reduce | flops 768 | bytes 6144 | tf_op jit(solution)/shard_map/psum | solution.py:45
  438.5 12.7 %all-reduce.4 = (f32[256]{0:T(256)}, f32[128]{0:T(128)}, f32[128]{0:T(128)}, f32[256]{0:T(256)}) all-reduce(f32[256]{0:T(256)S(1)} %get-tuple-element.45, f32[128]{0:T(128)S(1)} %get-tuple-element.52, f32[128]{0:T(128)S(1)} %get-tuple-element.53, f32[256]{0:T(256)S(1)} %get-tuple-element.43), channel_id=1, replica_groups=mesh['dev'=4,'gx'=4,'gy'=2] {'dev','gy'}, use_global_device_ids=true, to_apply=%region_20.21 | all-reduce | flops 768 | bytes 6144 | tf_op jit(solution)/shard_map/psum | solution.py:288
  451.2 5.3 reduce-scatter.14.cloned.1.call-done
  456.5 2.3 fusion.59
  458.8 102.3 %all-reduce.9.cloned.1.call-done = (bf16[512,512]{0,1:T(8,128)(2,1)}, bf16[512,512]{1,0:T(8,128)(2,1)}, bf16[512,256]{1,0:T(8,128)(2,1)}, bf16[512,256]{1,0:T(8,...) async-done(((bf16[512,512]{0,1:T(8,128)(2,1)}, bf16[512,512]{1,0:T(8,128)(2,1)}, bf16[512,256]{1,0:T(8,128)(2,1)}, ...) | async-done | bytes 3932176 | tf_op jit(solution)/shard_map/psum | solution.py:320
  561.2 2.3 convert_element_type.214
  563.4 1.8 convert_element_type.216
  569.8 1.4 transpose.114
  (209 shorter events, 35.1 us)
Async XLA Ops:
  7.2 18.7 %copy-start.45 = (bf16[128]{0:T(256)(128)(2,1)S(1)}, bf16[128]{0:T(256)(128)(2,1)}, u32[]{:S(2)}) copy-start(bf16[128]{0:T(256)(128)(2,1)} %param.20) | copy-start | bytes 772
  7.2 18.7 %copy-start.41 = (s32[1024]{0:T(1024)S(1)}, s32[1024]{0:T(1024)}, u32[]{:S(2)}) copy-start(s32[1024]{0:T(1024)} %param.29) | copy-start | bytes 12292
  7.2 18.8 %copy-start.42 = (s32[1024]{0:T(1024)S(1)}, s32[1024]{0:T(1024)}, u32[]{:S(2)}) copy-start(s32[1024]{0:T(1024)} %param.28) | copy-start | bytes 12292
  7.2 20.9 %copy-start.38 = (bf16[512,256]{1,0:T(8,128)(2,1)S(1)}, bf16[512,256]{1,0:T(8,128)(2,1)}, u32[]{:S(2)}) copy-start(bf16[512,256]{1,0:T(8,128)(2,1)} %param.18) | copy-start | bytes 786436
  7.2 26.8 %all-gather.14.cloned.1.call-start = ((), (), s32[]{:S(2)}) async-start(), calls=%async_computation.12 | async-start | bytes 1572864 | tf_op jit(solution)/shard_map/all_gather | solution.py:98
  8.0 22.4 %copy-start.46 = (bf16[128]{0:T(256)(128)(2,1)S(1)}, bf16[128]{0:T(256)(128)(2,1)}, u32[]{:S(2)}) copy-start(bf16[128]{0:T(256)(128)(2,1)} %param.21) | copy-start | bytes 772
  8.0 22.4 %copy-start.39 = (bf16[512,256]{1,0:T(8,128)(2,1)S(1)}, bf16[512,256]{1,0:T(8,128)(2,1)}, u32[]{:S(2)}) copy-start(bf16[512,256]{1,0:T(8,128)(2,1)} %param.19) | copy-start | bytes 786436
  8.0 46.9 %all-gather.12.cloned.1.call-start = ((), (), s32[]{:S(2)}) async-start(), calls=%async_computation.11 | async-start | bytes 1310720 | tf_op jit(solution)/shard_map/all_gather | solution.py:49
  25.1 59.6 %all-gather.16.cloned.1.call-start = ((), (), s32[]{:S(2)}) async-start(), calls=%async_computation.13 | async-start | bytes 1572864 | tf_op jit(solution)/shard_map/all_gather | solution.py:105
  25.8 87.6 %reduce-scatter.12.cloned.1.call-start = ((), (), s32[]{:S(2)}) async-start(), calls=%async_computation.14 | async-start | bytes 1310720 | tf_op jit(solution)/shard_map/reduce_scatter | solution.py:53
  28.2 43.3 %copy-start.11 = (f32[512,128]{1,0:T(8,128)}, f32[512,128]{1,0:T(8,128)S(1)}, u32[]{:S(2)}) copy-start(f32[512,128]{1,0:T(8,128)S(1)} %get-tuple-element.81) | copy-start | bytes 786436
  30.3 34.3 %copy-start.6 = (bf16[1024,256]{1,0:T(8,128)(2,1)}, bf16[1024,256]{1,0:T(8,128)(2,1)S(1)}, u32[]{:S(2)}) copy-start(bf16[1024,256]{1,0:T(8,128)(2,1)S(1)} %all_gather.54) | copy-start | bytes 1572868
  32.5 45.6 %copy-start.4 = (bf16[1024,256]{1,0:T(8,128)(2,1)}, bf16[1024,256]{1,0:T(8,128)(2,1)S(1)}, u32[]{:S(2)}) copy-start(bf16[1024,256]{1,0:T(8,128)(2,1)S(1)} %all_gather.57) | copy-start | bytes 1572868
  60.9 3.8 copy-start
  67.6 3.9 copy-start.8
  67.6 3.9 copy-start.9
  67.7 3.9 copy-start.10
  72.9 3.0 copy-start.21
  75.9 4.8 copy-start.2
  78.6 6.2 %copy-start.25 = (bf16[512,256]{0,1:T(8,128)(2,1)}, bf16[512,256]{0,1:T(8,128)(2,1)S(1)}, u32[]{:S(2)}) copy-start(bf16[512,256]{0,1:T(8,128)(2,1)S(1)} %convolution_convert_fusion.10) | copy-start | bytes 786436
  84.7 3.8 copy-start.48
  84.7 3.8 copy-start.47
  84.8 28.7 %copy-start.1 = (bf16[512,256]{1,0:T(8,128)(2,1)S(1)}, bf16[512,256]{1,0:T(8,128)(2,1)}, u32[]{:S(2)}) copy-start(bf16[512,256]{1,0:T(8,128)(2,1)} %param.15) | copy-start | bytes 786436
  87.9 40.4 %all-gather.20.cloned.1.call-start = ((), (), s32[]{:S(2)}) async-start(), calls=%async_computation.16 | async-start | bytes 2359296 | tf_op jit(solution)/shard_map/all_gather | solution.py:101
  88.5 68.4 %all-gather.18.cloned.1.call-start = ((), (), s32[]{:S(2)}) async-start(), calls=%async_computation.15 | async-start | bytes 1310720 | tf_op jit(solution)/shard_map/all_gather | solution.py:49
  125.8 40.9 %all-gather.22.cloned.1.call-start = ((), (), s32[]{:S(2)}) async-start(), calls=%async_computation.17 | async-start | bytes 2359296 | tf_op jit(solution)/shard_map/all_gather | solution.py:102
  126.6 73.1 %all-gather.26.cloned.1.call-start = ((), (), s32[]{:S(2)}) async-start(), calls=%async_computation.20 | async-start | bytes 1310720 | tf_op jit(solution)/shard_map/all_gather | solution.py:49
  127.3 82.2 %all-gather.24.cloned.1.call-start = ((), (), s32[]{:S(2)}) async-start(), calls=%async_computation.18 | async-start | bytes 2359296 | tf_op jit(solution)/shard_map/all_gather | solution.py:106
  128.1 119.2 %reduce-scatter.16.cloned.1.call-start = ((), (), s32[]{:S(2)}) async-start(), calls=%async_computation.21 | async-start | bytes 1310720 | tf_op jit(solution)/shard_map/reduce_scatter | solution.py:53
  209.5 5.3 copy-start.43
  214.8 2.0 copy-start.44
  216.8 30.5 %copy-start.3 = (bf16[512,256]{1,0:T(8,128)(2,1)S(1)}, bf16[512,256]{1,0:T(8,128)(2,1)}, u32[]{:S(2)}) copy-start(bf16[512,256]{1,0:T(8,128)(2,1)} %reduce-scatter.12.cloned.1.call-done) | copy-start | bytes 786436
  216.8 41.1 %copy-start.19 = (bf16[512,256]{1,0:T(8,128)(2,1)S(1)}, bf16[512,256]{1,0:T(8,128)(2,1)}, u32[]{:S(2)}) copy-start(bf16[512,256]{1,0:T(8,128)(2,1)} %param.27) | copy-start | bytes 786436
  218.8 70.0 %all-gather.28.cloned.1.call-start = ((), (), s32[]{:S(2)}) async-start(), calls=%async_computation.22 | async-start | bytes 1310720 | tf_op jit(solution)/shard_map/all_gather | solution.py:49
  259.8 46.5 %all-gather.30.cloned.1.call-start = ((), (), s32[]{:S(2)}) async-start(), calls=%async_computation.23 | async-start | bytes 1572864 | tf_op jit(solution)/shard_map/all_gather | solution.py:239
  260.4 54.1 %all-gather.32.cloned.1.call-start = ((), (), s32[]{:S(2)}) async-start(), calls=%async_computation.24 | async-start | bytes 1572864 | tf_op jit(solution)/shard_map/all_gather | solution.py:240
  291.9 71.9 %reduce-scatter.28.cloned.1.call-start = ((), (), s32[]{:S(2)}) async-start(), calls=%async_computation.30 | async-start | bytes 2359296 | tf_op jit(solution)/shard_map/reduce_scatter | solution.py:301
  295.6 68.2 %reduce-scatter.30.cloned.1.call-start = ((), (), s32[]{:S(2)}) async-start(), calls=%async_computation.31 | async-start | bytes 2359296 | tf_op jit(solution)/shard_map/reduce_scatter | solution.py:304
  299.3 64.5 %reduce-scatter.32.cloned.1.call-start = ((), (), s32[]{:S(2)}) async-start(), calls=%async_computation.32 | async-start | bytes 2359296 | tf_op jit(solution)/shard_map/reduce_scatter | solution.py:310
  300.7 5.6 copy-start.17
  304.3 59.5 %reduce-scatter.22.cloned.1.call-start = ((), (), s32[]{:S(2)}) async-start(), calls=%async_computation.27 | async-start | bytes 786432 | tf_op jit(solution)/shard_map/reduce_scatter | solution.py:295
  306.3 5.9 %copy-start.23 = (bf16[512,512]{0,1:T(8,128)(2,1)S(1)}, bf16[512,512]{0,1:T(8,128)(2,1)}, u32[]{:S(2)}) copy-start(bf16[512,512]{0,1:T(8,128)(2,1)} %convolution_convert_fusion.9) | copy-start | bytes 1572868
  306.3 5.9 %copy-start.29 = (f32[2,2,512,128]{2,3,1,0:T(8,128)S(1)}, f32[2,2,512,128]{2,3,1,0:T(8,128)}, u32[]{:S(2)}) copy-start(f32[2,2,512,128]{2,3,1,0:T(8,128)} %get-tuple-element.93) | copy-start | bytes 3145732
  323.2 1.5 copy-start.37
  326.3 2.5 copy-start.36
  328.8 43.8 %reduce-scatter.24.cloned.1.call-start = ((), (), s32[]{:S(2)}) async-start(), calls=%async_computation.28 | async-start | bytes 786432 | tf_op jit(solution)/shard_map/reduce_scatter | solution.py:298
  334.6 2.1 copy-start.14
  334.6 2.9 copy-start.12
  336.6 48.1 %reduce-scatter.26.cloned.1.call-start = ((), (), s32[]{:S(2)}) async-start(), calls=%async_computation.29 | async-start | bytes 1572864 | tf_op jit(solution)/shard_map/reduce_scatter | solution.py:307
  338.3 3.5 copy-start.22
  341.5 55.0 %reduce-scatter.20.cloned.1.call-start = ((), (), s32[]{:S(2)}) async-start(), calls=%async_computation.26 | async-start | bytes 1572864 | tf_op jit(solution)/shard_map/reduce_scatter | solution.py:292
  350.0 1.6 copy-start.15
  350.0 1.7 copy-start.28
  355.0 2.3 copy-start.7
  355.0 72.8 %reduce-scatter.18.cloned.1.call-start = ((), (), s32[]{:S(2)}) async-start(), calls=%async_computation.25 | async-start | bytes 1310720 | tf_op jit(solution)/shard_map/reduce_scatter | solution.py:53
  360.0 96.5 %reduce-scatter.14.cloned.1.call-start = ((), (), s32[]{:S(2)}) async-start(), calls=%async_computation.19 | async-start | bytes 1310720 | tf_op jit(solution)/shard_map/reduce_scatter | solution.py:53
  363.7 197.5 %all-reduce.9.cloned.1.call-start = ((), (), s32[]{:S(2)}) async-start(), calls=%async_computation.33 | async-start | bytes 7864320 | tf_op jit(solution)/shard_map/psum | solution.py:320
  396.5 60.0 %copy-start.18 = (bf16[512,256]{1,0:T(8,128)(2,1)S(1)}, bf16[512,256]{1,0:T(8,128)(2,1)}, u32[]{:S(2)}) copy-start(bf16[512,256]{1,0:T(8,128)(2,1)} %reduce-scatter.16.cloned.1.call-done) | copy-start | bytes 786436
  396.5 60.0 %copy-start.20 = (bf16[512,256]{1,0:T(8,128)(2,1)S(1)}, bf16[512,256]{1,0:T(8,128)(2,1)}, u32[]{:S(2)}) copy-start(bf16[512,256]{1,0:T(8,128)(2,1)} %param.27) | copy-start | bytes 786436
  561.2 4.0 copy-start.40
  561.2 4.9 copy-start.34
  561.2 6.1 %copy-start.33 = (bf16[512,768]{1,0:T(8,128)(2,1)S(1)}, bf16[512,768]{1,0:T(8,128)(2,1)}, u32[]{:S(2)}) copy-start(bf16[512,768]{1,0:T(8,128)(2,1)} %get-tuple-element.58) | copy-start | bytes 2359300
  566.1 2.4 copy-start.32
  567.2 2.5 copy-start.31
  (10 other events, 9.8 us)
Sparse Core Ops, SparseCore 0:
  9.6 11.7 all-gather.13
  25.2 29.6 all-gather.11
  56.4 7.3 all-gather.15
  88.0 25.3 reduce-scatter.11
  114.9 8.4 all-gather.19
  125.9 30.9 all-gather.17
  158.5 8.1 all-gather.21
  168.3 31.3 all-gather.25
  201.3 8.1 all-gather.23
  218.9 28.2 reduce-scatter.15
  260.0 28.7 all-gather.27
  290.8 7.3 all-gather.29
  300.3 10.1 all-gather.31
  313.2 10.1 reduce-scatter.27
  326.2 10.2 reduce-scatter.29
  339.1 10.2 reduce-scatter.31
  352.2 9.1 reduce-scatter.21
  363.5 9.0 reduce-scatter.23
  374.9 9.6 reduce-scatter.25
  386.8 9.6 reduce-scatter.19
  399.5 28.2 reduce-scatter.17
  430.7 25.7 reduce-scatter.13
  460.9 100.2 all-reduce.8
where the time goes:
time: 587 us; the launch traced here: 578 us
  waiting for transfers between devices  352 us (60%)
  matrix products  87.2 us (15%)
  blocking collectives  67.1 us (11%)
  other arithmetic  38.1 us (6%)
  local copies, waits for them, and re-layouts  16.7 us (3%)
  between operations  15.2 us (3%)
    all_gather x4, waiting for transfers between devices, row_pieces(): return lax.all_gather(block, 'gx', axis=1, tiled=True)  107 us
    psum x1, waiting for transfers between devices, per_device(): lax.psum(narrowed[5].astype(jnp.bfloat16), 'dev').astype(jnp.float32)  102 us
    reduce_scatter x4, waiting for transfers between devices, head_sums(): lax.psum_scatter(term.astype(jnp.bfloat16), 'gx', scatter_dimension=1, ti...  89.8 us
    psum x4, blocking collectives, row_stats(): return lax.psum(parts, 'gx')  41.7 us
    dot_general x7, matrix products, contract_rows(): lax.dot_general(left, right, (((0,), (0,)), ((), ())), preferred_element_...  18.4 us
    dot_general x7, matrix products, contract_cols(): lax.dot_general(left, right, (((1,), (1,)), ((), ())), preferred_element_...  15.6 us
    psum x1, blocking collectives, per_device(): lax.psum((gain_one_part, gain_two_part, query_gain_sum, key_gain_sum), ('...  12.7 us
    reduce_scatter x1, waiting for transfers between devices, per_device(): lax.psum_scatter(out_grad.astype(jnp.bfloat16), 'gy', scatter_dimension=0...  12.1 us
  transfers between devices with their start and end apart: 23, of which 14 were waited for; matrix products, arithmetic and copies ran while one was open for 19% of the time, Pallas kernels for 0%

commit v1 on v0

v1 whole, which is shorter than its diff:
```python
import functools

import jax
import jax.numpy as jnp
from jax import lax
from jax.experimental import pallas as pl
from jax.experimental.pallas import tpu as pltpu
from jax.sharding import PartitionSpec as P

EPS = 1e-06
THETA = 1000000.0
NEGATIVE = -1e30
BF = jnp.bfloat16
F32 = jnp.float32
VMEM = pl.BlockSpec(memory_space=pltpu.VMEM)
SMEM = pl.BlockSpec(memory_space=pltpu.SMEM)


def dot(left, right):
    return lax.dot_general(left, right, (((1,), (0,)), ((), ())), preferred_element_type=F32)


def dot_cols(left, right):
    return lax.dot_general(left, right, (((1,), (1,)), ((), ())), preferred_element_type=F32)


def dot_rows(left, right):
    return lax.dot_general(left, right, (((0,), (0,)), ((), ())), preferred_element_type=F32)


def span(offset, size):
    return pl.ds(pl.multiple_of(offset, size), size)


def turn(vectors):
    return pltpu.roll(vectors, vectors.shape[-1] // 2, 1)


def shifted(block, axis, shift):
    size = lax.axis_size(axis)
    return lax.ppermute(block, axis, [(i, (i + shift) % size) for i in range(size)])


def pieces_of(block):
    return [block] + [shifted(block, "gx", s) for s in range(1, lax.axis_size("gx"))]


def piece_sum(own, others):
    total = own
    for s, part in enumerate(others, 1):
        total = total + shifted(part, "gx", s).astype(F32)
    return total


def gather_width(block, axis):
    if lax.axis_size("gy") == 2:
        return jnp.concatenate([block, shifted(block, "gy", 1)], axis=axis)
    return lax.all_gather(block, "gy", axis=axis, tiled=True)


def scatter_width(make, axis, width):
    count = lax.axis_size("gy")
    if count == 2:
        half = width // 2
        sent = make(half, half).astype(BF)
        return make(0, half) + shifted(sent, "gy", 1).astype(F32)
    return lax.psum_scatter(
        make(0, width).astype(BF), "gy", scatter_dimension=axis, tiled=True
    ).astype(F32)


def dev_sum(arrays):
    count = lax.axis_size("dev")
    here = lax.axis_index("dev")
    if count == 1:
        return arrays
    even = count & (count - 1) == 0

    def partner(m):
        return here ^ m if even else (here + m) % count

    def giver(m):
        return here ^ m if even else (here - m) % count

    def send(block, m):
        return lax.ppermute(
            block, "dev", [(i, i ^ m if even else (i + m) % count) for i in range(count)]
        )

    sizes = [a.shape[0] // count for a in arrays]
    low = [a.astype(BF) for a in arrays]
    mine = [
        lax.dynamic_slice_in_dim(a, here * size, size).astype(F32)
        for a, size in zip(arrays, sizes)
    ]
    for m in range(1, count):
        for k, (a, size) in enumerate(zip(low, sizes)):
            got = send(lax.dynamic_slice_in_dim(a, partner(m) * size, size), m)
            mine[k] = mine[k] + got.astype(F32)
    out = []
    for total, size, a in zip(mine, sizes, arrays):
        whole = jnp.zeros(a.shape, F32)
        whole = lax.dynamic_update_slice_in_dim(whole, total, here * size, 0)
        total = total.astype(BF)
        for m in range(1, count):
            whole = lax.dynamic_update_slice_in_dim(
                whole, send(total, m).astype(F32), giver(m) * size, 0
            )
        out.append(whole)
    return out


def small_sum(block, axis):
    total = block
    for s in range(1, lax.axis_size(axis)):
        total = total + shifted(block, axis, s)
    return total


def place(count, offset_ref, s):
    return lambda width: span(offset_ref[s], width)


def cot_kernel(count, offset_ref, *refs):
    pieces, (down_ref, whole_ref, grad_ref) = refs[:count], refs[count:]
    width = pieces[0].shape[1]
    for s in range(count):
        whole_ref[:, span(offset_ref[s], width)] = pieces[s][...]
    grad_ref[...] = dot_cols(whole_ref[...], down_ref[...])


def qkv_kernel(count, head, offset_ref, *refs):
    pieces = refs[:count]
    gain_ref, wq_ref, wk_ref, wv_ref, qg_ref, kg_ref, cos_ref, sin_ref = refs[count : count + 8]
    normed_ref, scale_ref, ql_ref, kl_ref, q_ref, k_ref, v_ref = refs[count + 8 :]
    width = pieces[0].shape[1]
    blocks = [p[...].astype(F32) for p in pieces]
    square = sum(jnp.sum(b * b, axis=1, keepdims=True) for b in blocks)
    scale = lax.rsqrt(square / (width * count) + EPS)
    scale_ref[...] = scale
    for s in range(count):
        normed_ref[:, span(offset_ref[s], width)] = (
            blocks[s] * scale * gain_ref[s : s + 1, :]
        ).astype(BF)
    normed = normed_ref[...]
    ql_ref[...] = dot(normed, wq_ref[...])
    kl_ref[...] = dot(normed, wk_ref[...])
    v_ref[...] = dot(normed, wv_ref[...]).astype(BF)
    cosine, sine = cos_ref[...], sin_ref[...]
    for lin_ref, gain, out_ref in ((ql_ref, qg_ref, q_ref), (kl_ref, kg_ref, k_ref)):
        for h in range(lin_ref.shape[1] // head):
            cut = slice(h * head, (h + 1) * head)
            u = lin_ref[:, cut]
            u = u * lax.rsqrt(jnp.mean(u * u, axis=1, keepdims=True) + EPS) * gain[...]
            out_ref[:, cut] = (u * cosine + turn(u) * sine).astype(BF)


def visible_bias(seq_col, pos_col, seq_row, pos_row):
    seen = (seq_col == seq_row) & (pos_col <= pos_row)
    return jnp.where(seen, 0.0, NEGATIVE)


def attend_kernel(
    head, tile, offset_ref, q_ref, k_ref, v_ref, row_ref, col_ref, wo_ref, *outs
):
    parts, (mixed_ref, att_ref, log_ref) = outs[:-3], outs[-3:]
    peers, rows = k_ref.shape[0], q_ref.shape[0]
    kv_heads = k_ref.shape[2] // head
    ratio = q_ref.shape[1] // head // kv_heads
    factor = head ** (-0.5)
    width = wo_ref.shape[1] // len(parts)
    for t in range(rows // tile):
        part = slice(t * tile, (t + 1) * tile)
        extent = (t + 1) * tile
        seq_row, pos_row = row_ref[0:1, part], row_ref[1:2, part]

        def bias_of(p):
            one = visible_bias(
                col_ref[p, :extent, 0:1], col_ref[p, :extent, 1:2], seq_row, pos_row
            )
            return jnp.concatenate([one] * ratio, axis=1)

        biases = [bias_of(p) for p in range(peers)] if peers <= 2 else None
        for j in range(kv_heads):
            cut = slice(j * head, (j + 1) * head)
            queries = jnp.concatenate(
                [
                    q_ref[part, (j * ratio + i) * head : (j * ratio + i + 1) * head]
                    for i in range(ratio)
                ],
                axis=0,
            )

            def step(p, carry, bias=None):
                high, total, accum = carry
                if bias is None:
                    bias = bias_of(p)
                scores = dot_cols(k_ref[p, :extent, cut], queries) * factor + bias
                newest = jnp.maximum(high, jnp.max(scores, axis=0, keepdims=True))
                weights = jnp.exp(scores - newest)
                shrink = jnp.exp(high - newest)
                total = total * shrink + jnp.sum(weights, axis=0, keepdims=True)
                accum = accum * shrink + dot_rows(v_ref[p, :extent, cut], weights.astype(BF))
                return newest, total, accum

            carry = (
                jnp.full((1, ratio * tile), NEGATIVE, F32),
                jnp.zeros((1, ratio * tile), F32),
                jnp.zeros((head, ratio * tile), F32),
            )
            if peers <= 2:
                for p in range(peers):
                    carry = step(p, carry, biases[p])
            else:
                carry = lax.fori_loop(0, peers, step, carry)
            high, total, accum = carry
            attended = accum / total
            logs = high + jnp.log(total)
            back = jnp.transpose(attended)
            for i in range(ratio):
                h = j * ratio + i
                lane = slice(i * tile, (i + 1) * tile)
                att_ref[h * head : (h + 1) * head, part] = attended[:, lane]
                log_ref[h : h + 1, part] = logs[:, lane]
                mixed_ref[part, h * head : (h + 1) * head] = back[lane, :].astype(BF)
    for s in range(len(parts)):
        weight = wo_ref[:, span(offset_ref[len(parts) + s], width)]
        parts[s][...] = dot(mixed_ref[...], weight).astype(parts[s].dtype)


def ffn_kernel(count, offset_ref, *refs):
    pieces = refs[:count]
    gain_ref, wg_ref, wu_ref, grad_ref = refs[count : count + 4]
    outs = refs[count + 4 :]
    parts, (normed_ref, scale_ref, product_ref, gate_ref, up_ref) = outs[:count], outs[count:]
    width = pieces[0].shape[1]
    blocks = [p[...].astype(F32) for p in pieces]
    square = sum(jnp.sum(b * b, axis=1, keepdims=True) for b in blocks)
    scale = lax.rsqrt(square / (width * count) + EPS)
    scale_ref[...] = scale
    for s in range(count):
        normed_ref[:, span(offset_ref[s], width)] = (
            blocks[s] * scale * gain_ref[s : s + 1, :]
        ).astype(BF)
    normed = normed_ref[...]
    gate = dot(normed, wg_ref[...])
    up = dot(normed, wu_ref[...])
    sig = 1.0 / (1.0 + jnp.exp(-gate))
    silu = gate * sig
    product_ref[...] = (silu * up).astype(BF)
    grad = grad_ref[...]
    gate_ref[...] = (grad * up * (sig + silu * (1.0 - sig))).astype(BF)
    up_ref[...] = (grad * silu).astype(BF)
    for s in range(count):
        at = span(offset_ref[count + s], width)
        parts[s][...] = (
            dot_cols(gate_ref[...], wg_ref[at, :]) + dot_cols(up_ref[...], wu_ref[at, :])
        ).astype(parts[s].dtype)


def split_dot_kernel(count, offset_ref, left_ref, weight_ref, *parts):
    width = weight_ref.shape[1] // count
    for s in range(count):
        weight = weight_ref[:, span(offset_ref[count + s], width)]
        parts[s][...] = dot(left_ref[...], weight).astype(parts[s].dtype)


def unrotate(grad, lin, gain, cosine, sine):
    size = lin.shape[1]
    inner = grad * cosine + turn(grad * sine)
    inverse = lax.rsqrt(jnp.mean(lin * lin, axis=1, keepdims=True) + EPS)
    unit = lin * inverse
    part = jnp.sum(inner * unit, axis=0, keepdims=True)
    inner = inner * gain
    mean = jnp.sum(inner * unit, axis=1, keepdims=True) / size
    return inverse * (inner - unit * mean), part


def attend_back_kernel(
    count, head, tile, offset_ref, *refs
):
    hidden, grads = refs[:count], refs[count : 2 * count]
    (gain_ref, scale_ref, cot_ref, wo_ref, q_ref, ql_ref, k_ref, v_ref, row_ref, col_ref,
     att_ref, log_ref, qg_ref, cos_ref, sin_ref) = refs[2 * count : 2 * count + 15]
    branch_ref, dql_ref, dk_ref, dv_ref, qpart_ref, dk_sum, dv_sum = refs[2 * count + 15 :]
    peers, rows = k_ref.shape[0], q_ref.shape[0]
    kv_heads = k_ref.shape[2] // head
    ratio = q_ref.shape[1] // head // kv_heads
    factor = head ** (-0.5)
    width = hidden[0].shape[1]
    dk_sum[...] = jnp.zeros_like(dk_sum)
    dv_sum[...] = jnp.zeros_like(dv_sum)
    gain_part = jnp.zeros((1, head), F32)
    for t in range(rows // tile):
        part = slice(t * tile, (t + 1) * tile)
        extent = (t + 1) * tile
        scale = scale_ref[part, :]
        blocks = [(h[part, :].astype(F32), g[part, :].astype(F32)) for h, g in zip(hidden, grads)]
        scaled = [g * gain_ref[s : s + 1, :] for s, (_, g) in enumerate(blocks)]
        inner = sum(
            jnp.sum(h * g, axis=1, keepdims=True) for (h, _), g in zip(blocks, scaled)
        )
        lessen = scale * scale * scale * (inner / (width * count))
        for s in range(count):
            at = span(offset_ref[s], width)
            branch_ref[part, at] = (
                cot_ref[part, at].astype(F32) + scale * scaled[s] - blocks[s][0] * lessen
            ).astype(BF)
        grad_mixed = dot_cols(branch_ref[part, :], wo_ref[...]).astype(BF)
        grad_back = jnp.transpose(grad_mixed.astype(F32))
        seq_row, pos_row = row_ref[0:1, part], row_ref[1:2, part]

        def bias_of(p):
            one = visible_bias(
                col_ref[p, :extent, 0:1], col_ref[p, :extent, 1:2], seq_row, pos_row
            )
            return jnp.concatenate([one] * ratio, axis=1)

        biases = [bias_of(p) for p in range(peers)] if peers <= 2 else None
        for j in range(kv_heads):
            cut = slice(j * head, (j + 1) * head)
            heads = [j * ratio + i for i in range(ratio)]
            lanes = [slice(h * head, (h + 1) * head) for h in heads]
            queries = jnp.concatenate([q_ref[part, lane] for lane in lanes], axis=0)
            grad_heads = jnp.concatenate([grad_mixed[:, lane] for lane in lanes], axis=0)
            logs = jnp.concatenate([log_ref[h : h + 1, part] for h in heads], axis=1)
            delta = jnp.concatenate(
                [
                    jnp.sum(grad_back[lane, :] * att_ref[lane, part], axis=0, keepdims=True)
                    for lane in lanes
                ],
                axis=1,
            )

            def step(p, accum, bias=None):
                if bias is None:
                    bias = bias_of(p)
                keys, values = k_ref[p, :extent, cut], v_ref[p, :extent, cut]
                probs = jnp.exp(dot_cols(keys, queries) * factor + bias - logs)
                grad_probs = dot_cols(values, grad_heads)
                grad_scores = (probs * (grad_probs - delta)).astype(BF)
                dv_sum[p, :extent, cut] += dot(probs.astype(BF), grad_heads)
                dk_sum[p, :extent, cut] += dot(grad_scores, queries)
                return accum + dot_rows(keys, grad_scores)

            accum = jnp.zeros((head, ratio * tile), F32)
            if peers <= 2:
                for p in range(peers):
                    accum = step(p, accum, biases[p])
            else:
                accum = lax.fori_loop(0, peers, step, accum)
            grad_query = jnp.transpose(accum) * factor
            for i, lane in enumerate(lanes):
                lin, one = unrotate(
                    grad_query[i * tile : (i + 1) * tile, :],
                    ql_ref[part, lane],
                    qg_ref[...],
                    cos_ref[part, :],
                    sin_ref[part, :],
                )
                dql_ref[part, lane] = lin.astype(BF)
                gain_part = gain_part + one
    qpart_ref[...] = gain_part
    dk_ref[...] = (dk_sum[...] * factor).astype(dk_ref.dtype)
    dv_ref[...] = dv_sum[...].astype(dv_ref.dtype)


def lin_back_kernel(count, head, parts_in, offset_ref, *refs):
    (dql_ref, ql_ref, kl_ref, v_ref) = refs[:4]
    dks, dvs = refs[4 : 4 + parts_in], refs[4 + parts_in : 4 + 2 * parts_in]
    (kg_ref, cos_ref, sin_ref, wq_ref, wk_ref, wv_ref, normed_ref) = refs[
        4 + 2 * parts_in : 11 + 2 * parts_in
    ]
    outs = refs[11 + 2 * parts_in :]
    parts, (dkl_ref, dvl_ref, inner_ref, kpart_ref, npart_ref) = outs[:count], outs[count:]
    width = wq_ref.shape[0] // count

    @pl.when(pl.program_id(0) == 0)
    def _():
        kpart_ref[...] = jnp.zeros_like(kpart_ref)
        npart_ref[...] = jnp.zeros_like(npart_ref)

    grad_keys = sum(r[...].astype(F32) for r in dks)
    dvl_ref[...] = sum(r[...].astype(F32) for r in dvs).astype(BF)
    for h in range(kl_ref.shape[1] // head):
        cut = slice(h * head, (h + 1) * head)
        lin, one = unrotate(
            grad_keys[:, cut], kl_ref[:, cut], kg_ref[...], cos_ref[...], sin_ref[...]
        )
        dkl_ref[:, cut] = lin.astype(BF)
        kpart_ref[...] += one
    grad_q, grad_k, grad_v = dql_ref[...], dkl_ref[...], dvl_ref[...]
    inner_ref[...] = (
        jnp.sum(grad_q.astype(F32) * ql_ref[...], axis=1, keepdims=True)
        + jnp.sum(grad_k.astype(F32) * kl_ref[...], axis=1, keepdims=True)
        + jnp.sum(grad_v.astype(F32) * v_ref[...].astype(F32), axis=1, keepdims=True)
    )
    for s in range(count):
        at = span(offset_ref[count + s], width)
        term = (
            dot_cols(grad_q, wq_ref[at, :])
            + dot_cols(grad_k, wk_ref[at, :])
            + dot_cols(grad_v, wv_ref[at, :])
        )
        parts[s][...] = term.astype(parts[s].dtype)


def out(shape, dtype):
    return jax.ShapeDtypeStruct(shape, dtype)


def rows_block(tile, width):
    return pl.BlockSpec((tile, width), lambda i: (i, 0))


def same_block(shape):
    return pl.BlockSpec(shape, lambda i: (0,) * len(shape))


def call(kernel, grid, in_specs, out_specs, out_shape, flops, scratch=()):
    extra = dict(grid=grid) if grid else {}
    return pl.pallas_call(
        kernel,
        in_specs=in_specs,
        out_specs=out_specs,
        out_shape=out_shape,
        scratch_shapes=scratch,
        compiler_params=pltpu.CompilerParams(vmem_limit_bytes=50 * 2**20),
        cost_estimate=pl.CostEstimate(
            flops=flops, bytes_accessed=4 * 2**20, transcendentals=0
        ),
        **extra,
    )


def per_device(
    tokens,
    norm_gain,
    w_query,
    key_projection,
    value_projection,
    query_gain,
    key_gain,
    w_out,
    ffn_gain,
    w_gate,
    w_up,
    w_down,
    cotangent,
    sequence,
    position,
):
    rows, piece = tokens.shape
    count = lax.axis_size("gx")
    peers = lax.axis_size("gy")
    width = piece * count
    head = query_gain.shape[0]
    q_cols, kv_cols, hidden_units = w_query.shape[1], key_projection.shape[1], w_gate.shape[1]
    gx, gy = lax.axis_index("gx"), lax.axis_index("gy")
    tile = min(256, rows)
    small_tile = min(128, rows)
    grid = (rows // tile,)

    def lies_at(block):
        if peers == 2 and count % 2 == 0:
            half = count // 2
            return ((block // half) ^ gy) * (half * piece) + (block % half) * piece
        return block * piece

    offsets = jnp.stack(
        [lies_at((gx - s) % count) for s in range(count)]
        + [lies_at((gx + s) % count) for s in range(count)]
    ).astype(jnp.int32)

    gains = jnp.stack([norm_gain, ffn_gain] + [norm_gain] * 14).astype(F32)[:8]
    token_pieces = pieces_of(tokens)
    gain_pieces = pieces_of(gains)
    gain_one = jnp.concatenate([g[0:1] for g in gain_pieces], axis=0)
    gain_two = jnp.concatenate([g[1:2] for g in gain_pieces], axis=0)
    full_query, full_key, full_value = (
        gather_width(w, 0) for w in (w_query, key_projection, value_projection)
    )
    full_out = gather_width(w_out, 1)
    full_down = gather_width(w_down, 1)
    full_gate, full_up = gather_width(w_gate, 0), gather_width(w_up, 0)
    cot_pieces = pieces_of(cotangent)

    all_seq, all_pos = sequence.reshape(peers, rows), position.reshape(peers, rows)
    if peers == 2:
        order = lambda a: jnp.where(gy == 0, a, a[::-1])
        all_seq, all_pos = order(all_seq), order(all_pos)
        own_seq, own_pos = all_seq[0], all_pos[0]
    else:
        own_seq = lax.dynamic_index_in_dim(all_seq, gy, 0, False)
        own_pos = lax.dynamic_index_in_dim(all_pos, gy, 0, False)
    row_info = jnp.concatenate(
        [own_seq[None], own_pos[None], jnp.zeros((6, rows), jnp.int32)], axis=0
    )
    col_info = jnp.stack([all_seq, all_pos], axis=-1)
    rates = THETA ** (-(jnp.arange(head // 2, dtype=F32) * 2.0) / head)
    phase = own_pos.astype(F32)[:, None] * rates[None, :]
    cosine = jnp.concatenate([jnp.cos(phase)] * 2, axis=1)
    sine = jnp.concatenate([-jnp.sin(phase), jnp.sin(phase)], axis=1)
    q_scale = query_gain.astype(F32)[None]
    k_scale = key_gain.astype(F32)[None]

    normed_one, scale_one, query_lin, key_lin, query_bf, key_bf, value_bf = call(
        functools.partial(qkv_kernel, count, head),
        grid,
        [SMEM]
        + [rows_block(tile, piece)] * count
        + [
            same_block((count, piece)),
            same_block((width, q_cols)),
            same_block((width, kv_cols)),
            same_block((width, kv_cols)),
            same_block((1, head)),
            same_block((1, head)),
            rows_block(tile, head),
            rows_block(tile, head),
        ],
        [
            rows_block(tile, width),
            rows_block(tile, 1),
            rows_block(tile, q_cols),
            rows_block(tile, kv_cols),
            rows_block(tile, q_cols),
            rows_block(tile, kv_cols),
            rows_block(tile, kv_cols),
        ],
        [
            out((rows, width), BF),
            out((rows, 1), F32),
            out((rows, q_cols), F32),
            out((rows, kv_cols), F32),
            out((rows, q_cols), BF),
            out((rows, kv_cols), BF),
            out((rows, kv_cols), BF),
        ],
        2 * rows * width * (q_cols + 2 * kv_cols),
    )(
        offsets, *token_pieces, gain_one, full_query, full_key, full_value,
        q_scale, k_scale, cosine, sine,
    )

    if peers == 2:
        all_keys = jnp.stack([key_bf, shifted(key_bf, "gy", 1)])
        all_values = jnp.stack([value_bf, shifted(value_bf, "gy", 1)])
    else:
        all_keys = lax.all_gather(key_bf, "gy", axis=0)
        all_values = lax.all_gather(value_bf, "gy", axis=0)

    split_out = [out((rows, piece), F32)] + [out((rows, piece), BF)] * (count - 1)
    attend_flops = 4 * rows * rows * peers * q_cols
    *out_parts, mixed, attended, logs = call(
        functools.partial(attend_kernel, head, small_tile),
        None,
        [SMEM] + [VMEM] * 6,
        [VMEM] * (count + 3),
        split_out
        + [
            out((rows, q_cols), BF),
            out((q_cols, rows), F32),
            out((max(8, q_cols // head), rows), F32),
        ],
        attend_flops + 2 * rows * q_cols * width,
    )(offsets, query_bf, all_keys, all_values, row_info, col_info, full_out)

    cot_whole, grad_product = call(
        functools.partial(cot_kernel, count),
        grid,
        [SMEM] + [rows_block(tile, piece)] * count + [same_block((hidden_units, width))],
        [rows_block(tile, width), rows_block(tile, hidden_units)],
        [out((rows, width), BF), out((rows, hidden_units), F32)],
        2 * rows * width * hidden_units,
    )(offsets, *cot_pieces, full_down)

    inputs = tokens.astype(F32)
    hidden = inputs + piece_sum(out_parts[0], out_parts[1:])
    hidden_pieces = pieces_of(hidden.astype(BF))

    *grad_parts, normed_two, scale_two, product, gate_bf, up_bf = call(
        functools.partial(ffn_kernel, count),
        grid,
        [SMEM]
        + [rows_block(tile, piece)] * count
        + [
            same_block((count, piece)),
            same_block((width, hidden_units)),
            same_block((width, hidden_units)),
            rows_block(tile, hidden_units),
        ],
        [rows_block(tile, piece)] * count
        + [
            rows_block(tile, width),
            rows_block(tile, 1),
            rows_block(tile, hidden_units),
            rows_block(tile, hidden_units),
            rows_block(tile, hidden_units),
        ],
        split_out
        + [
            out((rows, width), BF),
            out((rows, 1), F32),
            out((rows, hidden_units), BF),
            out((rows, hidden_units), BF),
            out((rows, hidden_units), BF),
        ],
        8 * rows * width * hidden_units,
    )(offsets, *hidden_pieces, gain_two, full_gate, full_up, grad_product)

    grad_normed_two = piece_sum(grad_parts[0], grad_parts[1:])
    grad_pieces = pieces_of(grad_normed_two.astype(BF))

    result_parts = call(
        functools.partial(split_dot_kernel, count),
        grid,
        [SMEM, rows_block(tile, hidden_units), same_block((hidden_units, width))],
        [rows_block(tile, piece)] * count,
        split_out,
        2 * rows * width * hidden_units,
    )(offsets, product, full_down)
    result = hidden + piece_sum(result_parts[0], result_parts[1:])

    def rows_share(whole, grads):
        return scatter_width(
            lambda start, size: dot_rows(whole[:, start : start + size], grads), 0, width
        )

    def cols_share(left, whole):
        return scatter_width(
            lambda start, size: dot_rows(left, whole[:, start : start + size]), 1, width
        )

    down_grad = cols_share(product, cot_whole)
    gate_grad = rows_share(normed_two, gate_bf)
    up_grad = rows_share(normed_two, up_bf)
    down_grad, gate_grad, up_grad = dev_sum([down_grad, gate_grad, up_grad])

    branch, grad_query_lin, key_parts, value_parts, query_gain_part = call(
        functools.partial(attend_back_kernel, count, head, small_tile),
        None,
        [SMEM] + [VMEM] * (2 * count + 15),
        [VMEM] * 5,
        [
            out((rows, width), BF),
            out((rows, q_cols), BF),
            out((peers, rows, kv_cols), BF),
            out((peers, rows, kv_cols), BF),
            out((1, head), F32),
        ],
        5 * attend_flops // 2 + 2 * rows * q_cols * width,
        [pltpu.VMEM((peers, rows, kv_cols), F32), pltpu.VMEM((peers, rows, kv_cols), F32)],
    )(
        offsets, *hidden_pieces, *grad_pieces, gain_two, scale_two, cot_whole, full_out,
        query_bf, query_lin, all_keys, all_values, row_info, col_info, attended, logs,
        q_scale, cosine, sine,
    )
    if peers == 2:
        key_terms = [key_parts[0], shifted(key_parts[1], "gy", 1)]
        value_terms = [value_parts[0], shifted(value_parts[1], "gy", 1)]
    else:
        share = lambda a: lax.psum_scatter(a, "gy", scatter_dimension=0, tiled=True)[0]
        key_terms, value_terms = [share(key_parts)], [share(value_parts)]

    out_grad = cols_share(mixed, branch)
    (out_grad,) = dev_sum([out_grad])

    *last_parts, grad_key_lin, grad_value_lin, inner_part, key_gain_part, _ = call(
        functools.partial(lin_back_kernel, count, head, len(key_terms)),
        grid,
        [SMEM]
        + [rows_block(tile, q_cols), rows_block(tile, q_cols), rows_block(tile, kv_cols)]
        + [rows_block(tile, kv_cols)] * (1 + 2 * len(key_terms))
        + [
            same_block((1, head)),
            rows_block(tile, head),
            rows_block(tile, head),
            same_block((width, q_cols)),
            same_block((width, kv_cols)),
            same_block((width, kv_cols)),
            rows_block(tile, width),
        ],
        [rows_block(tile, piece)] * count
        + [
            rows_block(tile, kv_cols),
            rows_block(tile, kv_cols),
            rows_block(tile, 1),
            same_block((1, head)),
            same_block((1, head)),
        ],
        split_out
        + [
            out((rows, kv_cols), BF),
            out((rows, kv_cols), BF),
            out((rows, 1), F32),
            out((1, head), F32),
            out((1, head), F32),
        ],
        2 * rows * width * (q_cols + 2 * kv_cols),
    )(
        offsets, grad_query_lin, query_lin, key_lin, value_bf, *key_terms, *value_terms,
        k_scale, cosine, sine, full_query, full_key, full_value, normed_one,
    )

    query_grad = rows_share(normed_one, grad_query_lin)
    key_grad = rows_share(normed_one, grad_key_lin)
    value_grad = rows_share(normed_one, grad_value_lin)
    query_grad, key_grad, value_grad = dev_sum([query_grad, key_grad, value_grad])

    pad = lambda a, n: jnp.pad(a, ((0, 0), (0, n - a.shape[1])))
    wide = max(rows, head)
    small = jnp.concatenate(
        [
            pad(inner_part.reshape(1, rows), wide),
            pad(query_gain_part, wide),
            pad(key_gain_part, wide),
            jnp.zeros((5, wide), F32),
        ],
        axis=0,
    )
    small = small_sum(small, "gx")
    inner_one = small[0, :rows][:, None] / scale_one

    grad_normed_one = piece_sum(last_parts[0], last_parts[1:])
    own_gain_one, own_gain_two = norm_gain.astype(F32), ffn_gain.astype(F32)
    scaled_two = grad_normed_two * own_gain_two
    inner_two = sum(
        jnp.sum(h.astype(F32) * g.astype(F32) * gain_two[s], axis=1, keepdims=True)
        for s, (h, g) in enumerate(zip(hidden_pieces, grad_pieces))
    )
    grad_hidden = (
        cotangent.astype(F32)
        + scale_two * scaled_two
        - hidden * scale_two**3 * (inner_two / width)
    )
    grad_inputs = (
        grad_hidden
        + scale_one * own_gain_one * grad_normed_one
        - inputs * scale_one**3 * (inner_one / width)
    )
    gain_two_part = jnp.sum(grad_normed_two * hidden * scale_two, axis=0)
    gain_one_part = jnp.sum(grad_normed_one * inputs * scale_one, axis=0)
    last = jnp.concatenate([gain_one_part, gain_two_part, small[1, :head], small[2, :head]])
    length = last.shape[0]
    last = jnp.pad(last, (0, -length % 1024)).reshape(8, -1)
    if peers == 2:
        last = small_sum(small_sum(last, "gy"), "dev")
    else:
        last = lax.psum(last, ("dev", "gy"))
    last = last.reshape(-1)
    return (
        result.astype(BF),
        grad_inputs,
        last[:piece],
        query_grad,
        key_grad,
        value_grad,
        last[2 * piece : 2 * piece + head],
        last[2 * piece + head : 2 * piece + 2 * head],
        out_grad,
        last[piece : 2 * piece],
        gate_grad,
        up_grad,
        down_grad,
    )


def solution(mesh):
    wide = P(("dev", "gy"), "gx")
    weight, back = P("gy", "gx"), P("gx", "gy")
    return jax.shard_map(
        per_device,
        mesh=mesh,
        in_specs=(
            wide, P("gx"), weight, weight, weight, P(), P(), back, P("gx"), weight, weight, back,
            wide, P("dev"), P("dev"),
        ),
        out_specs=(
            wide, wide, P("gx"), weight, weight, weight, P(), P(), back, P("gx"), weight, weight,
            back,
        ),
        check_vma=False,
    )
```

time: 587 us -> 386 us (0.66)
  waiting for transfers between devices: 352 us -> 160 us
  starting transfers between devices: 1.36 us -> 114 us
  matrix products: 87.2 us -> 19.8 us
  blocking collectives: 67.1 us -> 0 us
  Pallas kernels: 0 us -> 40.3 us
  other arithmetic: 38.1 us -> 17.2 us
  between operations: 15.2 us -> 2.41 us
  local copies, waits for them, and re-layouts: 16.7 us -> 26.6 us
    ppermute x0 -> x94, waiting for transfers between devices: none -> 160 us  [the longest x52 106 us: shifted(): lax.ppermute(block, axis, [(i, (i + shift) % size) for i in range(size)])]
    all_gather x11 -> x0, waiting for transfers between devices: 123 us -> none  [the longest x4 107 us: row_pieces(): return lax.all_gather(block, 'gx', axis=1, tiled=True)]
    reduce_scatter x11 -> x0, waiting for transfers between devices: 123 us -> none  [the longest x4 89.8 us: head_sums(): lax.psum_scatter(term.astype(jnp.bfloat16), 'gx', scatter_dimension=1, ti...]
    ppermute x0 -> x94, starting transfers between devices: none -> 114 us  [the longest x52 64.3 us: shifted(): lax.ppermute(block, axis, [(i, (i + shift) % size) for i in range(size)])]
    psum x1 -> x0, waiting for transfers between devices: 102 us -> none  [per_device(): lax.psum(narrowed[5].astype(jnp.bfloat16), 'dev').astype(jnp.float32)]
    dot_general x27 -> x14, matrix products: 87.2 us -> 19.8 us  [dot_rows(): lax.dot_general(left, right, (((0,), (0,)), ((), ())), preferred_element_...]
    psum x5 -> x0, blocking collectives: 54.4 us -> none  [the longest x4 41.7 us: row_stats(): return lax.psum(parts, 'gx')]
    pallas_call x0 -> x7, Pallas kernels: none -> 40.3 us  [the longest x1 10.5 us: per_device(): call(functools.partial(attend_back_kernel, count, head, small_tile), None...]
  transfers between devices with their start and end apart: 23 -> 94, of which waited for: 14 -> 38; matrix products, arithmetic and copies ran while one was open for 19% -> 14% of each run, Pallas kernels for 0% -> 9%
where the time goes in v1:
time: 386 us; the launch traced here: 380 us
  waiting for transfers between devices  160 us (41%)
  starting transfers between devices  114 us (30%)
  Pallas kernels  40.3 us (10%)
  local copies, waits for them, and re-layouts  26.6 us (7%)
  matrix products  19.8 us (5%)
  other arithmetic  17.2 us (4%)
    ppermute x52, waiting for transfers between devices, shifted(): lax.ppermute(block, axis, [(i, (i + shift) % size) for i in range(size)])  106 us
    ppermute x52, starting transfers between devices, shifted(): lax.ppermute(block, axis, [(i, (i + shift) % size) for i in range(size)])  64.3 us
    ppermute x42, waiting for transfers between devices, send(): lax.ppermute(block, 'dev', [(i, i ^ m if even else (i + m) % count) for i...  54 us
    ppermute x42, starting transfers between devices, send(): lax.ppermute(block, 'dev', [(i, i ^ m if even else (i + m) % count) for i...  49.5 us
    dot_general x14, matrix products, dot_rows(): lax.dot_general(left, right, (((0,), (0,)), ((), ())), preferred_element_...  19.8 us
    unnamed x141, local copies, waits for them, and re-layouts  15.1 us
    pallas_call x1, Pallas kernels, per_device(): call(functools.partial(attend_back_kernel, count, head, small_tile), None...  10.5 us
  transfers between devices with their start and end apart: 94, of which 38 were waited for; matrix products, arithmetic and copies ran while one was open for 14% of the time, Pallas kernels for 9%

profile of v1, /device:TPU:0, one launch (start us, length us, event | category | flops | bytes accessed | tf_op | source)
XLA Modules:
  0.0 379.6 jit_solution(12549237643869558701)
XLA Ops:
  0.7 3.1 collective-permute-start
  3.8 2.6 collective-permute-start.1
  13.9 2.1 constant_dynamic-update-slice_fusion.9
  16.6 7.7 %collective-permute-done.4 = f32[8,256]{1,0:T(8,128)S(1)} collective-permute-done((f32[8,256]{1,0:T(8,128)S(1)}, f32[8,256]{1,0:T(8,128)S(1)}, u32[]{:S(2)}, u32[]{:S(2)}) %collective-permute-start.4) | collective-permute-done | bytes 8224 | tf_op jit(solution)/shard_map/ppermute | solution.py:41
  26.0 1.5 collective-permute-start.2
  29.3 5.1 %collective-permute-done.2.refs_3_ = bf16[512,256]{1,0:T(8,128)(2,1)S(1)} collective-permute-done((bf16[512,256]{1,0:T(8,128)(2,1)S(1)}, bf16[512,256]{1,0:T(8,128)(2,1)S(1)}, u32[]{:S(2)}, u32[]{:S(2)}) %collective-permute-start.2) | collective-permute-done | bytes 262176 | tf_op jit(solution)/shard_map/ppermute | solution.py:41
  34.4 4.8 %shard_map.246 = (bf16[512,1024]{1,0:T(8,128)(2,1)}, f32[512,1]{1,0:T(8,128)S(1)}, f32[512,512]{1,0:T(8,128)}, f32[512,256]{1,0:T(8,128)S(1)}, bf16[512,512]{1,0...) custom-call(s32[8]{0:T(128)S(1)} %stack.82.offset_ref, bf16[512,256]{1,0:T(8,128)(2,1)S(1)} %copy-done.3, ...), custom_call_target="tpu_custom_call" | custom-call | flops 1073741824 | bytes 4194304 | tf_op jit(solution)/shard_map/pallas_call | solution.py:507
  43.1 1.9 constant_dynamic-update-slice_fusion.6.wo_ref.refs_11_
  47.3 7.5 %shard_map.247 = (f32[512,256]{1,0:T(8,128)S(1)}, bf16[512,256]{1,0:T(8,128)(2,1)S(1)}, bf16[512,256]{1,0:T(8,128)(2,1)S(1)}, bf16[512,256]{1,0:T(8,128)(2,1)S(1...) custom-call(s32[8]{0:T(128)S(1)} %stack.82.offset_ref, ...), custom_call_target="tpu_custom_call" | custom-call | flops 1610612736 | bytes 4194304 | tf_op jit(solution)/shard_map/pallas_call | solution.py:555
  54.8 3.3 collective-permute-start.14
  58.8 2.7 pad_maximum_fusion.refs_5_
  61.5 3.4 collective-permute-done.14
  65.2 27.1 %collective-permute-done.13 = bf16[512,256]{1,0:T(8,128)(2,1)S(1)} collective-permute-done((bf16[512,256]{1,0:T(8,128)(2,1)S(1)}, bf16[512,256]{1,0:T(8,128)(2,1)S(1)}, u32[]{:S(2)}, u32[]{:S(2)}) %collective-permute-start.13) | collective-permute-done | bytes 262176 | tf_op jit(solution)/shard_map/ppermute | solution.py:41
  92.5 2.1 collective-permute-start.15
  94.6 17.5 %collective-permute-done.21.refs_2_ = bf16[512,256]{1,0:T(8,128)(2,1)S(1)} collective-permute-done((bf16[512,256]{1,0:T(8,128)(2,1)S(1)}, bf16[512,256]{1,0:T(8,128)(2,1)S(1)}, u32[]{:S(2)}, u32[]{:S(2)}) %collective-permute-start.21) | collective-permute-done | bytes 262176 | tf_op jit(solution)/shard_map/ppermute | solution.py:41
  114.8 2.7 shard_map.248
  119.2 5.7 %collective-permute-done.16.refs_2_ = bf16[512,256]{1,0:T(8,128)(2,1)S(1)} collective-permute-done((bf16[512,256]{1,0:T(8,128)(2,1)S(1)}, bf16[512,256]{1,0:T(8,128)(2,1)S(1)}, u32[]{:S(2)}, u32[]{:S(2)}) %collective-permute-start.16) | collective-permute-done | bytes 262176 | tf_op jit(solution)/shard_map/ppermute | solution.py:41
  124.9 7.6 %shard_map.249 = (f32[512,256]{1,0:T(8,128)S(1)}, bf16[512,256]{1,0:T(8,128)(2,1)S(1)}, bf16[512,256]{1,0:T(8,128)(2,1)S(1)}, bf16[512,256]{1,0:T(8,128)(2,1)S(1...) custom-call(s32[8]{0:T(128)S(1)} %stack.82.offset_ref, ...), custom_call_target="tpu_custom_call" | custom-call | flops 3221225472 | bytes 4194304 | tf_op jit(solution)/shard_map/pallas_call | solution.py:582
  132.7 5.5 %collective-permute-start.29 = (bf16[512,256]{1,0:T(8,128)(2,1)S(1)}, bf16[512,256]{1,0:T(8,128)(2,1)S(1)}, u32[]{:S(2)}, u32[]{:S(2)}) collective-permute-start(bf16[512,256]{1,0:T(8,128)(2,1)S(1)} %get-tuple-element.72), channel_id=1, source_target_pairs={{0,6},{2,0},{4,2},{6,4},{1,7},{3,1},{5,3},{7,5},{8,14},{10,8},{12,... | collective-permute-start | bytes 786440 | tf_op jit(solution)/shard_map/ppermute | solution.py:41
  139.1 1.8 shard_map.250
  140.9 3.9 %collective-permute-start.26 = (bf16[512,256]{1,0:T(8,128)(2,1)S(1)}, bf16[512,256]{1,0:T(8,128)(2,1)S(1)}, u32[]{:S(2)}, u32[]{:S(2)}) collective-permute-start(bf16[512,256]{1,0:T(8,128)(2,1)S(1)} %get-tuple-element.67), channel_id=1, source_target_pairs={{0,6},{2,0},{4,2},{6,4},{1,7},{3,1},{5,3},{7,5},{8,14},{10,8},{12,... | collective-permute-start | bytes 786440 | tf_op jit(solution)/shard_map/ppermute | solution.py:41
  146.5 11.6 %collective-permute-start.24 = (bf16[512,256]{1,0:T(8,128)(2,1)S(1)}, bf16[512,256]{1,0:T(8,128)(2,1)S(1)}, u32[]{:S(2)}, u32[]{:S(2)}) collective-permute-start(bf16[512,256]{1,0:T(8,128)(2,1)S(1)} %get-tuple-element.65), channel_id=1, source_target_pairs={{0,2},{2,4},{4,6},{6,0},{1,3},{3,5},{5,7},{7,1},{8,10},{10,12},{12... | collective-permute-start | bytes 786440 | tf_op jit(solution)/shard_map/ppermute | solution.py:41
  159.6 14.8 %collective-permute-done.28 = bf16[512,256]{1,0:T(8,128)(2,1)S(1)} collective-permute-done((bf16[512,256]{1,0:T(8,128)(2,1)S(1)}, bf16[512,256]{1,0:T(8,128)(2,1)S(1)}, u32[]{:S(2)}, u32[]{:S(2)}) %collective-permute-start.28) | collective-permute-done | bytes 262176 | tf_op jit(solution)/shard_map/ppermute | solution.py:41
  174.9 8.5 %collective-permute-done.25 = bf16[512,256]{1,0:T(8,128)(2,1)S(1)} collective-permute-done((bf16[512,256]{1,0:T(8,128)(2,1)S(1)}, bf16[512,256]{1,0:T(8,128)(2,1)S(1)}, u32[]{:S(2)}, u32[]{:S(2)}) %collective-permute-start.25) | collective-permute-done | bytes 262176 | tf_op jit(solution)/shard_map/ppermute | solution.py:41
  185.2 2.0 collective-permute-start.31
  187.2 2.8 collective-permute-start.32
  191.5 4.2 %collective-permute-done.30.refs_5_ = bf16[512,256]{1,0:T(8,128)(2,1)S(1)} collective-permute-done((bf16[512,256]{1,0:T(8,128)(2,1)S(1)}, bf16[512,256]{1,0:T(8,128)(2,1)S(1)}, u32[]{:S(2)}, u32[]{:S(2)}) %collective-permute-start.30) | collective-permute-done | bytes 262176 | tf_op jit(solution)/shard_map/ppermute | solution.py:41
  195.8 8.1 %collective-permute-done.31.refs_6_ = bf16[512,256]{1,0:T(8,128)(2,1)S(1)} collective-permute-done((bf16[512,256]{1,0:T(8,128)(2,1)S(1)}, bf16[512,256]{1,0:T(8,128)(2,1)S(1)}, u32[]{:S(2)}, u32[]{:S(2)}) %collective-permute-start.31) | collective-permute-done | bytes 262176 | tf_op jit(solution)/shard_map/ppermute | solution.py:41
  203.9 10.5 %shard_map.251 = (bf16[512,1024]{1,0:T(8,128)(2,1)}, bf16[512,512]{1,0:T(8,128)(2,1)S(1)}, bf16[2,512,256]{2,1,0:T(8,128)(2,1)S(1)}, bf16[2,512,256]{2,1,0:T(8,128)(2,1)}, f32[1,128]{1,0:T(1,128)S(1)}) custom-call(s32[8]{0:T(128)S(1)} %stack.82.offset_ref, bf16[512,256]{1,0:T(8,128)(2,1)S(1)} %get-tuple-element.106.refs_0_, ...), custom_call_target="tpu_custom_call" | custom-call | flops 3221225472 | bytes 4194304 | tf_op jit(solution)/shard_map/pallas_call | solution.py:640
  219.4 5.3 %shard_map.252 = (f32[512,256]{1,0:T(8,128)S(1)}, bf16[512,256]{1,0:T(8,128)(2,1)S(1)}, bf16[512,256]{1,0:T(8,128)(2,1)S(1)}, bf16[512,256]{1,0:T(8,128)(2,1)S(1...) custom-call(s32[8]{0:T(128)S(1)} %stack.82.offset_ref, ...), custom_call_target="tpu_custom_call" | custom-call | flops 1073741824 | bytes 4194304 | tf_op jit(solution)/shard_map/pallas_call | solution.py:669
  227.7 8.3 %collective-permute-start.40 = (f32[8,512]{1,0:T(8,128)S(1)}, f32[8,512]{1,0:T(8,128)S(1)}, u32[]{:S(2)}, u32[]{:S(2)}) collective-permute-start(f32[8,512]{1,0:T(8,128)S(1)} %fusion.21), channel_id=1, source_target_pairs={{0,6},{2,0},{4,2},{6,4},{1,7},{3,1},{5,3},{7,5},{8,14},{10,8},{12,... | collective-permute-start | bytes 49160 | tf_op jit(solution)/shard_map/ppermute | solution.py:41
  236.7 3.3 fusion.45
  240.0 3.3 collective-permute-start.37
  243.3 2.9 fusion.46
  250.0 2.4 collective-permute-start.76
  252.5 2.9 fusion.47
  257.2 2.4 collective-permute-start.83
  260.8 4.3 %collective-permute-done.75 = bf16[128,768]{1,0:T(8,128)(2,1)S(1)} collective-permute-done((bf16[128,768]{1,0:T(8,128)(2,1)}, bf16[128,768]{1,0:T(8,128)(2,1)S(1)}, u32[]{:S(2)}, u32[]{:S(2)}) %collective-permute-start.75) | collective-permute-done | bytes 196640 | tf_op jit(solution)/shard_map/ppermute | solution.py:86
  265.1 2.9 collective-permute-start.81
  274.6 2.1 collective-permute-done.90
  279.7 2.6 collective-permute-done.88
  284.3 2.1 collective-permute-done.36
  286.5 1.7 collective-permute-start.77
  288.2 2.3 fusion.3
  297.4 2.3 collective-permute-start.55
  302.9 2.1 collective-permute-start.62
  306.5 1.6 collective-permute-done.62
  308.1 2.2 collective-permute-start.48
  311.9 3.8 collective-permute-done.56
  316.6 4.0 %collective-permute-done.57 = bf16[128,256]{1,0:T(8,128)(2,1)S(1)} collective-permute-done((bf16[128,256]{1,0:T(8,128)(2,1)S(1)}, bf16[128,256]{1,0:T(8,128)(2,1)S(1)}, u32[]{:S(2)}, u32[]{:S(2)}) %collective-permute-start.57) | collective-permute-done | bytes 65568 | tf_op jit(solution)/shard_map/ppermute | solution.py:86
  320.6 1.9 collective-permute-start.58
  322.5 3.3 collective-permute-done.58
  325.9 4.6 %collective-permute-done.63 = bf16[128,256]{1,0:T(8,128)(2,1)S(1)} collective-permute-done((bf16[128,256]{1,0:T(8,128)(2,1)S(1)}, bf16[128,256]{1,0:T(8,128)(2,1)S(1)}, u32[]{:S(2)}, u32[]{:S(2)}) %collective-permute-start.63) | collective-permute-done | bytes 65568 | tf_op jit(solution)/shard_map/ppermute | solution.py:86
  331.6 3.1 collective-permute-done.64
  334.8 1.9 collective-permute-start.65
  336.7 3.4 collective-permute-done.65
  341.1 1.5 collective-permute-start.69
  343.7 2.8 collective-permute-done.46
  347.7 2.1 collective-permute-done.69
  356.9 1.6 collective-permute-done.79
  359.7 2.7 collective-permute-done.84
  362.4 1.8 collective-permute-start.93
  364.9 2.1 collective-permute-done.86
  376.5 1.9 collective-permute-done.72
  (394 shorter events, 95.4 us)
Async XLA Ops:
  0.7 27.6 %collective-permute-start = (bf16[512,256]{1,0:T(8,128)(2,1)}, bf16[512,256]{1,0:T(8,128)(2,1)S(1)}, u32[]{:S(2)}, u32[]{:S(2)}) collective-permute-start(bf16[512,256]{1,0:T(8,128)(2,1)} %refs_0_.2), channel_id=1, source_target_pairs={{0,2},{2,4},{4,6},{6,0},{1,3},{3,5},{5,7},{7,1},{8,10},{10,12},{12... | collective-permute-start | bytes 786440 | tf_op jit(solution)/shard_map/ppermute | solution.py:41
  3.8 24.7 %collective-permute-start.1 = (bf16[512,256]{1,0:T(8,128)(2,1)}, bf16[512,256]{1,0:T(8,128)(2,1)S(1)}, u32[]{:S(2)}, u32[]{:S(2)}) collective-permute-start(bf16[512,256]{1,0:T(8,128)(2,1)} %refs_0_.2), channel_id=1, source_target_pairs={{0,4},{2,6},{4,0},{6,2},{1,5},{3,7},{5,1},{7,3},{8,12},{10,14},{12... | collective-permute-start | bytes 786440 | tf_op jit(solution)/shard_map/ppermute | solution.py:41
  7.7 8.8 %collective-permute-start.5 = (f32[8,256]{1,0:T(8,128)S(1)}, f32[8,256]{1,0:T(8,128)S(1)}, u32[]{:S(2)}, u32[]{:S(2)}) collective-permute-start(f32[8,256]{1,0:T(8,128)S(1)} %slice.145), channel_id=1, source_target_pairs={{0,6},{2,0},{4,2},{6,4},{1,7},{3,1},{5,3},{7,5},{8,14},{10,8},{12,... | collective-permute-start | bytes 24584 | tf_op jit(solution)/shard_map/ppermute | solution.py:41
  9.2 15.1 %collective-permute-start.4 = (f32[8,256]{1,0:T(8,128)S(1)}, f32[8,256]{1,0:T(8,128)S(1)}, u32[]{:S(2)}, u32[]{:S(2)}) collective-permute-start(f32[8,256]{1,0:T(8,128)S(1)} %slice.145), channel_id=1, source_target_pairs={{0,4},{2,6},{4,0},{6,2},{1,5},{3,7},{5,1},{7,3},{8,12},{10,14},{12... | collective-permute-start | bytes 24584 | tf_op jit(solution)/shard_map/ppermute | solution.py:41
  9.3 15.0 %collective-permute-start.3 = (f32[8,256]{1,0:T(8,128)S(1)}, f32[8,256]{1,0:T(8,128)S(1)}, u32[]{:S(2)}, u32[]{:S(2)}) collective-permute-start(f32[8,256]{1,0:T(8,128)S(1)} %slice.145), channel_id=1, source_target_pairs={{0,2},{2,4},{4,6},{6,0},{1,3},{3,5},{5,7},{7,1},{8,10},{10,12},{12... | collective-permute-start | bytes 24584 | tf_op jit(solution)/shard_map/ppermute | solution.py:41
  16.5 11.2 %collective-permute-start.6 = (bf16[512,512]{1,0:T(8,128)(2,1)}, bf16[512,512]{1,0:T(8,128)(2,1)S(1)}, u32[]{:S(2)}, u32[]{:S(2)}) collective-permute-start(bf16[512,512]{1,0:T(8,128)(2,1)} %param.17), channel_id=1, source_target_pairs={{0,1},{1,0},{2,3},{3,2},{4,5},{5,4},{6,7},{7,6},{8,9},{9,8},{10,11... | collective-permute-start | bytes 1572872 | tf_op jit(solution)/shard_map/ppermute | solution.py:41
  26.0 8.3 %collective-permute-start.2 = (bf16[512,256]{1,0:T(8,128)(2,1)S(1)}, bf16[512,256]{1,0:T(8,128)(2,1)S(1)}, u32[]{:S(2)}, u32[]{:S(2)}) collective-permute-start(bf16[512,256]{1,0:T(8,128)(2,1)S(1)} %copy-done.3), channel_id=1, source_target_pairs={{0,6},{2,0},{4,2},{6,4},{1,7},{3,1},{5,3},{7,5},{8,14},{10,8},{12,... | collective-permute-start | bytes 786440 | tf_op jit(solution)/shard_map/ppermute | solution.py:41
  27.6 15.4 %collective-permute-start.11 = (bf16[512,512]{1,0:T(8,128)(2,1)}, bf16[512,512]{1,0:T(8,128)(2,1)}, u32[]{:S(2)}, u32[]{:S(2)}) collective-permute-start(bf16[512,512]{1,0:T(8,128)(2,1)} %param.22), channel_id=1, source_target_pairs={{0,1},{1,0},{2,3},{3,2},{4,5},{5,4},{6,7},{7,6},{8,9},{9,8},{10,11... | collective-permute-start | bytes 1572872 | tf_op jit(solution)/shard_map/ppermute | solution.py:41
  27.7 84.4 %collective-permute-start.23 = (bf16[768,512]{1,0:T(8,128)(2,1)}, bf16[768,512]{1,0:T(8,128)(2,1)}, u32[]{:S(2)}, u32[]{:S(2)}) collective-permute-start(bf16[768,512]{1,0:T(8,128)(2,1)} %param.26), channel_id=1, source_target_pairs={{0,1},{1,0},{2,3},{3,2},{4,5},{5,4},{6,7},{7,6},{8,9},{9,8},{10,11... | collective-permute-start | bytes 2359304 | tf_op jit(solution)/shard_map/ppermute | solution.py:41
  28.3 29.8 %collective-permute-start.18 = (bf16[512,768]{1,0:T(8,128)(2,1)}, bf16[512,768]{1,0:T(8,128)(2,1)}, u32[]{:S(2)}, u32[]{:S(2)}) collective-permute-start(bf16[512,768]{1,0:T(8,128)(2,1)} %param.24), channel_id=1, source_target_pairs={{0,1},{1,0},{2,3},{3,2},{4,5},{5,4},{6,7},{7,6},{8,9},{9,8},{10,11... | collective-permute-start | bytes 2359304 | tf_op jit(solution)/shard_map/ppermute | solution.py:41
  43.0 74.5 %collective-permute-start.19 = (bf16[512,768]{1,0:T(8,128)(2,1)}, bf16[512,768]{1,0:T(8,128)(2,1)S(1)}, u32[]{:S(2)}, u32[]{:S(2)}) collective-permute-start(bf16[512,768]{1,0:T(8,128)(2,1)} %param.25), channel_id=1, source_target_pairs={{0,1},{1,0},{2,3},{3,2},{4,5},{5,4},{6,7},{7,6},{8,9},{9,8},{10,11... | collective-permute-start | bytes 2359304 | tf_op jit(solution)/shard_map/ppermute | solution.py:41
  54.8 10.0 %collective-permute-start.14 = (bf16[512,256]{1,0:T(8,128)(2,1)S(1)}, bf16[512,256]{1,0:T(8,128)(2,1)S(1)}, u32[]{:S(2)}, u32[]{:S(2)}) collective-permute-start(bf16[512,256]{1,0:T(8,128)(2,1)S(1)} %get-tuple-element.61), channel_id=1, source_target_pairs={{0,6},{2,0},{4,2},{6,4},{1,7},{3,1},{5,3},{7,5},{8,14},{10,8},{12,... | collective-permute-start | bytes 786440 | tf_op jit(solution)/shard_map/ppermute | solution.py:41
  58.1 34.1 %collective-permute-start.13 = (bf16[512,256]{1,0:T(8,128)(2,1)S(1)}, bf16[512,256]{1,0:T(8,128)(2,1)S(1)}, u32[]{:S(2)}, u32[]{:S(2)}) collective-permute-start(bf16[512,256]{1,0:T(8,128)(2,1)S(1)} %get-tuple-element.60), channel_id=1, source_target_pairs={{0,4},{2,6},{4,0},{6,2},{1,5},{3,7},{5,1},{7,3},{8,12},{10,14},{12... | collective-permute-start | bytes 786440 | tf_op jit(solution)/shard_map/ppermute | solution.py:41
  58.1 34.1 %collective-permute-start.12 = (bf16[512,256]{1,0:T(8,128)(2,1)S(1)}, bf16[512,256]{1,0:T(8,128)(2,1)S(1)}, u32[]{:S(2)}, u32[]{:S(2)}) collective-permute-start(bf16[512,256]{1,0:T(8,128)(2,1)S(1)} %get-tuple-element.59), channel_id=1, source_target_pairs={{0,2},{2,4},{4,6},{6,0},{1,3},{3,5},{5,7},{7,1},{8,10},{10,12},{12... | collective-permute-start | bytes 786440 | tf_op jit(solution)/shard_map/ppermute | solution.py:41
  64.8 27.6 %collective-permute-start.20 = (bf16[512,256]{1,0:T(8,128)(2,1)S(1)}, bf16[512,256]{1,0:T(8,128)(2,1)S(1)}, u32[]{:S(2)}, u32[]{:S(2)}) collective-permute-start(bf16[512,256]{1,0:T(8,128)(2,1)S(1)} %copy-done.17), channel_id=1, source_target_pairs={{0,2},{2,4},{4,6},{6,0},{1,3},{3,5},{5,7},{7,1},{8,10},{10,12},{12... | collective-permute-start | bytes 786440 | tf_op jit(solution)/shard_map/ppermute | solution.py:41
  92.3 19.8 %collective-permute-start.21 = (bf16[512,256]{1,0:T(8,128)(2,1)S(1)}, bf16[512,256]{1,0:T(8,128)(2,1)S(1)}, u32[]{:S(2)}, u32[]{:S(2)}) collective-permute-start(bf16[512,256]{1,0:T(8,128)(2,1)S(1)} %copy-done.17), channel_id=1, source_target_pairs={{0,4},{2,6},{4,0},{6,2},{1,5},{3,7},{5,1},{7,3},{8,12},{10,14},{12... | collective-permute-start | bytes 786440 | tf_op jit(solution)/shard_map/ppermute | solution.py:41
  92.3 21.4 %collective-permute-start.22 = (bf16[512,256]{1,0:T(8,128)(2,1)S(1)}, bf16[512,256]{1,0:T(8,128)(2,1)S(1)}, u32[]{:S(2)}, u32[]{:S(2)}) collective-permute-start(bf16[512,256]{1,0:T(8,128)(2,1)S(1)} %copy-done.17), channel_id=1, source_target_pairs={{0,6},{2,0},{4,2},{6,4},{1,7},{3,1},{5,3},{7,5},{8,14},{10,8},{12,... | collective-permute-start | bytes 786440 | tf_op jit(solution)/shard_map/ppermute | solution.py:41
  92.5 26.7 %collective-permute-start.15 = (bf16[512,256]{1,0:T(8,128)(2,1)S(1)}, bf16[512,256]{1,0:T(8,128)(2,1)S(1)}, u32[]{:S(2)}, u32[]{:S(2)}) collective-permute-start(bf16[512,256]{1,0:T(8,128)(2,1)S(1)} %get-tuple-element.106.refs_0_), channel_id=1, source_target_pairs={{0,2},{2,4},{4,6},{6,0},{1,3},{3,5},{5,7},{7,1},{8,10},{10,12},{12... | collective-permute-start | bytes 786440 | tf_op jit(solution)/shard_map/ppermute | solution.py:41
  112.1 12.8 %collective-permute-start.16 = (bf16[512,256]{1,0:T(8,128)(2,1)S(1)}, bf16[512,256]{1,0:T(8,128)(2,1)S(1)}, u32[]{:S(2)}, u32[]{:S(2)}) collective-permute-start(bf16[512,256]{1,0:T(8,128)(2,1)S(1)} %get-tuple-element.106.refs_0_), channel_id=1, source_target_pairs={{0,4},{2,6},{4,0},{6,2},{1,5},{3,7},{5,1},{7,3},{8,12},{10,14},{12... | collective-permute-start | bytes 786440 | tf_op jit(solution)/shard_map/ppermute | solution.py:41
  112.1 12.8 %collective-permute-start.17 = (bf16[512,256]{1,0:T(8,128)(2,1)S(1)}, bf16[512,256]{1,0:T(8,128)(2,1)S(1)}, u32[]{:S(2)}, u32[]{:S(2)}) collective-permute-start(bf16[512,256]{1,0:T(8,128)(2,1)S(1)} %get-tuple-element.106.refs_0_), channel_id=1, source_target_pairs={{0,6},{2,0},{4,2},{6,4},{1,7},{3,1},{5,3},{7,5},{8,14},{10,8},{12,... | collective-permute-start | bytes 786440 | tf_op jit(solution)/shard_map/ppermute | solution.py:41
  132.7 13.8 %collective-permute-start.29 = (bf16[512,256]{1,0:T(8,128)(2,1)S(1)}, bf16[512,256]{1,0:T(8,128)(2,1)S(1)}, u32[]{:S(2)}, u32[]{:S(2)}) collective-permute-start(bf16[512,256]{1,0:T(8,128)(2,1)S(1)} %get-tuple-element.72), channel_id=1, source_target_pairs={{0,6},{2,0},{4,2},{6,4},{1,7},{3,1},{5,3},{7,5},{8,14},{10,8},{12,... | collective-permute-start | bytes 786440 | tf_op jit(solution)/shard_map/ppermute | solution.py:41
  138.2 36.2 %collective-permute-start.28 = (bf16[512,256]{1,0:T(8,128)(2,1)S(1)}, bf16[512,256]{1,0:T(8,128)(2,1)S(1)}, u32[]{:S(2)}, u32[]{:S(2)}) collective-permute-start(bf16[512,256]{1,0:T(8,128)(2,1)S(1)} %get-tuple-element.71), channel_id=1, source_target_pairs={{0,4},{2,6},{4,0},{6,2},{1,5},{3,7},{5,1},{7,3},{8,12},{10,14},{12... | collective-permute-start | bytes 786440 | tf_op jit(solution)/shard_map/ppermute | solution.py:41
  139.1 35.3 %collective-permute-start.27 = (bf16[512,256]{1,0:T(8,128)(2,1)S(1)}, bf16[512,256]{1,0:T(8,128)(2,1)S(1)}, u32[]{:S(2)}, u32[]{:S(2)}) collective-permute-start(bf16[512,256]{1,0:T(8,128)(2,1)S(1)} %get-tuple-element.70), channel_id=1, source_target_pairs={{0,2},{2,4},{4,6},{6,0},{1,3},{3,5},{5,7},{7,1},{8,10},{10,12},{12... | collective-permute-start | bytes 786440 | tf_op jit(solution)/shard_map/ppermute | solution.py:41
  140.9 34.0 %collective-permute-start.26 = (bf16[512,256]{1,0:T(8,128)(2,1)S(1)}, bf16[512,256]{1,0:T(8,128)(2,1)S(1)}, u32[]{:S(2)}, u32[]{:S(2)}) collective-permute-start(bf16[512,256]{1,0:T(8,128)(2,1)S(1)} %get-tuple-element.67), channel_id=1, source_target_pairs={{0,6},{2,0},{4,2},{6,4},{1,7},{3,1},{5,3},{7,5},{8,14},{10,8},{12,... | collective-permute-start | bytes 786440 | tf_op jit(solution)/shard_map/ppermute | solution.py:41
  144.8 38.6 %collective-permute-start.25 = (bf16[512,256]{1,0:T(8,128)(2,1)S(1)}, bf16[512,256]{1,0:T(8,128)(2,1)S(1)}, u32[]{:S(2)}, u32[]{:S(2)}) collective-permute-start(bf16[512,256]{1,0:T(8,128)(2,1)S(1)} %get-tuple-element.66), channel_id=1, source_target_pairs={{0,4},{2,6},{4,0},{6,2},{1,5},{3,7},{5,1},{7,3},{8,12},{10,14},{12... | collective-permute-start | bytes 786440 | tf_op jit(solution)/shard_map/ppermute | solution.py:41
  146.5 36.9 %collective-permute-start.24 = (bf16[512,256]{1,0:T(8,128)(2,1)S(1)}, bf16[512,256]{1,0:T(8,128)(2,1)S(1)}, u32[]{:S(2)}, u32[]{:S(2)}) collective-permute-start(bf16[512,256]{1,0:T(8,128)(2,1)S(1)} %get-tuple-element.65), channel_id=1, source_target_pairs={{0,2},{2,4},{4,6},{6,0},{1,3},{3,5},{5,7},{7,1},{8,10},{10,12},{12... | collective-permute-start | bytes 786440 | tf_op jit(solution)/shard_map/ppermute | solution.py:41
  174.4 61.6 %collective-permute-start.73 = (bf16[512,768]{1,0:T(8,128)(2,1)}, bf16[512,768]{1,0:T(8,128)(2,1)}, u32[]{:S(2)}, u32[]{:S(2)}) collective-permute-start(bf16[512,768]{1,0:T(8,128)(2,1)} %convolution_convert_fusion.2), channel_id=1, source_target_pairs={{0,1},{1,0},{2,3},{3,2},{4,5},{5,4},{6,7},{7,6},{8,9},{9,8},{10,11... | collective-permute-start | bytes 2359304 | tf_op jit(solution)/shard_map/ppermute | solution.py:41
  174.4 65.5 %collective-permute-start.80 = (bf16[512,768]{1,0:T(8,128)(2,1)}, bf16[512,768]{1,0:T(8,128)(2,1)}, u32[]{:S(2)}, u32[]{:S(2)}) collective-permute-start(bf16[512,768]{1,0:T(8,128)(2,1)} %convolution_convert_fusion.1), channel_id=1, source_target_pairs={{0,1},{1,0},{2,3},{3,2},{4,5},{5,4},{6,7},{7,6},{8,9},{9,8},{10,11... | collective-permute-start | bytes 2359304 | tf_op jit(solution)/shard_map/ppermute | solution.py:41
  184.6 11.1 %collective-permute-start.30 = (bf16[512,256]{1,0:T(8,128)(2,1)S(1)}, bf16[512,256]{1,0:T(8,128)(2,1)S(1)}, u32[]{:S(2)}, u32[]{:S(2)}) collective-permute-start(bf16[512,256]{1,0:T(8,128)(2,1)S(1)} %get-tuple-element.105.refs_4_), channel_id=1, source_target_pairs={{0,2},{2,4},{4,6},{6,0},{1,3},{3,5},{5,7},{7,1},{8,10},{10,12},{12... | collective-permute-start | bytes 786440 | tf_op jit(solution)/shard_map/ppermute | solution.py:41
  185.2 18.7 %collective-permute-start.31 = (bf16[512,256]{1,0:T(8,128)(2,1)S(1)}, bf16[512,256]{1,0:T(8,128)(2,1)S(1)}, u32[]{:S(2)}, u32[]{:S(2)}) collective-permute-start(bf16[512,256]{1,0:T(8,128)(2,1)S(1)} %get-tuple-element.105.refs_4_), channel_id=1, source_target_pairs={{0,4},{2,6},{4,0},{6,2},{1,5},{3,7},{5,1},{7,3},{8,12},{10,14},{12... | collective-permute-start | bytes 786440 | tf_op jit(solution)/shard_map/ppermute | solution.py:41
  187.2 16.7 %collective-permute-start.32 = (bf16[512,256]{1,0:T(8,128)(2,1)S(1)}, bf16[512,256]{1,0:T(8,128)(2,1)S(1)}, u32[]{:S(2)}, u32[]{:S(2)}) collective-permute-start(bf16[512,256]{1,0:T(8,128)(2,1)S(1)} %get-tuple-element.105.refs_4_), channel_id=1, source_target_pairs={{0,6},{2,0},{4,2},{6,4},{1,7},{3,1},{5,3},{7,5},{8,14},{10,8},{12,... | collective-permute-start | bytes 786440 | tf_op jit(solution)/shard_map/ppermute | solution.py:41
  195.7 54.3 %collective-permute-start.87 = (bf16[768,512]{1,0:T(8,128)(2,1)}, bf16[768,512]{1,0:T(8,128)(2,1)}, u32[]{:S(2)}, u32[]{:S(2)}) collective-permute-start(bf16[768,512]{1,0:T(8,128)(2,1)} %convolution_convert_fusion), channel_id=1, source_target_pairs={{0,1},{1,0},{2,3},{3,2},{4,5},{5,4},{6,7},{7,6},{8,9},{9,8},{10,11... | collective-permute-start | bytes 2359304 | tf_op jit(solution)/shard_map/ppermute | solution.py:41
  227.7 28.4 %collective-permute-start.40 = (f32[8,512]{1,0:T(8,128)S(1)}, f32[8,512]{1,0:T(8,128)S(1)}, u32[]{:S(2)}, u32[]{:S(2)}) collective-permute-start(f32[8,512]{1,0:T(8,128)S(1)} %fusion.21), channel_id=1, source_target_pairs={{0,6},{2,0},{4,2},{6,4},{1,7},{3,1},{5,3},{7,5},{8,14},{10,8},{12,... | collective-permute-start | bytes 49160 | tf_op jit(solution)/shard_map/ppermute | solution.py:41
  236.0 20.6 %collective-permute-start.39 = (f32[8,512]{1,0:T(8,128)S(1)}, f32[8,512]{1,0:T(8,128)S(1)}, u32[]{:S(2)}, u32[]{:S(2)}) collective-permute-start(f32[8,512]{1,0:T(8,128)S(1)} %fusion.21), channel_id=1, source_target_pairs={{0,4},{2,6},{4,0},{6,2},{1,5},{3,7},{5,1},{7,3},{8,12},{10,14},{12... | collective-permute-start | bytes 49160 | tf_op jit(solution)/shard_map/ppermute | solution.py:41
  236.0 21.2 %collective-permute-start.38 = (f32[8,512]{1,0:T(8,128)S(1)}, f32[8,512]{1,0:T(8,128)S(1)}, u32[]{:S(2)}, u32[]{:S(2)}) collective-permute-start(f32[8,512]{1,0:T(8,128)S(1)} %fusion.21), channel_id=1, source_target_pairs={{0,2},{2,4},{4,6},{6,0},{1,3},{3,5},{5,7},{7,1},{8,10},{10,12},{12... | collective-permute-start | bytes 49160 | tf_op jit(solution)/shard_map/ppermute | solution.py:41
  240.0 43.8 %collective-permute-start.37 = (bf16[512,256]{1,0:T(8,128)(2,1)S(1)}, bf16[512,256]{1,0:T(8,128)(2,1)}, u32[]{:S(2)}, u32[]{:S(2)}) collective-permute-start(bf16[512,256]{1,0:T(8,128)(2,1)S(1)} %copy-done.24), channel_id=1, source_target_pairs={{0,6},{2,0},{4,2},{6,4},{1,7},{3,1},{5,3},{7,5},{8,14},{10,8},{12,... | collective-permute-start | bytes 786440 | tf_op jit(solution)/shard_map/ppermute | solution.py:41
  250.0 10.2 %collective-permute-start.76 = (bf16[128,768]{1,0:T(8,128)(2,1)}, bf16[128,768]{1,0:T(8,128)(2,1)}, u32[]{:S(2)}, u32[]{:S(2)}) collective-permute-start(bf16[128,768]{1,0:T(8,128)(2,1)} %get-tuple-element.127), channel_id=1, source_target_pairs={{0,24},{8,16},{16,8},{24,0},{1,25},{9,17},{17,9},{25,1},{2,26},{10... | collective-permute-start | bytes 589832 | tf_op jit(solution)/shard_map/ppermute | solution.py:86
  256.2 8.9 %collective-permute-start.75 = (bf16[128,768]{1,0:T(8,128)(2,1)}, bf16[128,768]{1,0:T(8,128)(2,1)S(1)}, u32[]{:S(2)}, u32[]{:S(2)}) collective-permute-start(bf16[128,768]{1,0:T(8,128)(2,1)} %get-tuple-element.128), channel_id=1, source_target_pairs={{0,16},{8,24},{16,0},{24,8},{1,17},{9,25},{17,1},{25,9},{2,18},{10... | collective-permute-start | bytes 589832 | tf_op jit(solution)/shard_map/ppermute | solution.py:86
  256.7 11.2 %collective-permute-start.74 = (bf16[128,768]{1,0:T(8,128)(2,1)}, bf16[128,768]{1,0:T(8,128)(2,1)S(1)}, u32[]{:S(2)}, u32[]{:S(2)}) collective-permute-start(bf16[128,768]{1,0:T(8,128)(2,1)} %get-tuple-element.126), channel_id=1, source_target_pairs={{0,8},{8,0},{16,24},{24,16},{1,9},{9,1},{17,25},{25,17},{2,10},{10... | collective-permute-start | bytes 589832 | tf_op jit(solution)/shard_map/ppermute | solution.py:86
  257.2 13.6 %collective-permute-start.83 = (bf16[128,768]{1,0:T(8,128)(2,1)}, bf16[128,768]{1,0:T(8,128)(2,1)}, u32[]{:S(2)}, u32[]{:S(2)}) collective-permute-start(bf16[128,768]{1,0:T(8,128)(2,1)} %get-tuple-element.124), channel_id=1, source_target_pairs={{0,24},{8,16},{16,8},{24,0},{1,25},{9,17},{17,9},{25,1},{2,26},{10... | collective-permute-start | bytes 589832 | tf_op jit(solution)/shard_map/ppermute | solution.py:86
  260.2 11.4 %collective-permute-start.82 = (bf16[128,768]{1,0:T(8,128)(2,1)}, bf16[128,768]{1,0:T(8,128)(2,1)S(1)}, u32[]{:S(2)}, u32[]{:S(2)}) collective-permute-start(bf16[128,768]{1,0:T(8,128)(2,1)} %get-tuple-element.125), channel_id=1, source_target_pairs={{0,16},{8,24},{16,0},{24,8},{1,17},{9,25},{17,1},{25,9},{2,18},{10... | collective-permute-start | bytes 589832 | tf_op jit(solution)/shard_map/ppermute | solution.py:86
  265.1 8.1 %collective-permute-start.81 = (bf16[128,768]{1,0:T(8,128)(2,1)}, bf16[128,768]{1,0:T(8,128)(2,1)S(1)}, u32[]{:S(2)}, u32[]{:S(2)}) collective-permute-start(bf16[128,768]{1,0:T(8,128)(2,1)} %get-tuple-element.123), channel_id=1, source_target_pairs={{0,8},{8,0},{16,24},{24,16},{1,9},{9,1},{17,25},{25,17},{2,10},{10... | collective-permute-start | bytes 589832 | tf_op jit(solution)/shard_map/ppermute | solution.py:86
  267.9 8.7 %collective-permute-start.90 = (bf16[192,512]{1,0:T(8,128)(2,1)}, bf16[192,512]{1,0:T(8,128)(2,1)S(1)}, u32[]{:S(2)}, u32[]{:S(2)}) collective-permute-start(bf16[192,512]{1,0:T(8,128)(2,1)} %get-tuple-element.121), channel_id=1, source_target_pairs={{0,24},{8,16},{16,8},{24,0},{1,25},{9,17},{17,9},{25,1},{2,26},{10... | collective-permute-start | bytes 589832 | tf_op jit(solution)/shard_map/ppermute | solution.py:86
  270.8 15.6 %collective-permute-start.36 = (bf16[512,256]{1,0:T(8,128)(2,1)S(1)}, bf16[512,256]{1,0:T(8,128)(2,1)S(1)}, u32[]{:S(2)}, u32[]{:S(2)}) collective-permute-start(bf16[512,256]{1,0:T(8,128)(2,1)S(1)} %copy-done.22), channel_id=1, source_target_pairs={{0,4},{2,6},{4,0},{6,2},{1,5},{3,7},{5,1},{7,3},{8,12},{10,14},{12... | collective-permute-start | bytes 786440 | tf_op jit(solution)/shard_map/ppermute | solution.py:41
  271.6 14.9 %collective-permute-start.35 = (bf16[512,256]{1,0:T(8,128)(2,1)S(1)}, bf16[512,256]{1,0:T(8,128)(2,1)S(1)}, u32[]{:S(2)}, u32[]{:S(2)}) collective-permute-start(bf16[512,256]{1,0:T(8,128)(2,1)S(1)} %copy-done.20), channel_id=1, source_target_pairs={{0,2},{2,4},{4,6},{6,0},{1,3},{3,5},{5,7},{7,1},{8,10},{10,12},{12... | collective-permute-start | bytes 786440 | tf_op jit(solution)/shard_map/ppermute | solution.py:41
  273.1 6.6 %collective-permute-start.89 = (bf16[192,512]{1,0:T(8,128)(2,1)S(1)}, bf16[192,512]{1,0:T(8,128)(2,1)S(1)}, u32[]{:S(2)}, u32[]{:S(2)}) collective-permute-start(bf16[192,512]{1,0:T(8,128)(2,1)S(1)} %copy-done.53), channel_id=1, source_target_pairs={{0,16},{8,24},{16,0},{24,8},{1,17},{9,25},{17,1},{25,9},{2,18},{10... | collective-permute-start | bytes 589832 | tf_op jit(solution)/shard_map/ppermute | solution.py:86
  279.7 12.1 %collective-permute-start.45 = (bf16[512,512]{1,0:T(8,128)(2,1)S(1)}, bf16[512,512]{1,0:T(8,128)(2,1)S(1)}, u32[]{:S(2)}, u32[]{:S(2)}) collective-permute-start(bf16[512,512]{1,0:T(8,128)(2,1)S(1)} %copy-done.61), channel_id=1, source_target_pairs={{0,1},{1,0},{2,3},{3,2},{4,5},{5,4},{6,7},{7,6},{8,9},{9,8},{10,11... | collective-permute-start | bytes 1572872 | tf_op jit(solution)/shard_map/ppermute | solution.py:41
  282.3 10.5 %collective-permute-start.66 = (bf16[512,512]{1,0:T(8,128)(2,1)S(1)}, bf16[512,512]{1,0:T(8,128)(2,1)S(1)}, u32[]{:S(2)}, u32[]{:S(2)}) collective-permute-start(bf16[512,512]{1,0:T(8,128)(2,1)S(1)} %copy-done.60), channel_id=1, source_target_pairs={{0,1},{1,0},{2,3},{3,2},{4,5},{5,4},{6,7},{7,6},{8,9},{9,8},{10,11... | collective-permute-start | bytes 1572872 | tf_op jit(solution)/shard_map/ppermute | solution.py:41
  283.8 6.8 %collective-permute-start.52 = (bf16[512,256]{1,0:T(8,128)(2,1)S(1)}, bf16[512,256]{1,0:T(8,128)(2,1)S(1)}, u32[]{:S(2)}, u32[]{:S(2)}) collective-permute-start(bf16[512,256]{1,0:T(8,128)(2,1)S(1)} %copy-done.63), channel_id=1, source_target_pairs={{0,1},{1,0},{2,3},{3,2},{4,5},{5,4},{6,7},{7,6},{8,9},{9,8},{10,11... | collective-permute-start | bytes 786440 | tf_op jit(solution)/shard_map/ppermute | solution.py:41
  286.5 67.8 %collective-permute-start.77 = (bf16[128,768]{1,0:T(8,128)(2,1)S(1)}, bf16[128,768]{1,0:T(8,128)(2,1)S(1)}, u32[]{:S(2)}, u32[]{:S(2)}) collective-permute-start(bf16[128,768]{1,0:T(8,128)(2,1)S(1)} %get-tuple-element.112), channel_id=1, source_target_pairs={{0,8},{8,0},{16,24},{24,16},{1,9},{9,1},{17,25},{25,17},{2,10},{10... | collective-permute-start | bytes 589832 | tf_op jit(solution)/shard_map/ppermute | solution.py:86
  290.6 65.1 %collective-permute-start.78 = (bf16[128,768]{1,0:T(8,128)(2,1)S(1)}, bf16[128,768]{1,0:T(8,128)(2,1)S(1)}, u32[]{:S(2)}, u32[]{:S(2)}) collective-permute-start(bf16[128,768]{1,0:T(8,128)(2,1)S(1)} %get-tuple-element.112), channel_id=1, source_target_pairs={{0,16},{8,24},{16,0},{24,8},{1,17},{9,25},{17,1},{25,9},{2,18},{10... | collective-permute-start | bytes 589832 | tf_op jit(solution)/shard_map/ppermute | solution.py:86
  308.1 33.0 %collective-permute-start.48 = (bf16[128,512]{1,0:T(8,128)(2,1)S(1)}, bf16[128,512]{1,0:T(8,128)(2,1)S(1)}, u32[]{:S(2)}, u32[]{:S(2)}) collective-permute-start(bf16[128,512]{1,0:T(8,128)(2,1)S(1)} %get-tuple-element.137), channel_id=1, source_target_pairs={{0,24},{8,16},{16,8},{24,0},{1,25},{9,17},{17,9},{25,1},{2,26},{10... | collective-permute-start | bytes 393224 | tf_op jit(solution)/shard_map/ppermute | solution.py:86
  310.3 32.3 %collective-permute-start.47 = (bf16[128,512]{1,0:T(8,128)(2,1)S(1)}, bf16[128,512]{1,0:T(8,128)(2,1)S(1)}, u32[]{:S(2)}, u32[]{:S(2)}) collective-permute-start(bf16[128,512]{1,0:T(8,128)(2,1)S(1)} %get-tuple-element.138), channel_id=1, source_target_pairs={{0,16},{8,24},{16,0},{24,8},{1,17},{9,25},{17,1},{25,9},{2,18},{10... | collective-permute-start | bytes 393224 | tf_op jit(solution)/shard_map/ppermute | solution.py:86
  341.1 8.7 %collective-permute-start.69 = (bf16[128,512]{1,0:T(8,128)(2,1)S(1)}, bf16[128,512]{1,0:T(8,128)(2,1)S(1)}, u32[]{:S(2)}, u32[]{:S(2)}) collective-permute-start(bf16[128,512]{1,0:T(8,128)(2,1)S(1)} %get-tuple-element.134), channel_id=1, source_target_pairs={{0,24},{8,16},{16,8},{24,0},{1,25},{9,17},{17,9},{25,1},{2,26},{10... | collective-permute-start | bytes 393224 | tf_op jit(solution)/shard_map/ppermute | solution.py:86
  342.6 9.3 %collective-permute-start.68 = (bf16[128,512]{1,0:T(8,128)(2,1)S(1)}, bf16[128,512]{1,0:T(8,128)(2,1)S(1)}, u32[]{:S(2)}, u32[]{:S(2)}) collective-permute-start(bf16[128,512]{1,0:T(8,128)(2,1)S(1)} %get-tuple-element.135), channel_id=1, source_target_pairs={{0,16},{8,24},{16,0},{24,8},{1,17},{9,25},{17,1},{25,9},{2,18},{10... | collective-permute-start | bytes 393224 | tf_op jit(solution)/shard_map/ppermute | solution.py:86
  349.8 8.8 %collective-permute-start.79 = (bf16[128,768]{1,0:T(8,128)(2,1)S(1)}, bf16[128,768]{1,0:T(8,128)(2,1)S(1)}, u32[]{:S(2)}, u32[]{:S(2)}) collective-permute-start(bf16[128,768]{1,0:T(8,128)(2,1)S(1)} %get-tuple-element.112), channel_id=1, source_target_pairs={{0,24},{8,16},{16,8},{24,0},{1,25},{9,17},{17,9},{25,1},{2,26},{10... | collective-permute-start | bytes 589832 | tf_op jit(solution)/shard_map/ppermute | solution.py:86
  351.9 10.5 %collective-permute-start.84 = (bf16[128,768]{1,0:T(8,128)(2,1)S(1)}, bf16[128,768]{1,0:T(8,128)(2,1)S(1)}, u32[]{:S(2)}, u32[]{:S(2)}) collective-permute-start(bf16[128,768]{1,0:T(8,128)(2,1)S(1)} %get-tuple-element.110), channel_id=1, source_target_pairs={{0,8},{8,0},{16,24},{24,16},{1,9},{9,1},{17,25},{25,17},{2,10},{10... | collective-permute-start | bytes 589832 | tf_op jit(solution)/shard_map/ppermute | solution.py:86
  353.0 11.2 %collective-permute-start.85 = (bf16[128,768]{1,0:T(8,128)(2,1)S(1)}, bf16[128,768]{1,0:T(8,128)(2,1)S(1)}, u32[]{:S(2)}, u32[]{:S(2)}) collective-permute-start(bf16[128,768]{1,0:T(8,128)(2,1)S(1)} %get-tuple-element.110), channel_id=1, source_target_pairs={{0,16},{8,24},{16,0},{24,8},{1,17},{9,25},{17,1},{25,9},{2,18},{10... | collective-permute-start | bytes 589832 | tf_op jit(solution)/shard_map/ppermute | solution.py:86
  354.2 12.8 %collective-permute-start.86 = (bf16[128,768]{1,0:T(8,128)(2,1)S(1)}, bf16[128,768]{1,0:T(8,128)(2,1)S(1)}, u32[]{:S(2)}, u32[]{:S(2)}) collective-permute-start(bf16[128,768]{1,0:T(8,128)(2,1)S(1)} %get-tuple-element.110), channel_id=1, source_target_pairs={{0,24},{8,16},{16,8},{24,0},{1,25},{9,17},{17,9},{25,1},{2,26},{10... | collective-permute-start | bytes 589832 | tf_op jit(solution)/shard_map/ppermute | solution.py:86
  355.7 13.0 %collective-permute-start.91 = (bf16[192,512]{1,0:T(8,128)(2,1)S(1)}, bf16[192,512]{1,0:T(8,128)(2,1)S(1)}, u32[]{:S(2)}, u32[]{:S(2)}) collective-permute-start(bf16[192,512]{1,0:T(8,128)(2,1)S(1)} %get-tuple-element.108), channel_id=1, source_target_pairs={{0,8},{8,0},{16,24},{24,16},{1,9},{9,1},{17,25},{25,17},{2,10},{10... | collective-permute-start | bytes 589832 | tf_op jit(solution)/shard_map/ppermute | solution.py:86
  358.6 11.4 %collective-permute-start.92 = (bf16[192,512]{1,0:T(8,128)(2,1)S(1)}, bf16[192,512]{1,0:T(8,128)(2,1)S(1)}, u32[]{:S(2)}, u32[]{:S(2)}) collective-permute-start(bf16[192,512]{1,0:T(8,128)(2,1)S(1)} %get-tuple-element.108), channel_id=1, source_target_pairs={{0,16},{8,24},{16,0},{24,8},{1,17},{9,25},{17,1},{25,9},{2,18},{10... | collective-permute-start | bytes 589832 | tf_op jit(solution)/shard_map/ppermute | solution.py:86
  362.4 9.0 %collective-permute-start.93 = (bf16[192,512]{1,0:T(8,128)(2,1)S(1)}, bf16[192,512]{1,0:T(8,128)(2,1)S(1)}, u32[]{:S(2)}, u32[]{:S(2)}) collective-permute-start(bf16[192,512]{1,0:T(8,128)(2,1)S(1)} %get-tuple-element.108), channel_id=1, source_target_pairs={{0,24},{8,16},{16,8},{24,0},{1,25},{9,17},{17,9},{25,1},{2,26},{10... | collective-permute-start | bytes 589832 | tf_op jit(solution)/shard_map/ppermute | solution.py:86
  364.3 8.2 %collective-permute-start.49 = (bf16[128,512]{1,0:T(8,128)(2,1)S(1)}, bf16[128,512]{1,0:T(8,128)(2,1)S(1)}, u32[]{:S(2)}, u32[]{:S(2)}) collective-permute-start(bf16[128,512]{1,0:T(8,128)(2,1)S(1)} %get-tuple-element.118), channel_id=1, source_target_pairs={{0,8},{8,0},{16,24},{24,16},{1,9},{9,1},{17,25},{25,17},{2,10},{10... | collective-permute-start | bytes 393224 | tf_op jit(solution)/shard_map/ppermute | solution.py:86
  367.1 6.7 %collective-permute-start.50 = (bf16[128,512]{1,0:T(8,128)(2,1)S(1)}, bf16[128,512]{1,0:T(8,128)(2,1)S(1)}, u32[]{:S(2)}, u32[]{:S(2)}) collective-permute-start(bf16[128,512]{1,0:T(8,128)(2,1)S(1)} %get-tuple-element.118), channel_id=1, source_target_pairs={{0,16},{8,24},{16,0},{24,8},{1,17},{9,25},{17,1},{25,9},{2,18},{10... | collective-permute-start | bytes 393224 | tf_op jit(solution)/shard_map/ppermute | solution.py:86
  (98 other events, 758.8 us)

commit v2 on v1

v2 whole, which is shorter than its diff:
```python
import functools

import jax
import jax.numpy as jnp
from jax import lax
from jax.experimental import pallas as pl
from jax.experimental.pallas import tpu as pltpu
from jax.sharding import PartitionSpec as P

EPS = 1e-06
THETA = 1000000.0
NEGATIVE = -1e30
BF = jnp.bfloat16
F32 = jnp.float32
VMEM = pl.BlockSpec(memory_space=pltpu.VMEM)
SMEM = pl.BlockSpec(memory_space=pltpu.SMEM)
ANY = pl.BlockSpec(memory_space=pl.ANY)


def dot(left, right):
    return lax.dot_general(left, right, (((1,), (0,)), ((), ())), preferred_element_type=F32)


def dot_cols(left, right):
    return lax.dot_general(left, right, (((1,), (1,)), ((), ())), preferred_element_type=F32)


def dot_rows(left, right):
    return lax.dot_general(left, right, (((0,), (0,)), ((), ())), preferred_element_type=F32)


def span(offset, size):
    return pl.ds(pl.multiple_of(offset, size), size)


def turn(vectors):
    return pltpu.roll(vectors, vectors.shape[-1] // 2, 1)


def shifted(block, axis, shift):
    size = lax.axis_size(axis)
    return lax.ppermute(block, axis, [(i, (i + shift) % size) for i in range(size)])


def pieces_of(block):
    return [block] + [shifted(block, "gx", s) for s in range(1, lax.axis_size("gx"))]


def piece_sum(own, others):
    total = own
    for s, part in enumerate(others, 1):
        total = total + shifted(part, "gx", s).astype(F32)
    return total


def gather_width(block, axis):
    if lax.axis_size("gy") == 2:
        return [block, shifted(block, "gy", 1)]
    return [lax.all_gather(block, "gy", axis=axis, tiled=True)]


def dev_partner(m):
    count, here = lax.axis_size("dev"), lax.axis_index("dev")
    return here ^ m if count & (count - 1) == 0 else (here + m) % count


def dev_giver(m):
    count, here = lax.axis_size("dev"), lax.axis_index("dev")
    return here ^ m if count & (count - 1) == 0 else (here - m) % count


def dev_send(block, m):
    count = lax.axis_size("dev")
    even = count & (count - 1) == 0
    return lax.ppermute(
        block, "dev", [(i, i ^ m if even else (i + m) % count) for i in range(count)]
    )


def nothing(*refs):
    pass


def after(arrays, *deps):
    if not deps or not arrays:
        return arrays
    return pl.pallas_call(
        nothing,
        in_specs=[ANY] * (len(arrays) + len(deps)),
        out_specs=[ANY] * len(arrays),
        out_shape=[jax.ShapeDtypeStruct(a.shape, a.dtype) for a in arrays],
        input_output_aliases={i: i for i in range(len(arrays))},
    )(*arrays, *deps)


def small_sum(block, axis):
    total = block
    for s in range(1, lax.axis_size(axis)):
        total = total + shifted(block, axis, s)
    return total


def pick(refs, offset, size, axis):
    half = refs[0].shape[axis]

    def cut(ref):
        at = span(offset % half, size)
        return ref[at, :] if axis == 0 else ref[:, at]

    if len(refs) == 1:
        return cut(refs[0])
    return jnp.where(offset < half, cut(refs[0]), cut(refs[1]))


def wide_dot(left_ref, refs, product, axis):
    step = left_ref.shape[1] // len(refs)
    return sum(
        product(left_ref[:, i * step : (i + 1) * step], ref[...]) for i, ref in enumerate(refs)
    )


def normalise(pieces, gains, row, offset_ref, normed_ref, scale_ref):
    count, width = len(pieces), pieces[0].shape[1]
    blocks = [p[...].astype(F32) for p in pieces]
    square = sum(jnp.sum(b * b, axis=1, keepdims=True) for b in blocks)
    scale = lax.rsqrt(square / (width * count) + EPS)
    scale_ref[...] = scale
    for s in range(count):
        gain = gains[s][row : row + 1, :].astype(F32)
        normed_ref[:, span(offset_ref[s], width)] = (blocks[s] * scale * gain).astype(BF)


def cot_kernel(count, offset_ref, *refs):
    pieces, normed_ref, downs = refs[:count], refs[count], refs[count + 1 : -3]
    whole_ref, grad_ref, turned_ref = refs[-3:]
    turned_ref[...] = jnp.transpose(normed_ref[...])
    width = pieces[0].shape[1]
    for s in range(count):
        whole_ref[:, span(offset_ref[s], width)] = pieces[s][...]
    grad_ref[...] = wide_dot(whole_ref, downs, dot_cols, 1)


def qkv_kernel(count, parts, head, offset_ref, *refs):
    pieces, gains, refs = refs[:count], refs[count : 2 * count], refs[2 * count :]
    wq, wk, wv = refs[:parts], refs[parts : 2 * parts], refs[2 * parts : 3 * parts]
    qg_ref, kg_ref, cos_ref, sin_ref = refs[3 * parts : 3 * parts + 4]
    normed_ref, scale_ref, ql_ref, kl_ref, q_ref, k_ref, v_ref = refs[-7:]
    normalise(pieces, gains, 0, offset_ref, normed_ref, scale_ref)
    ql_ref[...] = wide_dot(normed_ref, wq, dot, 0)
    kl_ref[...] = wide_dot(normed_ref, wk, dot, 0)
    v_ref[...] = wide_dot(normed_ref, wv, dot, 0).astype(BF)
    cosine, sine = cos_ref[...], sin_ref[...]
    for lin_ref, gain, out_ref in ((ql_ref, qg_ref, q_ref), (kl_ref, kg_ref, k_ref)):
        for h in range(lin_ref.shape[1] // head):
            cut = slice(h * head, (h + 1) * head)
            u = lin_ref[:, cut]
            u = u * lax.rsqrt(jnp.mean(u * u, axis=1, keepdims=True) + EPS) * gain[...]
            out_ref[:, cut] = (u * cosine + turn(u) * sine).astype(BF)


def visible_bias(seq_col, pos_col, seq_row, pos_row):
    seen = (seq_col == seq_row) & (pos_col <= pos_row)
    return jnp.where(seen, 0.0, NEGATIVE)


def peer_block(refs, p, extent, cut):
    return refs[p][:extent, cut] if len(refs) > 1 else refs[0][p, :extent, cut]


def columns_of(col_ref, peers):
    if peers > 2:
        return lambda p, extent: (col_ref[p, :extent, 0:1], col_ref[p, :extent, 1:2])
    turned = jnp.transpose(col_ref[...])
    return lambda p, extent: (
        turned[:extent, 2 * p : 2 * p + 1],
        turned[:extent, 2 * p + 1 : 2 * p + 2],
    )


def attend_kernel(head, tile, peers, q_ref, row_ref, col_ref, *refs):
    each = peers if peers <= 2 else 1
    keys, values = refs[:each], refs[each : 2 * each]
    mixed_ref, att_ref, log_ref = refs[-3:]
    column = columns_of(col_ref, peers)
    rows = q_ref.shape[0]
    kv_heads = keys[0].shape[-1] // head
    ratio = q_ref.shape[1] // head // kv_heads
    factor = head ** (-0.5)
    for t in range(rows // tile):
        part = slice(t * tile, (t + 1) * tile)
        extent = (t + 1) * tile
        seq_row, pos_row = row_ref[0:1, part], row_ref[1:2, part]

        def bias_of(p):
            one = visible_bias(*column(p, extent), seq_row, pos_row)
            return jnp.concatenate([one] * ratio, axis=1)

        biases = [bias_of(p) for p in range(peers)] if peers <= 2 else None
        for j in range(kv_heads):
            cut = slice(j * head, (j + 1) * head)
            queries = jnp.concatenate(
                [
                    q_ref[part, (j * ratio + i) * head : (j * ratio + i + 1) * head]
                    for i in range(ratio)
                ],
                axis=0,
            )

            def step(p, carry, bias=None):
                high, total, accum = carry
                if bias is None:
                    bias = bias_of(p)
                scores = dot_cols(peer_block(keys, p, extent, cut), queries) * factor + bias
                newest = jnp.maximum(high, jnp.max(scores, axis=0, keepdims=True))
                weights = jnp.exp(scores - newest)
                shrink = jnp.exp(high - newest)
                total = total * shrink + jnp.sum(weights, axis=0, keepdims=True)
                accum = accum * shrink + dot_rows(
                    peer_block(values, p, extent, cut), weights.astype(BF)
                )
                return newest, total, accum

            carry = (
                jnp.full((1, ratio * tile), NEGATIVE, F32),
                jnp.zeros((1, ratio * tile), F32),
                jnp.zeros((head, ratio * tile), F32),
            )
            if peers <= 2:
                for p in range(peers):
                    carry = step(p, carry, biases[p])
            else:
                carry = lax.fori_loop(0, peers, step, carry)
            high, total, accum = carry
            attended = accum / total
            logs = high + jnp.log(total)
            back = jnp.transpose(attended)
            for i in range(ratio):
                h = j * ratio + i
                lane = slice(i * tile, (i + 1) * tile)
                att_ref[h * head : (h + 1) * head, part] = attended[:, lane]
                log_ref[h : h + 1, part] = logs[:, lane]
                mixed_ref[part, h * head : (h + 1) * head] = back[lane, :].astype(BF)


def ffn_kernel(count, parts_in, offset_ref, *refs):
    pieces, gains, refs = refs[:count], refs[count : 2 * count], refs[2 * count :]
    wg, wu, grad_ref = refs[:parts_in], refs[parts_in : 2 * parts_in], refs[2 * parts_in]
    outs = refs[-count - 5 :]
    parts, (normed_ref, scale_ref, product_ref, gate_ref, up_ref) = outs[:count], outs[count:]
    width = pieces[0].shape[1]
    normalise(pieces, gains, 1, offset_ref, normed_ref, scale_ref)
    gate = wide_dot(normed_ref, wg, dot, 0)
    up = wide_dot(normed_ref, wu, dot, 0)
    sig = 1.0 / (1.0 + jnp.exp(-gate))
    silu = gate * sig
    product_ref[...] = (silu * up).astype(BF)
    grad = grad_ref[...]
    gate_ref[...] = (grad * up * (sig + silu * (1.0 - sig))).astype(BF)
    up_ref[...] = (grad * silu).astype(BF)
    for s in range(count):
        at = offset_ref[count + s]
        parts[s][...] = (
            dot_cols(gate_ref[...], pick(wg, at, width, 0))
            + dot_cols(up_ref[...], pick(wu, at, width, 0))
        ).astype(parts[s].dtype)


def split_dot_kernel(count, parts_in, offset_ref, left_ref, *refs):
    weights, parts = refs[:parts_in], refs[-count:]
    width = parts[0].shape[1]
    for s in range(count):
        weight = pick(weights, offset_ref[count + s], width, 1)
        parts[s][...] = dot(left_ref[...], weight).astype(parts[s].dtype)


def weight_grad_kernel(turned, *refs):
    own_ref, other_ref = refs[-2:]
    size = own_ref.shape[1]
    start = 0
    for i, across in enumerate(turned):
        own, other, right = refs[3 * i : 3 * i + 3]
        width = right.shape[1]
        both = jnp.concatenate([own[...], other[...]], axis=0 if across else 1)
        both = (dot if across else dot_rows)(both, right[...])
        own_ref[0, :, start : start + width] = both[:size].astype(BF)
        other_ref[0, :, start : start + width] = both[size:].astype(BF)
        start += width


def final_kernel(count, *refs):
    parts = refs[:count]
    (tok_ref, cot_ref, hid_ref, two_ref, one_scale, two_scale, two_inner, gain_ref) = refs[
        count : count + 8
    ]
    grad_ref, part_ref = refs[-2:]
    rows, width = tok_ref.shape
    size = width * count
    gain_one, gain_two = gain_ref[0:1, :].astype(F32), gain_ref[1:2, :].astype(F32)
    sums = [jnp.zeros((1, width), F32)] * 2
    small = sum(p[rows : rows + 16, :].astype(F32) for p in parts)
    count_rows = rows // width
    for i in range(count_rows):
        at = slice(i * width, (i + 1) * width)
        one = sum(p[at, :].astype(F32) for p in parts)
        inputs, hidden, two = tok_ref[at, :].astype(F32), hid_ref[at, :], two_ref[at, :]
        scale, later = one_scale[at, :], two_scale[at, :]
        inner = small[i : i + 1, :] + small[count_rows + i : count_rows + i + 1, :]
        inner = jnp.transpose(jnp.broadcast_to(inner, (128, width)))[:, 0:1]
        grad_ref[at, :] = (
            cot_ref[at, :].astype(F32)
            + later * (two * gain_two)
            - hidden * (later * later * later * (two_inner[at, :] / size))
            + scale * (one * gain_one)
            - inputs * (scale * scale * (inner / size))
        )
        sums[0] = sums[0] + jnp.sum(one * inputs * scale, axis=0, keepdims=True)
        sums[1] = sums[1] + jnp.sum(two * hidden * later, axis=0, keepdims=True)
    last = 2 * count_rows
    part_ref[...] = jnp.concatenate(
        sums
        + [small[last : last + 1, :] + small[last + 1 : last + 2, :], jnp.zeros((5, width), F32)],
        axis=0,
    )


def share_sum_kernel(shares, chunk_ref, *refs):
    owns, gots = refs[:shares], refs[shares : 2 * shares]
    blocks = owns[0].shape[0]
    for m, ref in enumerate(refs[-blocks:]):
        c = chunk_ref[m]
        start = 0
        for own, got in zip(owns, gots):
            stop = start + own.shape[2]
            ref[:, start:stop] = (own[c].astype(F32) + got[c].astype(F32)).astype(ref.dtype)
            start = stop


def result_share_kernel(count, parts_in, offset_ref, left_ref, *refs):
    weights, (own_ref, got_ref) = refs[:parts_in], refs[parts_in : parts_in + 2]
    split_dot_kernel(count, parts_in, offset_ref, left_ref, *weights, *refs[-count - 1 : -1])
    refs[-1][...] = (own_ref[0].astype(F32) + got_ref[0].astype(F32)).astype(BF)


def widen_kernel(pieces, whole_ref, *refs):
    for (start, width, turned), ref in zip(pieces, refs[-len(pieces) :]):
        value = whole_ref[:, start : start + width].astype(F32)
        ref[...] = jnp.transpose(value) if turned else value


def assemble_kernel(count, pieces, owner_ref, *refs):
    parts, outs = refs[:count], refs[-len(pieces) - 1 : -1]
    held = refs[-1]
    size = parts[0].shape[0]
    for (start, width, turned), ref in zip(pieces, outs):
        for m, part in enumerate(parts):
            at = pl.ds(pl.multiple_of(owner_ref[m] * size, size), size)
            value = part[:, start : start + width].astype(F32)
            if turned:
                held[at, :width] = value
            else:
                ref[at, :] = value
        if turned:
            ref[...] = jnp.transpose(held[:, :width])


def unrotate(grad, lin, gain, cosine, sine):
    size = lin.shape[1]
    inner = grad * cosine + turn(grad * sine)
    inverse = lax.rsqrt(jnp.mean(lin * lin, axis=1, keepdims=True) + EPS)
    unit = lin * inverse
    part = jnp.sum(inner * unit, axis=0, keepdims=True)
    inner = inner * gain
    mean = jnp.sum(inner * unit, axis=1, keepdims=True) / size
    return inverse * (inner - unit * mean), part


def branch_kernel(count, parts_in, offset_ref, *refs):
    hidden, grads, gains = refs[:count], refs[count : 2 * count], refs[2 * count : 3 * count]
    scale_ref, cot_ref = refs[3 * count : 3 * count + 2]
    weights = refs[3 * count + 2 : 3 * count + 2 + parts_in]
    branch_ref, mixed_ref, inner_ref = refs[-3:]
    width = hidden[0].shape[1]
    scale = scale_ref[...]
    blocks = [(h[...].astype(F32), g[...].astype(F32)) for h, g in zip(hidden, grads)]
    scaled = [g * gain[1:2, :].astype(F32) for gain, (_, g) in zip(gains, blocks)]
    inner = sum(jnp.sum(h * g, axis=1, keepdims=True) for (h, _), g in zip(blocks, scaled))
    inner_ref[...] = inner
    lessen = scale * scale * scale * (inner / (width * count))
    for s in range(count):
        at = span(offset_ref[s], width)
        branch_ref[:, at] = (
            cot_ref[:, at].astype(F32) + scale * scaled[s] - blocks[s][0] * lessen
        ).astype(BF)
    mixed_ref[...] = wide_dot(branch_ref, weights, dot_cols, 1).astype(BF)


def attend_back_kernel(head, tile, peers, *refs):
    each = peers if peers <= 2 else 1
    grad_ref, q_ref, ql_ref, row_ref, col_ref, att_ref, log_ref, qg_ref, cos_ref, sin_ref = refs[:10]
    all_keys, all_values = refs[10 : 10 + each], refs[10 + each : 10 + 2 * each]
    dql_ref, qpart_ref = refs[-4 - 2 * each : -2 - 2 * each]
    dk_refs, dv_refs = refs[-2 - 2 * each : -2 - each], refs[-2 - each : -2]
    dk_sum, dv_sum = refs[-2:]
    column = columns_of(col_ref, peers)
    rows = q_ref.shape[0]
    kv_heads = all_keys[0].shape[-1] // head
    ratio = q_ref.shape[1] // head // kv_heads
    factor = head ** (-0.5)
    dk_sum[...] = jnp.zeros_like(dk_sum)
    dv_sum[...] = jnp.zeros_like(dv_sum)
    gain_part = jnp.zeros((1, head), F32)
    for t in range(rows // tile):
        part = slice(t * tile, (t + 1) * tile)
        extent = (t + 1) * tile
        grad_mixed = grad_ref[part, :]
        grad_back = jnp.transpose(grad_mixed.astype(F32))
        seq_row, pos_row = row_ref[0:1, part], row_ref[1:2, part]

        def bias_of(p):
            one = visible_bias(*column(p, extent), seq_row, pos_row)
            return jnp.concatenate([one] * ratio, axis=1)

        biases = [bias_of(p) for p in range(peers)] if peers <= 2 else None
        for j in range(kv_heads):
            cut = slice(j * head, (j + 1) * head)
            heads = [j * ratio + i for i in range(ratio)]
            lanes = [slice(h * head, (h + 1) * head) for h in heads]
            queries = jnp.concatenate([q_ref[part, lane] for lane in lanes], axis=0)
            grad_heads = jnp.concatenate([grad_mixed[:, lane] for lane in lanes], axis=0)
            logs = jnp.concatenate([log_ref[h : h + 1, part] for h in heads], axis=1)
            delta = jnp.concatenate(
                [
                    jnp.sum(grad_back[lane, :] * att_ref[lane, part], axis=0, keepdims=True)
                    for lane in lanes
                ],
                axis=1,
            )

            def step(p, accum, bias=None):
                if bias is None:
                    bias = bias_of(p)
                keys = peer_block(all_keys, p, extent, cut)
                values = peer_block(all_values, p, extent, cut)
                probs = jnp.exp(dot_cols(keys, queries) * factor + bias - logs)
                grad_probs = dot_cols(values, grad_heads)
                grad_scores = (probs * (grad_probs - delta)).astype(BF)
                dv_sum[p, :extent, cut] += dot(probs.astype(BF), grad_heads)
                dk_sum[p, :extent, cut] += dot(grad_scores, queries)
                return accum + dot_rows(keys, grad_scores)

            accum = jnp.zeros((head, ratio * tile), F32)
            if peers <= 2:
                for p in range(peers):
                    accum = step(p, accum, biases[p])
            else:
                accum = lax.fori_loop(0, peers, step, accum)
            grad_query = jnp.transpose(accum) * factor
            for i, lane in enumerate(lanes):
                lin, one = unrotate(
                    grad_query[i * tile : (i + 1) * tile, :],
                    ql_ref[part, lane],
                    qg_ref[...],
                    cos_ref[part, :],
                    sin_ref[part, :],
                )
                dql_ref[part, lane] = lin.astype(BF)
                gain_part = gain_part + one
    qpart_ref[...] = gain_part
    for p in range(each):
        at = p if each > 1 or peers == 1 else slice(None)
        dk_refs[p][...] = (dk_sum[at] * factor).astype(BF)
        dv_refs[p][...] = dv_sum[at].astype(BF)


def lin_back_kernel(count, parts_in, head, terms, fused, offset_ref, *refs):
    dql_ref, ql_ref, kl_ref, v_ref, qpart_ref = refs[:5]
    dks, dvs = refs[5 : 5 + terms], refs[5 + terms : 5 + 2 * terms]
    kg_ref, cos_ref, sin_ref = refs[5 + 2 * terms : 8 + 2 * terms]
    weights = refs[8 + 2 * terms : 8 + 2 * terms + 3 * parts_in]
    wq, wk, wv = weights[:parts_in], weights[parts_in : 2 * parts_in], weights[2 * parts_in :]
    turned_ref = refs[8 + 2 * terms + 3 * parts_in] if fused else None
    outs = refs[-count - 2 :]
    parts, (dkl_ref, dvl_ref) = outs[:count], outs[count:]
    shares = refs[-count - 4 : -count - 2]
    rows, width = ql_ref.shape[0], parts[0].shape[1]
    gain_part = jnp.zeros((1, head), F32)
    inners = []
    for i in range(rows // width):
        at = slice(i * width, (i + 1) * width)
        grad_keys = sum(r[at, :].astype(F32) for r in dks)
        dvl_ref[at, :] = sum(r[at, :].astype(F32) for r in dvs).astype(BF)
        for h in range(kl_ref.shape[1] // head):
            cut = slice(h * head, (h + 1) * head)
            lin, one = unrotate(
                grad_keys[:, cut], kl_ref[at, cut], kg_ref[...], cos_ref[at, :], sin_ref[at, :]
            )
            dkl_ref[at, cut] = lin.astype(BF)
            gain_part = gain_part + one
        grad_q, grad_k, grad_v = dql_ref[at, :], dkl_ref[at, :], dvl_ref[at, :]
        inner = (
            jnp.sum(grad_q.astype(F32) * ql_ref[at, :], axis=1, keepdims=True)
            + jnp.sum(grad_k.astype(F32) * kl_ref[at, :], axis=1, keepdims=True)
            + jnp.sum(grad_v.astype(F32) * v_ref[at, :].astype(F32), axis=1, keepdims=True)
        )
        inners.append(jnp.transpose(jnp.broadcast_to(inner, (width, 128)))[0:1, :])
        for s in range(count):
            block = offset_ref[count + s]
            term = (
                dot_cols(grad_q, pick(wq, block, width, 0))
                + dot_cols(grad_k, pick(wk, block, width, 0))
                + dot_cols(grad_v, pick(wv, block, width, 0))
            )
            parts[s][at, :] = term.astype(parts[s].dtype)
    if fused:
        blocks, size, _ = shares[0].shape
        for c in range(blocks):
            at = slice(c * 2 * size, (c + 1) * 2 * size)
            start = 0
            for ref in (dql_ref, dkl_ref, dvl_ref):
                stop = start + ref.shape[1]
                both = dot(turned_ref[at, :], ref[...]).astype(BF)
                for k in range(2):
                    block = 2 * c + k
                    shares[block // blocks][block % blocks, :, start:stop] = both[
                        k * size : (k + 1) * size
                    ]
                start = stop
    inners.append(jnp.concatenate([qpart_ref[...], gain_part], axis=1))
    high = [v.astype(BF).astype(F32) for v in inners]
    low = [v - h for v, h in zip(inners, high)]
    lines = high[:-1] + low[:-1] + [high[-1], low[-1]]
    lines.append(jnp.zeros((16 - len(lines), width), F32))
    below = jnp.concatenate(lines, axis=0)
    for ref in parts:
        ref[rows : rows + 16, :] = below.astype(ref.dtype)


def out(shape, dtype):
    return jax.ShapeDtypeStruct(shape, dtype)


def rows_block(tile, width):
    return pl.BlockSpec((tile, width), lambda i: (i, 0))


def same_block(shape):
    return pl.BlockSpec(shape, lambda i: (0,) * len(shape))


def call(kernel, grid, in_specs, out_specs, out_shape, scratch=(), deps=(), prefetch=0):
    deps = list(deps)
    in_specs = in_specs + [ANY] * len(deps)
    extra = dict(
        in_specs=in_specs, out_specs=out_specs, scratch_shapes=scratch, **(dict(grid=grid) if grid else {})
    )
    if prefetch:
        extra = dict(
            grid_spec=pltpu.PrefetchScalarGridSpec(
                num_scalar_prefetch=prefetch,
                grid=grid,
                in_specs=in_specs,
                out_specs=out_specs,
                scratch_shapes=scratch,
            )
        )
    run = pl.pallas_call(
        kernel,
        out_shape=out_shape,
        compiler_params=pltpu.CompilerParams(vmem_limit_bytes=60 * 2**20),
        cost_estimate=pl.CostEstimate(flops=2**20, bytes_accessed=2**16, transcendentals=0),
        **extra,
    )
    return lambda *args: run(*args, *deps)


def weight_grads(pairs, deps=(), late=()):
    peers, blocks = lax.axis_size("gy"), lax.axis_size("dev")
    rows = pairs[0][1].shape[0]
    turned = [left.shape[1] == rows for left, _ in pairs]
    width = pairs[0][0].size // rows
    size = width // peers // blocks
    total = sum(right.shape[1] for _, right in pairs)
    if peers != 2:
        share = [(dot if t else dot_rows)(a, b) for t, (a, b) in zip(turned, pairs)]
        share = jnp.concatenate(share, axis=1).astype(BF)
        share = lax.psum_scatter(share, "gy", scatter_dimension=0, tiled=True)
        return share.reshape(blocks, size, total), None
    specs, operands = [], []
    for across, (left, right) in zip(turned, pairs):
        if across:
            specs += [
                pl.BlockSpec((size, rows), lambda c: (c, 0)),
                pl.BlockSpec((size, rows), lambda c: (blocks + c, 0)),
            ]
        else:
            specs += [
                pl.BlockSpec((rows, size), lambda c: (0, c)),
                pl.BlockSpec((rows, size), lambda c: (0, blocks + c)),
            ]
        specs.append(pl.BlockSpec(right.shape, lambda c: (0, 0)))
        operands += [left, left, right]
    chunk = pl.BlockSpec((1, size, total), lambda c: (c, 0, 0))
    own, other = call(
        functools.partial(weight_grad_kernel, turned),
        (blocks,),
        specs,
        [chunk, chunk],
        [out((blocks, size, total), BF), out((blocks, size, total), BF)],
        deps=deps,
    )(*operands)
    (other,) = after([other], *late)
    return own, shifted(other, "gy", 1)


def share_chunks(shares, deps=()):
    blocks, size, _ = shares[0][0].shape
    total = sum(own.shape[2] for own, _ in shares)
    if shares[0][1] is None:
        side = jnp.concatenate([own for own, _ in shares], axis=2)
        cut = lambda m: lax.dynamic_index_in_dim(side, dev_partner(m), 0, False)
        return [cut(0).astype(F32)] + [cut(m) for m in range(1, blocks)]
    chunks = jnp.stack([dev_partner(m) for m in range(blocks)]).astype(jnp.int32)
    return call(
        functools.partial(share_sum_kernel, len(shares)),
        None,
        [SMEM] + [VMEM] * (2 * len(shares)),
        [VMEM] * blocks,
        [out((size, total), F32)] + [out((size, total), BF)] * (blocks - 1),
        deps=deps,
    )(chunks, *[own for own, _ in shares], *[got for _, got in shares])


def dev_total(chunks):
    got = [dev_send(part, m) for m, part in enumerate(chunks[1:], 1)]
    total = chunks[0]
    for part in got:
        total = total + part.astype(F32)
    return total, got


def dev_all(total, deps=()):
    (sent,) = after([total.astype(BF)], *deps)
    return [dev_send(sent, m) for m in range(1, lax.axis_size("dev"))]


def widen(whole, pieces, deps=()):
    rows = whole.shape[0]
    shapes = [(w, rows) if turned else (rows, w) for _, w, turned in pieces]
    return call(
        functools.partial(widen_kernel, pieces),
        None,
        [VMEM],
        [VMEM] * len(pieces),
        [out(shape, F32) for shape in shapes],
        deps=deps,
    )(whole)


def assemble(total, others, pieces, deps=()):
    size, blocks = total.shape[0], 1 + len(others)
    owners = jnp.stack([lax.axis_index("dev")] + [dev_giver(m) for m in range(1, blocks)])
    shapes = [(w, size * blocks) if turned else (size * blocks, w) for _, w, turned in pieces]
    widest = max([w for _, w, turned in pieces if turned], default=128)
    return call(
        functools.partial(assemble_kernel, blocks, pieces),
        None,
        [SMEM] + [VMEM] * blocks,
        [VMEM] * len(pieces),
        [out(shape, F32) for shape in shapes],
        [pltpu.VMEM((size * blocks, widest), F32)],
        deps,
    )(owners.astype(jnp.int32), total, *others)


def per_device(
    tokens,
    norm_gain,
    w_query,
    key_projection,
    value_projection,
    query_gain,
    key_gain,
    w_out,
    ffn_gain,
    w_gate,
    w_up,
    w_down,
    cotangent,
    sequence,
    position,
):
    rows, piece = tokens.shape
    count = lax.axis_size("gx")
    peers = lax.axis_size("gy")
    width = piece * count
    head = query_gain.shape[0]
    q_cols, kv_cols, hidden_units = w_query.shape[1], key_projection.shape[1], w_gate.shape[1]
    gx, gy = lax.axis_index("gx"), lax.axis_index("gy")
    tile = min(256, rows)
    small_tile = min(128, rows)
    grid = (rows // tile,)

    def lies_at(block):
        if peers == 2 and count % 2 == 0:
            half = count // 2
            return ((block // half) ^ gy) * (half * piece) + (block % half) * piece
        return block * piece

    offsets = jnp.stack(
        [lies_at((gx - s) % count) for s in range(count)]
        + [lies_at((gx + s) % count) for s in range(count)]
    ).astype(jnp.int32)

    below = jnp.stack([norm_gain, ffn_gain] + [norm_gain] * 14)
    token_pieces = pieces_of(jnp.concatenate([tokens, below], axis=0))
    gain_block = pl.BlockSpec((16, piece), lambda i: (rows // 16, 0))
    query_parts, key_w_parts, value_w_parts = (
        gather_width(w, 0) for w in (w_query, key_projection, value_projection)
    )
    out_w_parts, down_parts = gather_width(w_out, 1), gather_width(w_down, 1)
    gate_parts, up_parts = gather_width(w_gate, 0), gather_width(w_up, 0)
    halves = len(gate_parts)

    all_seq, all_pos = sequence.reshape(peers, rows), position.reshape(peers, rows)
    if peers == 2:
        order = lambda a: jnp.where(gy == 0, a, a[::-1])
        all_seq, all_pos = order(all_seq), order(all_pos)
        own_seq, own_pos = all_seq[0], all_pos[0]
    else:
        own_seq = lax.dynamic_index_in_dim(all_seq, gy, 0, False)
        own_pos = lax.dynamic_index_in_dim(all_pos, gy, 0, False)
    row_info = jnp.concatenate(
        [own_seq[None], own_pos[None], jnp.zeros((6, rows), jnp.int32)], axis=0
    ).astype(F32)
    if peers == 2:
        col_info = jnp.concatenate(
            [all_seq[:1], all_pos[:1], all_seq[1:], all_pos[1:], jnp.zeros((4, rows), jnp.int32)],
            axis=0,
        ).astype(F32)
    else:
        col_info = jnp.stack([all_seq, all_pos], axis=-1).astype(F32)
    lane = jnp.arange(head)
    rates = THETA ** (-((lane % (head // 2)).astype(F32) * 2.0) / head)
    phase = own_pos.astype(F32)[:, None] * rates[None, :]
    cosine = jnp.cos(phase)
    sine = jnp.sin(phase) * jnp.where(lane < head // 2, -1.0, 1.0)[None, :]
    q_scale = query_gain.astype(F32)[None]
    k_scale = key_gain.astype(F32)[None]

    def whole(parts):
        return [same_block(p.shape) for p in parts]

    normed_one, scale_one, query_lin, key_lin, query_bf, key_bf, value_bf = call(
        functools.partial(qkv_kernel, count, halves, head),
        grid,
        [SMEM]
        + [rows_block(tile, piece)] * count
        + [gain_block] * count
        + whole(query_parts + key_w_parts + value_w_parts)
        + [same_block((1, head))] * 2
        + [rows_block(tile, head)] * 2,
        [
            rows_block(tile, width),
            rows_block(tile, 1),
            rows_block(tile, q_cols),
            rows_block(tile, kv_cols),
            rows_block(tile, q_cols),
            rows_block(tile, kv_cols),
            rows_block(tile, kv_cols),
        ],
        [
            out((rows, width), BF),
            out((rows, 1), F32),
            out((rows, q_cols), F32),
            out((rows, kv_cols), F32),
            out((rows, q_cols), BF),
            out((rows, kv_cols), BF),
            out((rows, kv_cols), BF),
        ],
        deps=[row_info, col_info],
    )(
        offsets, *token_pieces, *token_pieces, *query_parts, *key_w_parts, *value_w_parts,
        q_scale, k_scale, cosine, sine,
    )
    if peers == 2:
        keys = [key_bf, shifted(key_bf, "gy", 1)]
        values = [value_bf, shifted(value_bf, "gy", 1)]
    else:
        keys = [lax.all_gather(key_bf, "gy", axis=0)]
        values = [lax.all_gather(value_bf, "gy", axis=0)]
    (late_cotangent,) = after([cotangent], *token_pieces[1:])
    cot_pieces = [cotangent] + pieces_of(late_cotangent)[1:]

    mixed, attended, logs = call(
        functools.partial(attend_kernel, head, small_tile, peers),
        None,
        [VMEM] * (3 + 2 * len(keys)),
        [VMEM] * 3,
        [
            out((rows, q_cols), BF),
            out((q_cols, rows), F32),
            out((max(8, q_cols // head), rows), F32),
        ],
        deps=[cot_pieces[1], cot_pieces[-1]],
    )(query_bf, row_info, col_info, *keys, *values)

    split_out = [out((rows, piece), F32)] + [out((rows, piece), BF)] * (count - 1)

    def split_dot(left, weights, *deps):
        return call(
            functools.partial(split_dot_kernel, count, halves),
            grid,
            [SMEM, rows_block(tile, left.shape[1])] + whole(weights),
            [rows_block(tile, piece)] * count,
            split_out,
            deps=deps,
        )(offsets, left, *weights)

    out_parts = split_dot(mixed, out_w_parts, *cot_pieces[1:])
    inputs = tokens.astype(F32)
    hidden = inputs + piece_sum(out_parts[0], out_parts[1:])

    cot_whole, grad_product, normed_turned = call(
        functools.partial(cot_kernel, count),
        grid,
        [SMEM] + [rows_block(tile, piece)] * count + [rows_block(tile, width)] + whole(down_parts),
        [
            rows_block(tile, width),
            rows_block(tile, hidden_units),
            pl.BlockSpec((width, tile), lambda i: (0, i)),
        ],
        [out((rows, width), BF), out((rows, hidden_units), F32), out((width, rows), BF)],
    )(offsets, *cot_pieces, normed_one, *down_parts)

    hidden_pieces = pieces_of(hidden.astype(BF))
    *grad_parts, normed_two, scale_two, product, gate_bf, up_bf = call(
        functools.partial(ffn_kernel, count, halves),
        grid,
        [SMEM]
        + [rows_block(tile, piece)] * count
        + [gain_block] * count
        + whole(gate_parts + up_parts)
        + [rows_block(tile, hidden_units)],
        [rows_block(tile, piece)] * count
        + [rows_block(tile, width), rows_block(tile, 1)]
        + [rows_block(tile, hidden_units)] * 3,
        split_out
        + [out((rows, width), BF), out((rows, 1), F32)]
        + [out((rows, hidden_units), BF)] * 3,
    )(offsets, *hidden_pieces, *token_pieces, *gate_parts, *up_parts, grad_product)

    grad_got = [shifted(p, "gx", s) for s, p in enumerate(grad_parts[1:], 1)]
    ffn_own, ffn_got = weight_grads(
        [(normed_two, gate_bf), (normed_two, up_bf), (cot_whole, product)], late=grad_got
    )
    grad_normed_two = grad_parts[0]
    for part in grad_got:
        grad_normed_two = grad_normed_two + part.astype(F32)
    (grad_low,) = after([grad_normed_two.astype(BF)], ffn_own)
    grad_pieces = [grad_low] + pieces_of(grad_low)[1:]
    blocks, size, total = ffn_own.shape
    if peers == 2:
        row_tile = rows // blocks
        chunk = pl.BlockSpec((1, size, total), lambda i: (i, 0, 0))
        *result_parts, ffn_share = call(
            functools.partial(result_share_kernel, count, halves),
            (blocks,),
            [SMEM, rows_block(row_tile, hidden_units)] + whole(down_parts) + [chunk, chunk],
            [rows_block(row_tile, piece)] * count + [rows_block(size, total)],
            split_out + [out((blocks * size, total), BF)],
            deps=grad_got,
        )(offsets, product, *down_parts, ffn_own, ffn_got)
    else:
        result_parts = split_dot(product, down_parts)
        ffn_share = ffn_own.reshape(blocks * size, total)
    (ffn_share,) = after([ffn_share], *grad_pieces[1:])
    ffn_chunk = lax.psum_scatter(ffn_share, "dev", scatter_dimension=0, tiled=True)

    branch, grad_mixed, inner_two = call(
        functools.partial(branch_kernel, count, halves),
        grid,
        [SMEM]
        + [rows_block(tile, piece)] * (2 * count)
        + [gain_block] * count
        + [rows_block(tile, 1), rows_block(tile, width)]
        + whole(out_w_parts),
        [rows_block(tile, width), rows_block(tile, q_cols), rows_block(tile, 1)],
        [out((rows, width), BF), out((rows, q_cols), BF), out((rows, 1), F32)],
    )(
        offsets, *hidden_pieces, *grad_pieces, *token_pieces, scale_two, cot_whole, *out_w_parts
    )

    late_parts = after(result_parts[1:], *grad_pieces[1:])
    result_got = [shifted(p, "gx", s) for s, p in enumerate(late_parts, 1)]
    result = hidden + result_parts[0]
    for part in result_got:
        result = result + part.astype(F32)
    out_own, out_got = weight_grads([(branch, mixed)])

    grad_query_lin, query_gain_part, *kv_parts = call(
        functools.partial(attend_back_kernel, head, small_tile, peers),
        None,
        [VMEM] * (10 + 2 * len(keys)),
        [VMEM] * (2 + 2 * len(keys)),
        [out((rows, q_cols), BF), out((1, head), F32)]
        + [out(k.shape, BF) for k in keys + values],
        [pltpu.VMEM((peers, rows, kv_cols), F32), pltpu.VMEM((peers, rows, kv_cols), F32)],
        deps=[out_own, result_got[0], result_got[-1]],
    )(
        grad_mixed, query_bf, query_lin, row_info, col_info, attended, logs,
        q_scale, cosine, sine, *keys, *values,
    )
    if peers == 2:
        key_terms = [kv_parts[0], shifted(kv_parts[1], "gy", 1)]
        value_terms = [kv_parts[2], shifted(kv_parts[3], "gy", 1)]
    else:
        share = lambda a: lax.psum_scatter(a, "gy", scatter_dimension=0, tiled=True)[0]
        key_terms, value_terms = [share(kv_parts[0])], [share(kv_parts[1])]

    fused = peers == 2
    shares = [out(out_own.shape[:2] + (q_cols + 2 * kv_cols,), BF)] * 2 if fused else []
    *last_outs, grad_key_lin, grad_value_lin = call(
        functools.partial(lin_back_kernel, count, halves, head, len(key_terms), fused),
        None,
        [SMEM] + [VMEM] * (8 + 2 * len(key_terms) + 3 * halves + fused),
        [VMEM] * (count + 2 + len(shares)),
        shares
        + [out((rows + 16, piece), p.dtype) for p in split_out]
        + [out((rows, kv_cols), BF)] * 2,
        deps=result_got[1:-1],
    )(
        offsets, grad_query_lin, query_lin, key_lin, value_bf, query_gain_part,
        *key_terms, *value_terms, k_scale, cosine, sine,
        *query_parts, *key_w_parts, *value_w_parts, *([normed_turned] if fused else []),
    )
    last_parts = last_outs[len(shares) :]
    last_got = [shifted(p, "gx", s) for s, p in enumerate(last_parts[1:], 1)]
    if fused:
        last_share = last_outs[0], shifted(last_outs[1], "gy", 1)
    else:
        last_share = weight_grads(
            [(normed_turned, g) for g in (grad_query_lin, grad_key_lin, grad_value_lin)]
        )
    last_chunks = share_chunks([last_share, (out_own, out_got)])
    (ffn_low,) = after([ffn_chunk], last_chunks[1])
    ffn_sum = lax.all_gather(ffn_low, "dev", axis=0, tiled=True)
    last_total, dev_got = dev_total(last_chunks)
    last_others = dev_all(last_total)
    gate_grad, up_grad, down_grad = widen(
        ffn_sum,
        (
            (0, hidden_units, False),
            (hidden_units, hidden_units, False),
            (2 * hidden_units, hidden_units, True),
        ),
        [last_total],
    )
    cuts = (0, q_cols, q_cols + kv_cols, q_cols + 2 * kv_cols)
    query_grad, key_grad, value_grad, out_grad = assemble(
        last_total,
        last_others,
        (
            (cuts[0], q_cols, False),
            (cuts[1], kv_cols, False),
            (cuts[2], kv_cols, False),
            (cuts[3], q_cols, True),
        ),
        [down_grad],
    )

    grad_inputs, gain_part = call(
        functools.partial(final_kernel, count),
        None,
        [VMEM] * (count + 8),
        [VMEM] * 2,
        [out((rows, piece), F32), out((8, piece), F32)],
        deps=dev_got[:1],
    )(
        last_parts[0], *last_got, tokens, cotangent, hidden, grad_normed_two,
        scale_one, scale_two, inner_two, below,
    )
    if peers == 2:
        last = small_sum(small_sum(gain_part, "gy"), "dev")
    else:
        last = lax.psum(gain_part, ("dev", "gy"))
    return (
        result.astype(BF),
        grad_inputs,
        last[0],
        query_grad,
        key_grad,
        value_grad,
        last[2, :head],
        last[2, head : 2 * head],
        out_grad,
        last[1],
        gate_grad,
        up_grad,
        down_grad,
    )


def solution(mesh):
    wide = P(("dev", "gy"), "gx")
    weight, back = P("gy", "gx"), P("gx", "gy")
    return jax.shard_map(
        per_device,
        mesh=mesh,
        in_specs=(
            wide, P("gx"), weight, weight, weight, P(), P(), back, P("gx"), weight, weight, back,
            wide, P("dev"), P("dev"),
        ),
        out_specs=(
            wide, wide, P("gx"), weight, weight, weight, P(), P(), back, P("gx"), weight, weight,
            back,
        ),
        check_vma=False,
    )
```

time: 386 us -> 314 us (0.81); the launches traced: 380 us -> 313 us
  starting transfers between devices: 114 us -> 54.9 us
  Pallas kernels: 40.3 us -> 82.8 us
  waiting for transfers between devices: 160 us -> 125 us
  matrix products: 19.8 us -> 0 us
  between operations: 2.41 us -> 15 us
  local copies, waits for them, and re-layouts: 26.6 us -> 21.8 us
    ppermute x42 -> x6, waiting for transfers between devices: 54 us -> 0.02 us  [dev_send(): lax.ppermute(block, 'dev', [(i, i ^ m if even else (i + m) % count) for i...]
    pallas_call x7 -> x21, Pallas kernels: 40.3 us -> 82.8 us  [the longest x15 82.8 us: call(): return lambda *args: run(*args, *deps)]
    ppermute x42 -> x6, starting transfers between devices: 49.5 us -> 8.06 us  [dev_send(): lax.ppermute(block, 'dev', [(i, i ^ m if even else (i + m) % count) for i...]
    all_gather x0 -> x1, waiting for transfers between devices: none -> 25.6 us  [per_device(): ffn_sum = lax.all_gather(ffn_low, 'dev', axis=0, tiled=True)]
    dot_general x14 -> x0, matrix products: 19.8 us -> none  [dot_rows(): lax.dot_general(left, right, (((0,), (0,)), ((), ())), preferred_element_...]
    ppermute x52 -> x42, starting transfers between devices: 64.3 us -> 46.8 us  [shifted(): lax.ppermute(block, axis, [(i, (i + shift) % size) for i in range(size)])]
    ppermute x52 -> x42, waiting for transfers between devices: 106 us -> 99 us  [shifted(): lax.ppermute(block, axis, [(i, (i + shift) % size) for i in range(size)])]
    concatenate x8 -> x0, other arithmetic: 4.46 us -> none  [the longest x2 4.02 us: gather_width(): return jnp.concatenate([block, shifted(block, 'gy', 1)], axis=axis)]
  transfers between devices with their start and end apart: 94 -> 50, of which waited for: 38 -> 17; matrix products, arithmetic and copies ran while one was open for 14% -> 7% of each run, Pallas kernels for 9% -> 22%
where the time goes in v2:
time: 314 us; the launch traced here: 313 us
  waiting for transfers between devices  125 us (40%)
  Pallas kernels  82.8 us (26%)
  starting transfers between devices  54.9 us (17%)
  local copies, waits for them, and re-layouts  21.8 us (7%)
  between operations  15 us (5%)
  other arithmetic  14.1 us (4%)
    ppermute x42, waiting for transfers between devices, shifted(): lax.ppermute(block, axis, [(i, (i + shift) % size) for i in range(size)])  99 us
    pallas_call x15, Pallas kernels, call(): return lambda *args: run(*args, *deps)  82.8 us
    ppermute x42, starting transfers between devices, shifted(): lax.ppermute(block, axis, [(i, (i + shift) % size) for i in range(size)])  46.8 us
    all_gather x1, waiting for transfers between devices, per_device(): ffn_sum = lax.all_gather(ffn_low, 'dev', axis=0, tiled=True)  25.6 us
    unnamed x105, local copies, waits for them, and re-layouts  14.7 us
    ppermute x6, starting transfers between devices, dev_send(): lax.ppermute(block, 'dev', [(i, i ^ m if even else (i + m) % count) for i...  8.06 us
  transfers between devices with their start and end apart: 50, of which 17 were waited for; matrix products, arithmetic and copies ran while one was open for 7% of the time, Pallas kernels for 22%

profile of v2, /device:TPU:0, one launch (start us, length us, event | category | flops | bytes accessed | tf_op | source)
XLA Modules:
  0.0 313.3 jit_solution(8068433230096002915)
XLA Ops:
  8.5 1.0 concatenate.10.refs_0_.refs_4_.refs_8_
  9.6 5.1 %collective-permute-start.2 = (bf16[528,256]{1,0:T(8,128)(2,1)S(1)}, bf16[528,256]{1,0:T(8,128)(2,1)S(1)}, u32[]{:S(2)}, u32[]{:S(2)}) collective-permute-start(bf16[528,256]{1,0:T(8,128)(2,1)S(1)} %concatenate.10.refs_0_.refs_4_.refs_8_), channel_id=1, source_target_pairs={{0,6},{2,0},{4,2},{6,4},{1,7},{3,1},{5,3},{7,5},{8,14},{10,8},{12,... | collective-permute-start | bytes 811016 | tf_op jit(solution)/shard_map/ppermute | solution.py:42
  14.7 1.0 collective-permute-start
  18.6 1.1 bitcast_convert_fusion.1.refs_14_.refs_7_
  19.8 1.7 copy.36.refs_0_
  21.5 1.2 bitcast_convert_fusion.refs_15_.refs_9_
  22.6 15.1 %collective-permute-done.1.refs_2_.refs_6_.refs_10_ = bf16[528,256]{1,0:T(8,128)(2,1)S(1)} collective-permute-done((bf16[528,256]{1,0:T(8,128)(2,1)S(1)}, bf16[528,256]{1,0:T(8,128)(2,1)S(1)}, u32[]{:S(2)}, u32[]{:S(2)}) %collective-permute-start.1) | collective-permute-done | bytes 270368 | tf_op jit(solution)/shard_map/ppermute | solution.py:42
  38.4 0.7 copy-done.3
  40.7 1.8 fusion
  42.5 1.7 collective-permute-start.8
  45.2 5.7 %shard_map.246 = (bf16[512,1024]{1,0:T(8,128)(2,1)}, f32[512,1]{1,0:T(8,128)}, f32[512,512]{1,0:T(8,128)}, f32[512,256]{1,0:T(8,128)}, bf16[512,512]{1,0:T(8,128...) custom-call(s32[8]{0:T(128)} %stack.75.offset_ref, bf16[528,256]{1,0:T(8,128)(2,1)} %copy-done, ...), custom_call_target="tpu_custom_call" | custom-call | flops 1048576 | bytes 65536 | tf_op jit(solution)/shard_map/pallas_call | solution.py:573
  51.4 2.2 collective-permute-start.11
  54.8 7.5 %shard_map.248 = (bf16[512,512]{1,0:T(8,128)(2,1)}, f32[512,512]{1,0:T(8,128)}, f32[8,512]{1,0:T(8,128)}) custom-call(bf16[512,512]{1,0:T(8,128)(2,1)} %get-tuple-element.79.q_ref.refs_1_, f32[8,512]{1,0:T(8,128)} %add_convert_fusion.1.refs_18_.row_ref.refs_3_, f32[8,512]{1,0:T(8,128)} %convert_element_type.81.refs_19_.col_ref.refs_4_, ...), custom_call_target="tpu_custom_call" | custom-call | flops 1048576 | bytes 65536 | tf_op jit(solution)/shard_map/pallas_call | solution.py:573
  62.3 4.0 %collective-permute-done.11.refs_3_.refs_2_ = bf16[512,256]{1,0:T(8,128)(2,1)S(1)} collective-permute-done((bf16[512,256]{1,0:T(8,128)(2,1)S(1)}, bf16[512,256]{1,0:T(8,128)(2,1)S(1)}, u32[]{:S(2)}, u32[]{:S(2)}) %collective-permute-start.11) | collective-permute-done | bytes 262176 | tf_op jit(solution)/shard_map/ppermute | solution.py:42
  67.0 2.9 shard_map.249
  70.0 2.6 collective-permute-start.13
  72.6 1.2 collective-permute-start.14
  74.0 7.3 %collective-permute-done.12 = bf16[512,256]{1,0:T(8,128)(2,1)S(1)} collective-permute-done((bf16[512,256]{1,0:T(8,128)(2,1)}, bf16[512,256]{1,0:T(8,128)(2,1)S(1)}, u32[]{:S(2)}, u32[]{:S(2)}) %collective-permute-start.12) | collective-permute-done | bytes 262176 | tf_op jit(solution)/shard_map/ppermute | solution.py:42
  81.3 9.8 %collective-permute-done.13 = bf16[512,256]{1,0:T(8,128)(2,1)S(1)} collective-permute-done((bf16[512,256]{1,0:T(8,128)(2,1)}, bf16[512,256]{1,0:T(8,128)(2,1)S(1)}, u32[]{:S(2)}, u32[]{:S(2)}) %collective-permute-start.13) | collective-permute-done | bytes 262176 | tf_op jit(solution)/shard_map/ppermute | solution.py:42
  91.1 2.0 fusion.8
  93.1 4.2 %collective-permute-start.17 = (bf16[512,256]{1,0:T(8,128)(2,1)S(1)}, bf16[512,256]{1,0:T(8,128)(2,1)S(1)}, u32[]{:S(2)}, u32[]{:S(2)}) collective-permute-start(bf16[512,256]{1,0:T(8,128)(2,1)S(1)} %get-tuple-element.149.refs_0_), channel_id=1, source_target_pairs={{0,6},{2,0},{4,2},{6,4},{1,7},{3,1},{5,3},{7,5},{8,14},{10,8},{12,... | collective-permute-start | bytes 786440 | tf_op jit(solution)/shard_map/ppermute | solution.py:42
  97.3 3.4 %collective-permute-start.16 = (bf16[512,256]{1,0:T(8,128)(2,1)S(1)}, bf16[512,256]{1,0:T(8,128)(2,1)S(1)}, u32[]{:S(2)}, u32[]{:S(2)}) collective-permute-start(bf16[512,256]{1,0:T(8,128)(2,1)S(1)} %get-tuple-element.149.refs_0_), channel_id=1, source_target_pairs={{0,4},{2,6},{4,0},{6,2},{1,5},{3,7},{5,1},{7,3},{8,12},{10,14},{12... | collective-permute-start | bytes 786440 | tf_op jit(solution)/shard_map/ppermute | solution.py:42
  100.7 0.9 copy-done.6
  101.6 4.3 %shard_map.250 = (bf16[512,1024]{1,0:T(8,128)(2,1)}, f32[512,768]{1,0:T(8,128)}, bf16[1024,512]{1,0:T(8,128)(2,1)}) custom-call(s32[8]{0:T(128)} %stack.75.offset_ref, bf16[512,256]{1,0:T(8,128)(2,1)} %refs_5_.3, bf16[512,256]{1,0:T(8,128)(2,1)} %copy-done.11, bf16[512,256]{1,0:T(8,128)(2,1)} %copy-done.37, bf16[512,256]{1,0:T(8,128)(2,1)} %copy-done.10, ...), custom_call_target="tpu_custom_call" | custom-call | flops 1048576 | bytes 65536 | tf_op jit(solution)/shard_map/pallas_call | solution.py:573
  106.0 17.8 %collective-permute-done.16.refs_2_ = bf16[512,256]{1,0:T(8,128)(2,1)S(1)} collective-permute-done((bf16[512,256]{1,0:T(8,128)(2,1)S(1)}, bf16[512,256]{1,0:T(8,128)(2,1)S(1)}, u32[]{:S(2)}, u32[]{:S(2)}) %collective-permute-start.16) | collective-permute-done | bytes 262176 | tf_op jit(solution)/shard_map/ppermute | solution.py:42
  124.6 8.3 %shard_map.251 = (f32[512,256]{1,0:T(8,128)}, bf16[512,256]{1,0:T(8,128)(2,1)}, bf16[512,256]{1,0:T(8,128)(2,1)}, bf16[512,256]{1,0:T(8,128)(2,1)}, bf16[512,102...) custom-call(s32[8]{0:T(128)} %stack.75.offset_ref, ...), custom_call_target="tpu_custom_call" | custom-call | flops 1048576 | bytes 65536 | tf_op jit(solution)/shard_map/pallas_call | solution.py:573
  133.2 3.7 %collective-permute-start.23 = (bf16[512,256]{1,0:T(8,128)(2,1)}, bf16[512,256]{1,0:T(8,128)(2,1)S(1)}, u32[]{:S(2)}, u32[]{:S(2)}) collective-permute-start(bf16[512,256]{1,0:T(8,128)(2,1)} %get-tuple-element.98), channel_id=1, source_target_pairs={{0,6},{2,0},{4,2},{6,4},{1,7},{3,1},{5,3},{7,5},{8,14},{10,8},{12,... | collective-permute-start | bytes 786440 | tf_op jit(solution)/shard_map/ppermute | solution.py:42
  137.0 7.2 %shard_map.252 = (bf16[4,128,2304]{2,1,0:T(8,128)(2,1)}, bf16[4,128,2304]{2,1,0:T(8,128)(2,1)}) custom-call(bf16[512,1024]{1,0:T(8,128)(2,1)} %get-tuple-element.90.refs_0_.refs_1_.refs_3_.refs_4_, bf16[512,1024]{1,0:T(8,128)(2,1)} %get-tuple-element.90.refs_0_.refs_1_.refs_3_.refs_4_, bf16[512,768]{1,0:T(8,128)(2,1)} %get-tuple-element.91.refs_2_, ...), custom_call_target="tpu_custom_call" | custom-call | flops 1048576 | bytes 65536 | tf_op jit(solution)/shard_map/pallas_call | solution.py:573
  144.5 9.5 %collective-permute-done.22.refs_2_.refs_5_ = bf16[512,256]{1,0:T(8,128)(2,1)S(1)} collective-permute-done((bf16[512,256]{1,0:T(8,128)(2,1)}, bf16[512,256]{1,0:T(8,128)(2,1)S(1)}, u32[]{:S(2)}, u32[]{:S(2)}) %collective-permute-start.22) | collective-permute-done | bytes 262176 | tf_op jit(solution)/shard_map/ppermute | solution.py:42
  154.8 2.3 fusion.7
  157.1 4.4 %collective-permute-start.27 = (bf16[512,256]{1,0:T(8,128)(2,1)}, bf16[512,256]{1,0:T(8,128)(2,1)S(1)}, u32[]{:S(2)}, u32[]{:S(2)}) collective-permute-start(bf16[512,256]{1,0:T(8,128)(2,1)} %shard_map.255.refs_4_), channel_id=1, source_target_pairs={{0,6},{2,0},{4,2},{6,4},{1,7},{3,1},{5,3},{7,5},{8,14},{10,8},{12,... | collective-permute-start | bytes 786440 | tf_op jit(solution)/shard_map/ppermute | solution.py:42
  161.5 2.1 collective-permute-start.26
  163.7 1.5 copy-done.9
  165.1 6.6 %shard_map.254 = (f32[512,256]{1,0:T(8,128)}, bf16[512,256]{1,0:T(8,128)(2,1)}, bf16[512,256]{1,0:T(8,128)(2,1)}, bf16[512,256]{1,0:T(8,128)(2,1)}, bf16[512,2304]{1,0:T(8,128)(2,1)}) custom-call(s32[8]{0:T(128)} %stack.75.offset_ref, bf16[512,768]{1,0:T(8,128)(2,1)} %get-tuple-element.89.refs_8_.left_ref, bf16[768,512]{1,0:T(8,128)(2,1)} %refs_0_.6, ...), custom_call_target="tpu_custom_call" | custom-call | flops 1048576 | bytes 65536 | tf_op jit(solution)/shard_map/pallas_call | solution.py:573
  171.7 15.7 %collective-permute-done.26.refs_4_.refs_6_.refs_2_ = bf16[512,256]{1,0:T(8,128)(2,1)S(1)} collective-permute-done((bf16[512,256]{1,0:T(8,128)(2,1)}, bf16[512,256]{1,0:T(8,128)(2,1)S(1)}, u32[]{:S(2)}, u32[]{:S(2)}) %collective-permute-start.26) | collective-permute-done | bytes 262176 | tf_op jit(solution)/shard_map/ppermute | solution.py:42
  188.4 3.8 %collective-permute-start.30 = (bf16[512,256]{1,0:T(8,128)(2,1)}, bf16[512,256]{1,0:T(8,128)(2,1)S(1)}, u32[]{:S(2)}, u32[]{:S(2)}) collective-permute-start(bf16[512,256]{1,0:T(8,128)(2,1)} %get-tuple-element.106), channel_id=1, source_target_pairs={{0,6},{2,0},{4,2},{6,4},{1,7},{3,1},{5,3},{7,5},{8,14},{10,8},{12,... | collective-permute-start | bytes 786440 | tf_op jit(solution)/shard_map/ppermute | solution.py:42
  192.2 5.2 %shard_map.257 = (bf16[512,1024]{1,0:T(8,128)(2,1)}, bf16[512,512]{1,0:T(8,128)(2,1)}, f32[512,1]{1,0:T(8,128)}) custom-call(s32[8]{0:T(128)} %stack.75.offset_ref, bf16[512,256]{1,0:T(8,128)(2,1)} %copy-done.7, bf16[512,256]{1,0:T(8,128)(2,1)} %copy-done.26, bf16[512,256]{1,0:T(8,128)(2,1)} %copy-done.25, bf16[512,256]{1,0:T(8,128)(2,1)} %copy-done.24, ...), custom_call_target="tpu_custom_call" | custom-call | flops 1048576 | bytes 65536 | tf_op jit(solution)/shard_map/pallas_call | solution.py:573
  197.4 4.3 %shard_map.258 = (bf16[4,128,512]{2,1,0:T(8,128)(2,1)}, bf16[4,128,512]{2,1,0:T(8,128)(2,1)}) custom-call(bf16[512,1024]{1,0:T(8,128)(2,1)} %get-tuple-element.112.refs_0_.refs_1_, bf16[512,1024]{1,0:T(8,128)(2,1)} %get-tuple-element.112.refs_0_.refs_1_, bf16[512,512]{1,0:T(8,128)(2,1)} %get-tuple-element.82.left_ref.refs_2_), custom_call_target="tpu_custom_call" | custom-call | flops 1048576 | bytes 65536 | tf_op jit(solution)/shard_map/pallas_call | solution.py:573
  202.9 8.1 %shard_map.259 = (bf16[512,512]{1,0:T(8,128)(2,1)}, f32[1,128]{1,0:T(1,128)}, bf16[512,256]{1,0:T(8,128)(2,1)}, bf16[512,256]{1,0:T(8,128)(2,1)}, bf16[512,256]{1,0:T(8,128)(2,1)}, /*index=5*/bf16[512,256]{1,0:T(8,128)(2,1)}) custom-call(bf16[512,512]{1,0:T(8,128)(2,1)} %get-tuple-element.108.refs_0_, bf16[512,512]{1,0:T(8,128)(2,1)} %get-tuple-element.79.q_ref.refs_1_, ...), custom_call_target="tpu_custom_call" | custom-call | flops 1048576 | bytes 65536 | tf_op jit(solution)/shard_map/pallas_call | solution.py:573
  211.5 3.0 collective-permute-done.29.refs_19_
  215.5 8.2 %shard_map.260 = (bf16[4,128,1024]{2,1,0:T(8,128)(2,1)}, bf16[4,128,1024]{2,1,0:T(8,128)(2,1)}, f32[528,256]{1,0:T(8,128)}, bf16[528,256]{1,0:T(8,128)(2,1)}, bf...) custom-call(s32[8]{0:T(128)} %stack.75.offset_ref, ...), custom_call_target="tpu_custom_call" | custom-call | flops 1048576 | bytes 65536 | tf_op jit(solution)/shard_map/pallas_call | solution.py:573
  224.9 2.2 collective-permute-done.37.refs_3_
  227.2 0.7 copy-done.42
  228.3 3.4 %shard_map.261 = (f32[128,1536]{1,0:T(8,128)}, bf16[128,1536]{1,0:T(8,128)(2,1)}, bf16[128,1536]{1,0:T(8,128)(2,1)}, bf16[128,1536]{1,0:T(8,128)(2,1)}) custom-call(s32[4]{0:T(128)} %pad_add_fusion.chunk_ref.owner_ref, bf16[4,128,1024]{2,1,0:T(8,128)(2,1)} %get-tuple-element.128.refs_0_, bf16[4,128,512]{2,1,0:T(8,128)(2,1)} %get-tuple-element.113.refs_14_.refs_1_, ...), custom_call_target="tpu_custom_call" | custom-call | flops 1048576 | bytes 65536 | tf_op jit(solution)/shard_map/pallas_call | solution.py:573
  231.7 1.6 collective-permute-start.38
  233.5 1.9 collective-permute-start.34
  235.4 2.7 collective-permute-start.35
  238.1 1.5 collective-permute-start.43
  239.7 5.1 %collective-permute-done.33.refs_1_ = bf16[528,256]{1,0:T(8,128)(2,1)S(1)} collective-permute-done((bf16[528,256]{1,0:T(8,128)(2,1)}, bf16[528,256]{1,0:T(8,128)(2,1)S(1)}, u32[]{:S(2)}, u32[]{:S(2)}) %collective-permute-start.33) | collective-permute-done | bytes 270368 | tf_op jit(solution)/shard_map/ppermute | solution.py:42
  244.8 1.5 collective-permute-start.44
  246.2 1.2 stack.78.refs_11_
  247.5 7.8 %collective-permute-done.34.refs_2_ = bf16[528,256]{1,0:T(8,128)(2,1)S(1)} collective-permute-done((bf16[528,256]{1,0:T(8,128)(2,1)}, bf16[528,256]{1,0:T(8,128)(2,1)S(1)}, u32[]{:S(2)}, u32[]{:S(2)}) %collective-permute-start.34) | collective-permute-done | bytes 270368 | tf_op jit(solution)/shard_map/ppermute | solution.py:42
  256.1 3.5 %shard_map.262 = (f32[512,256]{1,0:T(8,128)}, f32[8,256]{1,0:T(8,128)}) custom-call(f32[528,256]{1,0:T(8,128)} %get-tuple-element.122.refs_0_, bf16[528,256]{1,0:T(8,128)(2,1)} %copy-done.46, bf16[528,256]{1,0:T(8,128)(2,1)} %copy-done.47, bf16[528,256]{1,0:T(8,128)(2,1)} %collective-permute-done.35.refs_3_, bf16[512,256]{1,0:T(8,128)(2,1)} %refs_4_.1, ...), custom_call_target="tpu_custom_call" | custom-call | flops 1048576 | bytes 65536 | tf_op jit(solution)/shard_map/pallas_call | solution.py:573
  259.7 0.9 add_convert_fusion
  261.0 0.7 add.188
  261.7 1.5 collective-permute-start.42
  263.7 1.6 collective-permute-start.40
  265.3 2.2 fusion.6
  267.5 1.3 collective-permute-start.47
  268.8 1.6 collective-permute-start.46
  272.1 25.6 %all-gather.2.cloned.1.call-done.whole_ref = bf16[512,2304]{1,0:T(8,128)(2,1)} async-done(((bf16[128,2304]{1,0:T(8,128)(2,1)}), bf16[512,2304]{1,0:T(8,128)(2,1)}) %all-gather.2.cloned.1.call-update) | async-done | bytes 2359312 | tf_op jit(solution)/shard_map/all_gather | solution.py:946
  297.7 4.2 %shard_map.265 = (f32[512,768]{1,0:T(8,128)}, f32[512,768]{1,0:T(8,128)}, f32[768,512]{1,0:T(8,128)}) custom-call(bf16[512,2304]{1,0:T(8,128)(2,1)} %all-gather.2.cloned.1.call-done.whole_ref, f32[128,1536]{1,0:T(8,128)} %get-tuple-element.146.refs_0_), custom_call_target="tpu_custom_call" | custom-call | flops 1048576 | bytes 65536 | tf_op jit(solution)/shard_map/pallas_call | solution.py:573
  301.9 0.7 copy-done.43
  303.0 3.5 %shard_map.266 = (f32[512,512]{1,0:T(8,128)}, f32[512,256]{1,0:T(8,128)}, f32[512,256]{1,0:T(8,128)}, f32[512,512]{1,0:T(8,128)}) custom-call(s32[4]{0:T(128)} %pad_add_fusion.chunk_ref.owner_ref, f32[128,1536]{1,0:T(8,128)} %get-tuple-element.146.refs_0_, bf16[128,1536]{1,0:T(8,128)(2,1)} %copy-done.45, bf16[128,1536]{1,0:T(8,128)(2,1)} %copy-done.44, ...), custom_call_target="tpu_custom_call" | custom-call | flops 1048576 | bytes 65536 | tf_op jit(solution)/shard_map/pallas_call | solution.py:573
  (195 shorter events, 21.2 us)
Async XLA Ops:
  7.2 224.5 %reduce-scatter.2.cloned.1.call-start = ((), (), s32[]{:S(2)}) async-start(), calls=%async_computation.1 | async-start | bytes 2949120 | tf_op jit(solution)/shard_map/reduce_scatter | solution.py:877
  9.6 34.7 %copy-start = (bf16[528,256]{1,0:T(8,128)(2,1)}, bf16[528,256]{1,0:T(8,128)(2,1)S(1)}, u32[]{:S(2)}) copy-start(bf16[528,256]{1,0:T(8,128)(2,1)S(1)} %concatenate.10.refs_0_.refs_4_.refs_8_) | copy-start | bytes 811012
  9.6 13.0 %collective-permute-start.2 = (bf16[528,256]{1,0:T(8,128)(2,1)S(1)}, bf16[528,256]{1,0:T(8,128)(2,1)S(1)}, u32[]{:S(2)}, u32[]{:S(2)}) collective-permute-start(bf16[528,256]{1,0:T(8,128)(2,1)S(1)} %concatenate.10.refs_0_.refs_4_.refs_8_), channel_id=1, source_target_pairs={{0,6},{2,0},{4,2},{6,4},{1,7},{3,1},{5,3},{7,5},{8,14},{10,8},{12,... | collective-permute-start | bytes 811016 | tf_op jit(solution)/shard_map/ppermute | solution.py:42
  14.7 23.0 %collective-permute-start.1 = (bf16[528,256]{1,0:T(8,128)(2,1)S(1)}, bf16[528,256]{1,0:T(8,128)(2,1)S(1)}, u32[]{:S(2)}, u32[]{:S(2)}) collective-permute-start(bf16[528,256]{1,0:T(8,128)(2,1)S(1)} %concatenate.10.refs_0_.refs_4_.refs_8_), channel_id=1, source_target_pairs={{0,4},{2,6},{4,0},{6,2},{1,5},{3,7},{5,1},{7,3},{8,12},{10,14},{12... | collective-permute-start | bytes 811016 | tf_op jit(solution)/shard_map/ppermute | solution.py:42
  14.7 23.0 %collective-permute-start = (bf16[528,256]{1,0:T(8,128)(2,1)S(1)}, bf16[528,256]{1,0:T(8,128)(2,1)S(1)}, u32[]{:S(2)}, u32[]{:S(2)}) collective-permute-start(bf16[528,256]{1,0:T(8,128)(2,1)S(1)} %concatenate.10.refs_0_.refs_4_.refs_8_), channel_id=1, source_target_pairs={{0,2},{2,4},{4,6},{6,0},{1,3},{3,5},{5,7},{7,1},{8,10},{10,12},{12... | collective-permute-start | bytes 811016 | tf_op jit(solution)/shard_map/ppermute | solution.py:42
  15.7 26.8 %collective-permute-start.4 = (bf16[512,256]{1,0:T(8,128)(2,1)}, bf16[512,256]{1,0:T(8,128)(2,1)S(1)}, u32[]{:S(2)}, u32[]{:S(2)}) collective-permute-start(bf16[512,256]{1,0:T(8,128)(2,1)} %refs_14_.3), channel_id=1, source_target_pairs={{0,1},{1,0},{2,3},{3,2},{4,5},{5,4},{6,7},{7,6},{8,9},{9,8},{10,11... | collective-permute-start | bytes 786440 | tf_op jit(solution)/shard_map/ppermute | solution.py:42
  15.7 28.6 %collective-permute-start.3 = (bf16[512,512]{1,0:T(8,128)(2,1)}, bf16[512,512]{1,0:T(8,128)(2,1)S(1)}, u32[]{:S(2)}, u32[]{:S(2)}) collective-permute-start(bf16[512,512]{1,0:T(8,128)(2,1)} %refs_12_.3), channel_id=1, source_target_pairs={{0,1},{1,0},{2,3},{3,2},{4,5},{5,4},{6,7},{7,6},{8,9},{9,8},{10,11... | collective-permute-start | bytes 1572872 | tf_op jit(solution)/shard_map/ppermute | solution.py:42
  22.6 15.1 %copy-start.1 = (bf16[528,256]{1,0:T(8,128)(2,1)}, bf16[528,256]{1,0:T(8,128)(2,1)S(1)}, u32[]{:S(2)}) copy-start(bf16[528,256]{1,0:T(8,128)(2,1)S(1)} %collective-permute-done.2.refs_3_.refs_7_.refs_11_) | copy-start | bytes 811012
  22.6 21.6 %collective-permute-start.5 = (bf16[512,256]{1,0:T(8,128)(2,1)}, bf16[512,256]{1,0:T(8,128)(2,1)S(1)}, u32[]{:S(2)}, u32[]{:S(2)}) collective-permute-start(bf16[512,256]{1,0:T(8,128)(2,1)} %refs_16_.1), channel_id=1, source_target_pairs={{0,1},{1,0},{2,3},{3,2},{4,5},{5,4},{6,7},{7,6},{8,9},{9,8},{10,11... | collective-permute-start | bytes 786440 | tf_op jit(solution)/shard_map/ppermute | solution.py:42
  37.7 24.6 %collective-permute-start.10 = (bf16[512,512]{1,0:T(8,128)(2,1)}, bf16[512,512]{1,0:T(8,128)(2,1)S(1)}, u32[]{:S(2)}, u32[]{:S(2)}) collective-permute-start(bf16[512,512]{1,0:T(8,128)(2,1)} %refs_14_.2), channel_id=1, source_target_pairs={{0,1},{1,0},{2,3},{3,2},{4,5},{5,4},{6,7},{7,6},{8,9},{9,8},{10,11... | collective-permute-start | bytes 1572872 | tf_op jit(solution)/shard_map/ppermute | solution.py:42
  39.1 12.3 %collective-permute-start.9 = (bf16[512,256]{1,0:T(8,128)(2,1)}, bf16[512,256]{1,0:T(8,128)(2,1)S(1)}, u32[]{:S(2)}, u32[]{:S(2)}) collective-permute-start(bf16[512,256]{1,0:T(8,128)(2,1)} %shard_map.247), channel_id=1, source_target_pairs={{0,6},{2,0},{4,2},{6,4},{1,7},{3,1},{5,3},{7,5},{8,14},{10,8},{12,... | collective-permute-start | bytes 786440 | tf_op jit(solution)/shard_map/ppermute | solution.py:42
  42.5 11.4 %collective-permute-start.8 = (bf16[512,256]{1,0:T(8,128)(2,1)}, bf16[512,256]{1,0:T(8,128)(2,1)S(1)}, u32[]{:S(2)}, u32[]{:S(2)}) collective-permute-start(bf16[512,256]{1,0:T(8,128)(2,1)} %shard_map.247), channel_id=1, source_target_pairs={{0,2},{2,4},{4,6},{6,0},{1,3},{3,5},{5,7},{7,1},{8,10},{10,12},{12... | collective-permute-start | bytes 786440 | tf_op jit(solution)/shard_map/ppermute | solution.py:42
  50.8 19.1 %copy-start.5 = (bf16[768,512]{1,0:T(8,128)(2,1)S(1)}, bf16[768,512]{1,0:T(8,128)(2,1)}, u32[]{:S(2)}) copy-start(bf16[768,512]{1,0:T(8,128)(2,1)} %refs_0_.6) | copy-start | bytes 2359300
  50.8 40.3 %copy-start.8 = (bf16[512,256]{1,0:T(8,128)(2,1)S(1)}, bf16[512,256]{1,0:T(8,128)(2,1)}, u32[]{:S(2)}) copy-start(bf16[512,256]{1,0:T(8,128)(2,1)} %refs_4_.1) | copy-start | bytes 786436
  50.8 3.1 collective-permute-start.6
  50.9 3.0 collective-permute-start.7
  51.4 14.9 %collective-permute-start.11 = (bf16[512,256]{1,0:T(8,128)(2,1)S(1)}, bf16[512,256]{1,0:T(8,128)(2,1)S(1)}, u32[]{:S(2)}, u32[]{:S(2)}) collective-permute-start(bf16[512,256]{1,0:T(8,128)(2,1)S(1)} %copy-done.28), channel_id=1, source_target_pairs={{0,4},{2,6},{4,0},{6,2},{1,5},{3,7},{5,1},{7,3},{8,12},{10,14},{12... | collective-permute-start | bytes 786440 | tf_op jit(solution)/shard_map/ppermute | solution.py:42
  69.9 11.4 %collective-permute-start.12 = (bf16[512,256]{1,0:T(8,128)(2,1)}, bf16[512,256]{1,0:T(8,128)(2,1)S(1)}, u32[]{:S(2)}, u32[]{:S(2)}) collective-permute-start(bf16[512,256]{1,0:T(8,128)(2,1)} %get-tuple-element.84), channel_id=1, source_target_pairs={{0,2},{2,4},{4,6},{6,0},{1,3},{3,5},{5,7},{7,1},{8,10},{10,12},{12... | collective-permute-start | bytes 786440 | tf_op jit(solution)/shard_map/ppermute | solution.py:42
  70.0 30.8 %collective-permute-start.20 = (bf16[768,512]{1,0:T(8,128)(2,1)S(1)}, bf16[768,512]{1,0:T(8,128)(2,1)S(1)}, u32[]{:S(2)}, u32[]{:S(2)}) collective-permute-start(bf16[768,512]{1,0:T(8,128)(2,1)S(1)} %copy-done.5), channel_id=1, source_target_pairs={{0,1},{1,0},{2,3},{3,2},{4,5},{5,4},{6,7},{7,6},{8,9},{9,8},{10,11... | collective-permute-start | bytes 2359304 | tf_op jit(solution)/shard_map/ppermute | solution.py:42
  70.0 21.0 %collective-permute-start.13 = (bf16[512,256]{1,0:T(8,128)(2,1)}, bf16[512,256]{1,0:T(8,128)(2,1)S(1)}, u32[]{:S(2)}, u32[]{:S(2)}) collective-permute-start(bf16[512,256]{1,0:T(8,128)(2,1)} %get-tuple-element.85), channel_id=1, source_target_pairs={{0,4},{2,6},{4,0},{6,2},{1,5},{3,7},{5,1},{7,3},{8,12},{10,14},{12... | collective-permute-start | bytes 786440 | tf_op jit(solution)/shard_map/ppermute | solution.py:42
  72.6 18.4 %collective-permute-start.14 = (bf16[512,256]{1,0:T(8,128)(2,1)}, bf16[512,256]{1,0:T(8,128)(2,1)S(1)}, u32[]{:S(2)}, u32[]{:S(2)}) collective-permute-start(bf16[512,256]{1,0:T(8,128)(2,1)} %get-tuple-element.86), channel_id=1, source_target_pairs={{0,6},{2,0},{4,2},{6,4},{1,7},{3,1},{5,3},{7,5},{8,14},{10,8},{12,... | collective-permute-start | bytes 786440 | tf_op jit(solution)/shard_map/ppermute | solution.py:42
  73.8 32.2 %collective-permute-start.18 = (bf16[512,768]{1,0:T(8,128)(2,1)}, bf16[512,768]{1,0:T(8,128)(2,1)S(1)}, u32[]{:S(2)}, u32[]{:S(2)}) collective-permute-start(bf16[512,768]{1,0:T(8,128)(2,1)} %refs_8_.3), channel_id=1, source_target_pairs={{0,1},{1,0},{2,3},{3,2},{4,5},{5,4},{6,7},{7,6},{8,9},{9,8},{10,11... | collective-permute-start | bytes 2359304 | tf_op jit(solution)/shard_map/ppermute | solution.py:42
  81.3 24.7 %collective-permute-start.19 = (bf16[512,768]{1,0:T(8,128)(2,1)}, bf16[512,768]{1,0:T(8,128)(2,1)S(1)}, u32[]{:S(2)}, u32[]{:S(2)}) collective-permute-start(bf16[512,768]{1,0:T(8,128)(2,1)} %refs_10_.3), channel_id=1, source_target_pairs={{0,1},{1,0},{2,3},{3,2},{4,5},{5,4},{6,7},{7,6},{8,9},{9,8},{10,11... | collective-permute-start | bytes 2359304 | tf_op jit(solution)/shard_map/ppermute | solution.py:42
  93.1 30.7 %copy-start.7 = (bf16[512,256]{1,0:T(8,128)(2,1)}, bf16[512,256]{1,0:T(8,128)(2,1)S(1)}, u32[]{:S(2)}) copy-start(bf16[512,256]{1,0:T(8,128)(2,1)S(1)} %get-tuple-element.149.refs_0_) | copy-start | bytes 786436
  93.1 12.9 %collective-permute-start.17 = (bf16[512,256]{1,0:T(8,128)(2,1)S(1)}, bf16[512,256]{1,0:T(8,128)(2,1)S(1)}, u32[]{:S(2)}, u32[]{:S(2)}) collective-permute-start(bf16[512,256]{1,0:T(8,128)(2,1)S(1)} %get-tuple-element.149.refs_0_), channel_id=1, source_target_pairs={{0,6},{2,0},{4,2},{6,4},{1,7},{3,1},{5,3},{7,5},{8,14},{10,8},{12,... | collective-permute-start | bytes 786440 | tf_op jit(solution)/shard_map/ppermute | solution.py:42
  97.3 26.5 %collective-permute-start.16 = (bf16[512,256]{1,0:T(8,128)(2,1)S(1)}, bf16[512,256]{1,0:T(8,128)(2,1)S(1)}, u32[]{:S(2)}, u32[]{:S(2)}) collective-permute-start(bf16[512,256]{1,0:T(8,128)(2,1)S(1)} %get-tuple-element.149.refs_0_), channel_id=1, source_target_pairs={{0,4},{2,6},{4,0},{6,2},{1,5},{3,7},{5,1},{7,3},{8,12},{10,14},{12... | collective-permute-start | bytes 786440 | tf_op jit(solution)/shard_map/ppermute | solution.py:42
  100.7 23.1 %collective-permute-start.15 = (bf16[512,256]{1,0:T(8,128)(2,1)S(1)}, bf16[512,256]{1,0:T(8,128)(2,1)S(1)}, u32[]{:S(2)}, u32[]{:S(2)}) collective-permute-start(bf16[512,256]{1,0:T(8,128)(2,1)S(1)} %get-tuple-element.149.refs_0_), channel_id=1, source_target_pairs={{0,2},{2,4},{4,6},{6,0},{1,3},{3,5},{5,7},{7,1},{8,10},{10,12},{12... | collective-permute-start | bytes 786440 | tf_op jit(solution)/shard_map/ppermute | solution.py:42
  106.0 17.9 %copy-start.39 = (bf16[512,768]{1,0:T(8,128)(2,1)}, bf16[512,768]{1,0:T(8,128)(2,1)S(1)}, u32[]{:S(2)}) copy-start(bf16[512,768]{1,0:T(8,128)(2,1)S(1)} %collective-permute-done.18.refs_9_) | copy-start | bytes 2359300
  106.0 17.8 %copy-start.40 = (bf16[512,768]{1,0:T(8,128)(2,1)}, bf16[512,768]{1,0:T(8,128)(2,1)S(1)}, u32[]{:S(2)}) copy-start(bf16[512,768]{1,0:T(8,128)(2,1)S(1)} %collective-permute-done.19.refs_11_) | copy-start | bytes 2359300
  106.0 17.8 %copy-start.24 = (bf16[512,256]{1,0:T(8,128)(2,1)}, bf16[512,256]{1,0:T(8,128)(2,1)S(1)}, u32[]{:S(2)}) copy-start(bf16[512,256]{1,0:T(8,128)(2,1)S(1)} %collective-permute-done.17.refs_3_) | copy-start | bytes 786436
  132.9 11.6 %collective-permute-start.21 = (bf16[512,256]{1,0:T(8,128)(2,1)}, bf16[512,256]{1,0:T(8,128)(2,1)S(1)}, u32[]{:S(2)}, u32[]{:S(2)}) collective-permute-start(bf16[512,256]{1,0:T(8,128)(2,1)} %get-tuple-element.96), channel_id=1, source_target_pairs={{0,2},{2,4},{4,6},{6,0},{1,3},{3,5},{5,7},{7,1},{8,10},{10,12},{12... | collective-permute-start | bytes 786440 | tf_op jit(solution)/shard_map/ppermute | solution.py:42
  133.2 20.9 %collective-permute-start.22 = (bf16[512,256]{1,0:T(8,128)(2,1)}, bf16[512,256]{1,0:T(8,128)(2,1)S(1)}, u32[]{:S(2)}, u32[]{:S(2)}) collective-permute-start(bf16[512,256]{1,0:T(8,128)(2,1)} %get-tuple-element.97), channel_id=1, source_target_pairs={{0,4},{2,6},{4,0},{6,2},{1,5},{3,7},{5,1},{7,3},{8,12},{10,14},{12... | collective-permute-start | bytes 786440 | tf_op jit(solution)/shard_map/ppermute | solution.py:42
  133.2 20.8 %collective-permute-start.23 = (bf16[512,256]{1,0:T(8,128)(2,1)}, bf16[512,256]{1,0:T(8,128)(2,1)S(1)}, u32[]{:S(2)}, u32[]{:S(2)}) collective-permute-start(bf16[512,256]{1,0:T(8,128)(2,1)} %get-tuple-element.98), channel_id=1, source_target_pairs={{0,6},{2,0},{4,2},{6,4},{1,7},{3,1},{5,3},{7,5},{8,14},{10,8},{12,... | collective-permute-start | bytes 786440 | tf_op jit(solution)/shard_map/ppermute | solution.py:42
  154.8 8.9 %collective-permute-start.24 = (bf16[4,128,2304]{2,1,0:T(8,128)(2,1)}, bf16[4,128,2304]{2,1,0:T(8,128)(2,1)S(1)}, u32[]{:S(2)}, u32[]{:S(2)}) collective-permute-start(bf16[4,128,2304]{2,1,0:T(8,128)(2,1)} %shard_map.253), channel_id=1, source_target_pairs={{0,1},{1,0},{2,3},{3,2},{4,5},{5,4},{6,7},{7,6},{8,9},{9,8},{10,11... | collective-permute-start | bytes 7077896 | tf_op jit(solution)/shard_map/ppermute | solution.py:42
  157.1 14.6 %collective-permute-start.27 = (bf16[512,256]{1,0:T(8,128)(2,1)}, bf16[512,256]{1,0:T(8,128)(2,1)S(1)}, u32[]{:S(2)}, u32[]{:S(2)}) collective-permute-start(bf16[512,256]{1,0:T(8,128)(2,1)} %shard_map.255.refs_4_), channel_id=1, source_target_pairs={{0,6},{2,0},{4,2},{6,4},{1,7},{3,1},{5,3},{7,5},{8,14},{10,8},{12,... | collective-permute-start | bytes 786440 | tf_op jit(solution)/shard_map/ppermute | solution.py:42
  161.5 25.9 %collective-permute-start.26 = (bf16[512,256]{1,0:T(8,128)(2,1)}, bf16[512,256]{1,0:T(8,128)(2,1)S(1)}, u32[]{:S(2)}, u32[]{:S(2)}) collective-permute-start(bf16[512,256]{1,0:T(8,128)(2,1)} %shard_map.255.refs_4_), channel_id=1, source_target_pairs={{0,4},{2,6},{4,0},{6,2},{1,5},{3,7},{5,1},{7,3},{8,12},{10,14},{12... | collective-permute-start | bytes 786440 | tf_op jit(solution)/shard_map/ppermute | solution.py:42
  163.7 23.8 %collective-permute-start.25 = (bf16[512,256]{1,0:T(8,128)(2,1)}, bf16[512,256]{1,0:T(8,128)(2,1)S(1)}, u32[]{:S(2)}, u32[]{:S(2)}) collective-permute-start(bf16[512,256]{1,0:T(8,128)(2,1)} %shard_map.255.refs_4_), channel_id=1, source_target_pairs={{0,2},{2,4},{4,6},{6,0},{1,3},{3,5},{5,7},{7,1},{8,10},{10,12},{12... | collective-permute-start | bytes 786440 | tf_op jit(solution)/shard_map/ppermute | solution.py:42
  171.7 15.7 %copy-start.12 = (bf16[512,256]{1,0:T(8,128)(2,1)}, bf16[512,256]{1,0:T(8,128)(2,1)S(1)}, u32[]{:S(2)}) copy-start(bf16[512,256]{1,0:T(8,128)(2,1)S(1)} %collective-permute-done.27.refs_5_.refs_7_.refs_3_) | copy-start | bytes 786436
  188.2 109.4 %all-gather.2.cloned.1.call-start = ((), (), s32[]{:S(2)}) async-start(), calls=%async_computation.2 | async-start | bytes 2949120 | tf_op jit(solution)/shard_map/all_gather | solution.py:946
  188.3 13.5 %collective-permute-start.28 = (bf16[512,256]{1,0:T(8,128)(2,1)}, bf16[512,256]{1,0:T(8,128)(2,1)S(1)}, u32[]{:S(2)}, u32[]{:S(2)}) collective-permute-start(bf16[512,256]{1,0:T(8,128)(2,1)} %get-tuple-element.104), channel_id=1, source_target_pairs={{0,2},{2,4},{4,6},{6,0},{1,3},{3,5},{5,7},{7,1},{8,10},{10,12},{12... | collective-permute-start | bytes 786440 | tf_op jit(solution)/shard_map/ppermute | solution.py:42
  188.4 13.8 %collective-permute-start.30 = (bf16[512,256]{1,0:T(8,128)(2,1)}, bf16[512,256]{1,0:T(8,128)(2,1)S(1)}, u32[]{:S(2)}, u32[]{:S(2)}) collective-permute-start(bf16[512,256]{1,0:T(8,128)(2,1)} %get-tuple-element.106), channel_id=1, source_target_pairs={{0,6},{2,0},{4,2},{6,4},{1,7},{3,1},{5,3},{7,5},{8,14},{10,8},{12,... | collective-permute-start | bytes 786440 | tf_op jit(solution)/shard_map/ppermute | solution.py:42
  201.7 12.9 %collective-permute-start.29 = (bf16[512,256]{1,0:T(8,128)(2,1)S(1)}, bf16[512,256]{1,0:T(8,128)(2,1)S(1)}, u32[]{:S(2)}, u32[]{:S(2)}) collective-permute-start(bf16[512,256]{1,0:T(8,128)(2,1)S(1)} %copy-done.50), channel_id=1, source_target_pairs={{0,4},{2,6},{4,0},{6,2},{1,5},{3,7},{5,1},{7,3},{8,12},{10,14},{12... | collective-permute-start | bytes 786440 | tf_op jit(solution)/shard_map/ppermute | solution.py:42
  211.0 3.6 %collective-permute-start.31 = (bf16[512,256]{1,0:T(8,128)(2,1)}, bf16[512,256]{1,0:T(8,128)(2,1)S(1)}, u32[]{:S(2)}, u32[]{:S(2)}) collective-permute-start(bf16[512,256]{1,0:T(8,128)(2,1)} %get-tuple-element.118), channel_id=1, source_target_pairs={{0,1},{1,0},{2,3},{3,2},{4,5},{5,4},{6,7},{7,6},{8,9},{9,8},{10,11... | collective-permute-start | bytes 786440 | tf_op jit(solution)/shard_map/ppermute | solution.py:42
  211.0 3.5 %collective-permute-start.32 = (bf16[512,256]{1,0:T(8,128)(2,1)}, bf16[512,256]{1,0:T(8,128)(2,1)S(1)}, u32[]{:S(2)}, u32[]{:S(2)}) collective-permute-start(bf16[512,256]{1,0:T(8,128)(2,1)} %get-tuple-element.120), channel_id=1, source_target_pairs={{0,1},{1,0},{2,3},{3,2},{4,5},{5,4},{6,7},{7,6},{8,9},{9,8},{10,11... | collective-permute-start | bytes 786440 | tf_op jit(solution)/shard_map/ppermute | solution.py:42
  223.6 3.6 %collective-permute-start.36 = (bf16[4,128,1024]{2,1,0:T(8,128)(2,1)}, bf16[4,128,1024]{2,1,0:T(8,128)(2,1)S(1)}, u32[]{:S(2)}, u32[]{:S(2)}) collective-permute-start(bf16[4,128,1024]{2,1,0:T(8,128)(2,1)} %get-tuple-element.129), channel_id=1, source_target_pairs={{0,1},{1,0},{2,3},{3,2},{4,5},{5,4},{6,7},{7,6},{8,9},{9,8},{10,11... | collective-permute-start | bytes 3145736 | tf_op jit(solution)/shard_map/ppermute | solution.py:42
  223.7 3.4 %collective-permute-start.37 = (bf16[4,128,512]{2,1,0:T(8,128)(2,1)S(1)}, bf16[4,128,512]{2,1,0:T(8,128)(2,1)S(1)}, u32[]{:S(2)}, u32[]{:S(2)}) collective-permute-start(bf16[4,128,512]{2,1,0:T(8,128)(2,1)S(1)} %copy-done.51), channel_id=1, source_target_pairs={{0,1},{1,0},{2,3},{3,2},{4,5},{5,4},{6,7},{7,6},{8,9},{9,8},{10,11... | collective-permute-start | bytes 1572872 | tf_op jit(solution)/shard_map/ppermute | solution.py:42
  231.6 28.0 %copy-start.4 = (f32[512,256]{1,0:T(8,128)S(1)}, f32[512,256]{1,0:T(8,128)}, u32[]{:S(2)}) copy-start(f32[512,256]{1,0:T(8,128)} %get-tuple-element.150.refs_6_) | copy-start | bytes 1572868
  231.6 28.0 %copy-start.32 = (bf16[512,256]{1,0:T(8,128)(2,1)S(1)}, bf16[512,256]{1,0:T(8,128)(2,1)}, u32[]{:S(2)}) copy-start(bf16[512,256]{1,0:T(8,128)(2,1)} %copy-done.31) | copy-start | bytes 786436
  231.7 28.0 %copy-start.34 = (bf16[512,256]{1,0:T(8,128)(2,1)S(1)}, bf16[512,256]{1,0:T(8,128)(2,1)}, u32[]{:S(2)}) copy-start(bf16[512,256]{1,0:T(8,128)(2,1)} %copy-done.33) | copy-start | bytes 786436
  231.7 28.0 %copy-start.36 = (bf16[512,256]{1,0:T(8,128)(2,1)S(1)}, bf16[512,256]{1,0:T(8,128)(2,1)}, u32[]{:S(2)}) copy-start(bf16[512,256]{1,0:T(8,128)(2,1)} %copy-done.35) | copy-start | bytes 786436
  231.7 28.0 %copy-start.41 = (f32[512,256]{1,0:T(8,128)S(1)}, f32[512,256]{1,0:T(8,128)}, u32[]{:S(2)}) copy-start(f32[512,256]{1,0:T(8,128)} %get-tuple-element.99) | copy-start | bytes 1572868
  231.7 23.6 %collective-permute-start.38 = (bf16[128,1536]{1,0:T(8,128)(2,1)}, bf16[128,1536]{1,0:T(8,128)(2,1)S(1)}, u32[]{:S(2)}, u32[]{:S(2)}) collective-permute-start(bf16[128,1536]{1,0:T(8,128)(2,1)} %get-tuple-element.131.refs_1_), channel_id=1, source_target_pairs={{0,8},{8,0},{16,24},{24,16},{1,9},{9,1},{17,25},{25,17},{2,10},{10... | collective-permute-start | bytes 1179656 | tf_op jit(solution)/shard_map/ppermute | solution.py:75
  233.3 11.5 %collective-permute-start.33 = (bf16[528,256]{1,0:T(8,128)(2,1)}, bf16[528,256]{1,0:T(8,128)(2,1)S(1)}, u32[]{:S(2)}, u32[]{:S(2)}) collective-permute-start(bf16[528,256]{1,0:T(8,128)(2,1)} %get-tuple-element.123), channel_id=1, source_target_pairs={{0,2},{2,4},{4,6},{6,0},{1,3},{3,5},{5,7},{7,1},{8,10},{10,12},{12... | collective-permute-start | bytes 811016 | tf_op jit(solution)/shard_map/ppermute | solution.py:42
  233.5 21.9 %collective-permute-start.34 = (bf16[528,256]{1,0:T(8,128)(2,1)}, bf16[528,256]{1,0:T(8,128)(2,1)S(1)}, u32[]{:S(2)}, u32[]{:S(2)}) collective-permute-start(bf16[528,256]{1,0:T(8,128)(2,1)} %get-tuple-element.124), channel_id=1, source_target_pairs={{0,4},{2,6},{4,0},{6,2},{1,5},{3,7},{5,1},{7,3},{8,12},{10,14},{12... | collective-permute-start | bytes 811016 | tf_op jit(solution)/shard_map/ppermute | solution.py:42
  235.4 19.9 %collective-permute-start.35 = (bf16[528,256]{1,0:T(8,128)(2,1)}, bf16[528,256]{1,0:T(8,128)(2,1)}, u32[]{:S(2)}, u32[]{:S(2)}) collective-permute-start(bf16[528,256]{1,0:T(8,128)(2,1)} %get-tuple-element.125), channel_id=1, source_target_pairs={{0,6},{2,0},{4,2},{6,4},{1,7},{3,1},{5,3},{7,5},{8,14},{10,8},{12,... | collective-permute-start | bytes 811016 | tf_op jit(solution)/shard_map/ppermute | solution.py:42
  238.1 27.1 %collective-permute-start.43 = (bf16[128,1536]{1,0:T(8,128)(2,1)}, bf16[128,1536]{1,0:T(8,128)(2,1)S(1)}, u32[]{:S(2)}, u32[]{:S(2)}) collective-permute-start(bf16[128,1536]{1,0:T(8,128)(2,1)} %get-tuple-element.135), channel_id=1, source_target_pairs={{0,16},{8,24},{16,0},{24,8},{1,17},{9,25},{17,1},{25,9},{2,18},{10... | collective-permute-start | bytes 1179656 | tf_op jit(solution)/shard_map/ppermute | solution.py:75
  244.8 20.5 %collective-permute-start.44 = (bf16[128,1536]{1,0:T(8,128)(2,1)}, bf16[128,1536]{1,0:T(8,128)(2,1)}, u32[]{:S(2)}, u32[]{:S(2)}) collective-permute-start(bf16[128,1536]{1,0:T(8,128)(2,1)} %get-tuple-element.136), channel_id=1, source_target_pairs={{0,24},{8,16},{16,8},{24,0},{1,25},{9,17},{17,9},{25,1},{2,26},{10... | collective-permute-start | bytes 1179656 | tf_op jit(solution)/shard_map/ppermute | solution.py:75
  259.6 1.4 collective-permute-start.39
  261.7 8.7 %collective-permute-start.42 = (f32[8,256]{1,0:T(8,128)S(1)}, f32[8,256]{1,0:T(8,128)S(1)}, u32[]{:S(2)}, u32[]{:S(2)}) collective-permute-start(f32[8,256]{1,0:T(8,128)S(1)} %add.188), channel_id=1, source_target_pairs={{0,24},{8,0},{16,8},{24,16},{1,25},{9,1},{17,9},{25,17},{2,26},{10... | collective-permute-start | bytes 24584 | tf_op jit(solution)/shard_map/ppermute | solution.py:42
  263.2 7.8 %collective-permute-start.41 = (f32[8,256]{1,0:T(8,128)S(1)}, f32[8,256]{1,0:T(8,128)S(1)}, u32[]{:S(2)}, u32[]{:S(2)}) collective-permute-start(f32[8,256]{1,0:T(8,128)S(1)} %add.188), channel_id=1, source_target_pairs={{0,16},{8,24},{16,0},{24,8},{1,17},{9,25},{17,1},{25,9},{2,18},{10... | collective-permute-start | bytes 24584 | tf_op jit(solution)/shard_map/ppermute | solution.py:42
  263.7 7.3 %collective-permute-start.40 = (f32[8,256]{1,0:T(8,128)S(1)}, f32[8,256]{1,0:T(8,128)S(1)}, u32[]{:S(2)}, u32[]{:S(2)}) collective-permute-start(f32[8,256]{1,0:T(8,128)S(1)} %add.188), channel_id=1, source_target_pairs={{0,8},{8,16},{16,24},{24,0},{1,9},{9,17},{17,25},{25,1},{2,10},{10... | collective-permute-start | bytes 24584 | tf_op jit(solution)/shard_map/ppermute | solution.py:42
  267.5 34.4 %collective-permute-start.47 = (bf16[128,1536]{1,0:T(8,128)(2,1)S(1)}, bf16[128,1536]{1,0:T(8,128)(2,1)S(1)}, u32[]{:S(2)}, u32[]{:S(2)}) collective-permute-start(bf16[128,1536]{1,0:T(8,128)(2,1)S(1)} %get-tuple-element.145), channel_id=1, source_target_pairs={{0,24},{8,16},{16,8},{24,0},{1,25},{9,17},{17,9},{25,1},{2,26},{10... | collective-permute-start | bytes 1179656 | tf_op jit(solution)/shard_map/ppermute | solution.py:75
  268.8 33.2 %collective-permute-start.46 = (bf16[128,1536]{1,0:T(8,128)(2,1)S(1)}, bf16[128,1536]{1,0:T(8,128)(2,1)S(1)}, u32[]{:S(2)}, u32[]{:S(2)}) collective-permute-start(bf16[128,1536]{1,0:T(8,128)(2,1)S(1)} %get-tuple-element.145), channel_id=1, source_target_pairs={{0,16},{8,24},{16,0},{24,8},{1,17},{9,25},{17,1},{25,9},{2,18},{10... | collective-permute-start | bytes 1179656 | tf_op jit(solution)/shard_map/ppermute | solution.py:75
  270.4 31.5 %collective-permute-start.45 = (bf16[128,1536]{1,0:T(8,128)(2,1)S(1)}, bf16[128,1536]{1,0:T(8,128)(2,1)S(1)}, u32[]{:S(2)}, u32[]{:S(2)}) collective-permute-start(bf16[128,1536]{1,0:T(8,128)(2,1)S(1)} %get-tuple-element.145), channel_id=1, source_target_pairs={{0,8},{8,0},{16,24},{24,16},{1,9},{9,1},{17,25},{25,17},{2,10},{10... | collective-permute-start | bytes 1179656 | tf_op jit(solution)/shard_map/ppermute | solution.py:75
  (38 other events, 84.8 us)
Sparse Core Ops, SparseCore 0:
  188.4 35.7 reduce-scatter.1
  231.8 65.8 all-gather.1

commit v3 on v2

--- a/solution.py
+++ b/solution.py
@@ -130,13 +130,33 @@
         normed_ref[:, span(offset_ref[s], width)] = (blocks[s] * scale * gain).astype(BF)
 
 
+def prepare_kernel(seq_ref, pos_ref, rate_ref, row_ref, col_ref, cos_ref, sin_ref):
+    rows, head = cos_ref.shape
+    here = lax.axis_index("gy")
+    lines = []
+    for peer in (here, 1 - here):
+        at = span(peer * rows, rows)
+        lines += [seq_ref[:, at].astype(F32), pos_ref[:, at].astype(F32)]
+    row_ref[...] = jnp.concatenate(lines[:2] + [jnp.zeros((6, rows), F32)], axis=0)
+    col_ref[...] = jnp.concatenate(lines + [jnp.zeros((4, rows), F32)], axis=0)
+    place = jnp.transpose(col_ref[...])[:, 1:2]
+    phase = place * rate_ref[...]
+    lane = lax.broadcasted_iota(jnp.int32, (rows, head), 1)
+    cos_ref[...] = jnp.cos(phase)
+    sine = jnp.sin(phase)
+    sin_ref[...] = jnp.where(lane < head // 2, -sine, sine)
+
+
 def cot_kernel(count, offset_ref, *refs):
-    pieces, normed_ref, downs = refs[:count], refs[count], refs[count + 1 : -3]
-    whole_ref, grad_ref, turned_ref = refs[-3:]
+    pieces, normed_ref, downs = refs[:count], refs[count], refs[count + 1 : -5]
+    whole_ref, grad_ref, turned_ref, cot_turned_ref, cot_sent_ref = refs[-5:]
     turned_ref[...] = jnp.transpose(normed_ref[...])
     width = pieces[0].shape[1]
     for s in range(count):
         whole_ref[:, span(offset_ref[s], width)] = pieces[s][...]
+    half = whole_ref.shape[1] // 2
+    cot_turned_ref[...] = jnp.transpose(whole_ref[:, :half])
+    cot_sent_ref[...] = jnp.transpose(whole_ref[:, half:])
     grad_ref[...] = wide_dot(whole_ref, downs, dot_cols, 1)
 
 
@@ -246,14 +266,17 @@
     pieces, gains, refs = refs[:count], refs[count : 2 * count], refs[2 * count :]
     wg, wu, grad_ref = refs[:parts_in], refs[parts_in : 2 * parts_in], refs[2 * parts_in]
     outs = refs[-count - 5 :]
-    parts, (normed_ref, scale_ref, product_ref, gate_ref, up_ref) = outs[:count], outs[count:]
-    width = pieces[0].shape[1]
+    parts, (normed_ref, scale_ref, product_ref, delta_ref, sent_ref) = outs[:count], outs[count:]
+    width, units = pieces[0].shape[1], product_ref.shape[1]
+    gate_ref, up_ref = delta_ref.at[:, :units], delta_ref.at[:, units : 2 * units]
     normalise(pieces, gains, 1, offset_ref, normed_ref, scale_ref)
+    sent_ref[...] = normed_ref[:, normed_ref.shape[1] // 2 :]
     gate = wide_dot(normed_ref, wg, dot, 0)
     up = wide_dot(normed_ref, wu, dot, 0)
     sig = 1.0 / (1.0 + jnp.exp(-gate))
     silu = gate * sig
     product_ref[...] = (silu * up).astype(BF)
+    delta_ref[:, 2 * units :] = product_ref[...]
     grad = grad_ref[...]
     gate_ref[...] = (grad * up * (sig + silu * (1.0 - sig))).astype(BF)
     up_ref[...] = (grad * silu).astype(BF)
@@ -273,29 +296,42 @@
         parts[s][...] = dot(left_ref[...], weight).astype(parts[s].dtype)
 
 
-def weight_grad_kernel(turned, *refs):
+def ffn_share_kernel(own_ref, got_ref, cot_ref, cot_got_ref, delta_ref, delta_got_ref, share_ref):
+    units = share_ref.shape[1] // 3
+    left = jnp.transpose(own_ref[...]), jnp.transpose(got_ref[...])
+    back = cot_ref[...], cot_got_ref[...]
+    for i, pair in enumerate((left, left, back)):
+        at = slice(i * units, (i + 1) * units)
+        value = dot(pair[0], delta_ref[:, at]) + dot(pair[1], delta_got_ref[:, at])
+        share_ref[:, at] = value.astype(BF)
+
+
+def weight_grad_kernel(groups, *refs):
     own_ref, other_ref = refs[-2:]
     size = own_ref.shape[1]
     start = 0
-    for i, across in enumerate(turned):
-        own, other, right = refs[3 * i : 3 * i + 3]
-        width = right.shape[1]
-        both = jnp.concatenate([own[...], other[...]], axis=0 if across else 1)
-        both = (dot if across else dot_rows)(both, right[...])
-        own_ref[0, :, start : start + width] = both[:size].astype(BF)
-        other_ref[0, :, start : start + width] = both[size:].astype(BF)
-        start += width
+    for across, rights in groups:
+        own, other, refs = refs[0], refs[1], refs[2:]
+        left = jnp.concatenate([own[...], other[...]], axis=0 if across else 1)
+        if not across:
+            left = jnp.transpose(left)
+        for right in refs[:rights]:
+            width = right.shape[1]
+            both = dot(left, right[...]).astype(BF)
+            own_ref[0, :, start : start + width] = both[:size]
+            other_ref[0, :, start : start + width] = both[size:]
+            start += width
+        refs = refs[rights:]
 
 
 def final_kernel(count, *refs):
     parts = refs[:count]
-    (tok_ref, cot_ref, hid_ref, two_ref, one_scale, two_scale, two_inner, gain_ref) = refs[
-        count : count + 8
-    ]
+    (tok_ref, cot_ref, hid_ref, two_ref, one_scale, two_scale, two_inner) = refs[count : count + 7]
     grad_ref, part_ref = refs[-2:]
-    rows, width = tok_ref.shape
+    rows, width = hid_ref.shape
     size = width * count
-    gain_one, gain_two = gain_ref[0:1, :].astype(F32), gain_ref[1:2, :].astype(F32)
+    gains = tok_ref[rows : rows + 16, :].astype(F32)
+    gain_one, gain_two = gains[0:1, :], gains[1:2, :]
     sums = [jnp.zeros((1, width), F32)] * 2
     small = sum(p[rows : rows + 16, :].astype(F32) for p in parts)
     count_rows = rows // width
@@ -333,6 +369,45 @@
             stop = start + own.shape[2]
             ref[:, start:stop] = (own[c].astype(F32) + got[c].astype(F32)).astype(ref.dtype)
             start = stop
+
+
+def halving_kernel(shares, chunk_ref, *refs):
+    owns, gots = refs[:shares], refs[shares : 2 * shares]
+    outs = refs[-4:]
+    half = outs[0].shape[2]
+    start = 0
+    for own, got in zip(owns, gots):
+        stop = start + own.shape[2]
+        for side, (keep, send) in enumerate((outs[:2], outs[2:])):
+            low, high = max(start, side * half), min(stop, (side + 1) * half)
+            if low >= high:
+                continue
+            cut, at = slice(low - start, high - start), slice(low - side * half, high - side * half)
+            for ref, pair in ((keep, (0, 2 - side)), (send, (1 + side, 3))):
+                for k, which in enumerate(pair):
+                    c = chunk_ref[which]
+                    ref[k, :, at] = (
+                        own[c, :, cut].astype(F32) + got[c, :, cut].astype(F32)
+                    ).astype(ref.dtype)
+        start = stop
+
+
+def halving_add_kernel(keep_a, got_a, keep_b, got_b, mine_a, send_a, mine_b, send_b):
+    for keep, got, mine, send in (
+        (keep_a, got_a, mine_a, send_a),
+        (keep_b, got_b, mine_b, send_b),
+    ):
+        mine[...] = keep[0] + got[0].astype(F32)
+        send[...] = (keep[1] + got[1].astype(F32)).astype(BF)
+
+
+def halving_total_kernel(mine_a, got_a, mine_b, got_b, *refs):
+    total_ref, low_ref = refs[-2:]
+    half = mine_a.shape[1]
+    for start, mine, got in ((0, mine_a, got_a), (half, mine_b, got_b)):
+        value = mine[...] + got[...].astype(F32)
+        total_ref[:, start : start + half] = value
+        low_ref[:, start : start + half] = value.astype(BF)
 
 
 def result_share_kernel(count, parts_in, offset_ref, left_ref, *refs):
@@ -547,25 +622,16 @@
     return pl.BlockSpec(shape, lambda i: (0,) * len(shape))
 
 
-def call(kernel, grid, in_specs, out_specs, out_shape, scratch=(), deps=(), prefetch=0):
+def call(kernel, grid, in_specs, out_specs, out_shape, scratch=(), deps=(), aliases=None):
     deps = list(deps)
     in_specs = in_specs + [ANY] * len(deps)
     extra = dict(
         in_specs=in_specs, out_specs=out_specs, scratch_shapes=scratch, **(dict(grid=grid) if grid else {})
     )
-    if prefetch:
-        extra = dict(
-            grid_spec=pltpu.PrefetchScalarGridSpec(
-                num_scalar_prefetch=prefetch,
-                grid=grid,
-                in_specs=in_specs,
-                out_specs=out_specs,
-                scratch_shapes=scratch,
-            )
-        )
     run = pl.pallas_call(
         kernel,
         out_shape=out_shape,
+        input_output_aliases=aliases or {},
         compiler_params=pltpu.CompilerParams(vmem_limit_bytes=60 * 2**20),
         cost_estimate=pl.CostEstimate(flops=2**20, bytes_accessed=2**16, transcendentals=0),
         **extra,
@@ -573,20 +639,24 @@
     return lambda *args: run(*args, *deps)
 
 
-def weight_grads(pairs, deps=(), late=()):
+def weight_grads(groups):
     peers, blocks = lax.axis_size("gy"), lax.axis_size("dev")
-    rows = pairs[0][1].shape[0]
-    turned = [left.shape[1] == rows for left, _ in pairs]
-    width = pairs[0][0].size // rows
+    rows = groups[0][1][0].shape[0]
+    turned = [left.shape[1] == rows for left, _ in groups]
+    width = groups[0][0].size // rows
     size = width // peers // blocks
-    total = sum(right.shape[1] for _, right in pairs)
+    total = sum(right.shape[1] for _, rights in groups for right in rights)
     if peers != 2:
-        share = [(dot if t else dot_rows)(a, b) for t, (a, b) in zip(turned, pairs)]
+        share = [
+            (dot if t else dot_rows)(left, right)
+            for t, (left, rights) in zip(turned, groups)
+            for right in rights
+        ]
         share = jnp.concatenate(share, axis=1).astype(BF)
         share = lax.psum_scatter(share, "gy", scatter_dimension=0, tiled=True)
         return share.reshape(blocks, size, total), None
     specs, operands = [], []
-    for across, (left, right) in zip(turned, pairs):
+    for across, (left, rights) in zip(turned, groups):
         if across:
             specs += [
                 pl.BlockSpec((size, rows), lambda c: (c, 0)),
@@ -597,18 +667,18 @@
                 pl.BlockSpec((rows, size), lambda c: (0, c)),
                 pl.BlockSpec((rows, size), lambda c: (0, blocks + c)),
             ]
-        specs.append(pl.BlockSpec(right.shape, lambda c: (0, 0)))
-        operands += [left, left, right]
+        specs += [pl.BlockSpec(right.shape, lambda c: (0, 0)) for right in rights]
+        operands += [left, left, *rights]
     chunk = pl.BlockSpec((1, size, total), lambda c: (c, 0, 0))
     own, other = call(
-        functools.partial(weight_grad_kernel, turned),
+        functools.partial(
+            weight_grad_kernel, [(t, len(rights)) for t, (_, rights) in zip(turned, groups)]
+        ),
         (blocks,),
         specs,
         [chunk, chunk],
         [out((blocks, size, total), BF), out((blocks, size, total), BF)],
-        deps=deps,
     )(*operands)
-    (other,) = after([other], *late)
     return own, shifted(other, "gy", 1)
 
 
@@ -636,6 +706,36 @@
     for part in got:
         total = total + part.astype(F32)
     return total, got
+
+
+def halving_total(shares, before, deps):
+    blocks, size, _ = shares[0][0].shape
+    half = sum(own.shape[2] for own, _ in shares) // 2
+    chunks = (lax.axis_index("dev") ^ jnp.arange(4)).astype(jnp.int32)
+    pair = [out((2, size, half), F32), out((2, size, half), BF)]
+    keep_a, send_a, keep_b, send_b = call(
+        functools.partial(halving_kernel, len(shares)),
+        None,
+        [SMEM] + [VMEM] * (2 * len(shares)),
+        [VMEM] * 4,
+        pair * 2,
+        deps=before,
+    )(chunks, *[own for own, _ in shares], *[got for _, got in shares])
+    got_a, got_b = dev_send(send_a, 1), dev_send(send_b, 2)
+    one = [out((size, half), F32), out((size, half), BF)]
+    mine_a, next_a, mine_b, next_b = call(
+        halving_add_kernel, None, [VMEM] * 4, [VMEM] * 4, one * 2
+    )(keep_a, got_a, keep_b, got_b)
+    last_a, last_b = dev_send(next_a, 2), dev_send(next_b, 1)
+    total = call(
+        halving_total_kernel,
+        None,
+        [VMEM] * 4,
+        [VMEM] * 2,
+        [out((size, 2 * half), F32), out((size, 2 * half), BF)],
+        deps=deps,
+    )(mine_a, last_a, mine_b, last_b)
+    return total, [last_a, last_b]
 
 
 def dev_all(total, deps=()):
@@ -711,7 +811,9 @@
         + [lies_at((gx + s) % count) for s in range(count)]
     ).astype(jnp.int32)
 
-    below = jnp.stack([norm_gain, ffn_gain] + [norm_gain] * 14)
+    below = jnp.concatenate(
+        [norm_gain[None], ffn_gain[None], jnp.zeros((14, piece), tokens.dtype)], axis=0
+    )
     token_pieces = pieces_of(jnp.concatenate([tokens, below], axis=0))
     gain_block = pl.BlockSpec((16, piece), lambda i: (rows // 16, 0))
     query_parts, key_w_parts, value_w_parts = (
@@ -721,29 +823,27 @@
     gate_parts, up_parts = gather_width(w_gate, 0), gather_width(w_up, 0)
     halves = len(gate_parts)
 
-    all_seq, all_pos = sequence.reshape(peers, rows), position.reshape(peers, rows)
+    lane = jnp.arange(head)
+    rates = (THETA ** (-((lane % (head // 2)).astype(F32) * 2.0) / head))[None, :]
     if peers == 2:
-        order = lambda a: jnp.where(gy == 0, a, a[::-1])
-        all_seq, all_pos = order(all_seq), order(all_pos)
-        own_seq, own_pos = all_seq[0], all_pos[0]
+        row_info, col_info, cosine, sine = call(
+            prepare_kernel,
+            None,
+            [VMEM] * 3,
+            [VMEM] * 4,
+            [out((8, rows), F32), out((8, rows), F32), out((rows, head), F32), out((rows, head), F32)],
+        )(sequence[None], position[None], rates)
     else:
+        all_seq, all_pos = sequence.reshape(peers, rows), position.reshape(peers, rows)
         own_seq = lax.dynamic_index_in_dim(all_seq, gy, 0, False)
         own_pos = lax.dynamic_index_in_dim(all_pos, gy, 0, False)
-    row_info = jnp.concatenate(
-        [own_seq[None], own_pos[None], jnp.zeros((6, rows), jnp.int32)], axis=0
-    ).astype(F32)
-    if peers == 2:
-        col_info = jnp.concatenate(
-            [all_seq[:1], all_pos[:1], all_seq[1:], all_pos[1:], jnp.zeros((4, rows), jnp.int32)],
-            axis=0,
+        row_info = jnp.concatenate(
+            [own_seq[None], own_pos[None], jnp.zeros((6, rows), jnp.int32)], axis=0
         ).astype(F32)
-    else:
         col_info = jnp.stack([all_seq, all_pos], axis=-1).astype(F32)
-    lane = jnp.arange(head)
-    rates = THETA ** (-((lane % (head // 2)).astype(F32) * 2.0) / head)
-    phase = own_pos.astype(F32)[:, None] * rates[None, :]
-    cosine = jnp.cos(phase)
-    sine = jnp.sin(phase) * jnp.where(lane < head // 2, -1.0, 1.0)[None, :]
+        phase = own_pos.astype(F32)[:, None] * rates
+        cosine = jnp.cos(phase)
+        sine = jnp.sin(phase) * jnp.where(lane < head // 2, -1.0, 1.0)[None, :]
     q_scale = query_gain.astype(F32)[None]
     k_scale = key_gain.astype(F32)[None]
 
@@ -788,7 +888,7 @@
     else:
         keys = [lax.all_gather(key_bf, "gy", axis=0)]
         values = [lax.all_gather(value_bf, "gy", axis=0)]
-    (late_cotangent,) = after([cotangent], *token_pieces[1:])
+    (late_cotangent,) = after([cotangent], *token_pieces[1:], cosine, offsets)
     cot_pieces = [cotangent] + pieces_of(late_cotangent)[1:]
 
     mixed, attended, logs = call(
@@ -820,7 +920,7 @@
     inputs = tokens.astype(F32)
     hidden = inputs + piece_sum(out_parts[0], out_parts[1:])
 
-    cot_whole, grad_product, normed_turned = call(
+    cot_whole, grad_product, normed_turned, cot_turned, cot_sent = call(
         functools.partial(cot_kernel, count),
         grid,
         [SMEM] + [rows_block(tile, piece)] * count + [rows_block(tile, width)] + whole(down_parts),
@@ -828,12 +928,15 @@
             rows_block(tile, width),
             rows_block(tile, hidden_units),
             pl.BlockSpec((width, tile), lambda i: (0, i)),
+            pl.BlockSpec((width // 2, tile), lambda i: (0, i)),
+            pl.BlockSpec((width // 2, tile), lambda i: (0, i)),
         ],
-        [out((rows, width), BF), out((rows, hidden_units), F32), out((width, rows), BF)],
+        [out((rows, width), BF), out((rows, hidden_units), F32), out((width, rows), BF)]
+        + [out((width // 2, rows), BF)] * 2,
     )(offsets, *cot_pieces, normed_one, *down_parts)
 
     hidden_pieces = pieces_of(hidden.astype(BF))
-    *grad_parts, normed_two, scale_two, product, gate_bf, up_bf = call(
+    *grad_parts, normed_two, scale_two, product, deltas, normed_sent = call(
         functools.partial(ffn_kernel, count, halves),
         grid,
         [SMEM]
@@ -842,40 +945,45 @@
         + whole(gate_parts + up_parts)
         + [rows_block(tile, hidden_units)],
         [rows_block(tile, piece)] * count
-        + [rows_block(tile, width), rows_block(tile, 1)]
-        + [rows_block(tile, hidden_units)] * 3,
+        + [rows_block(tile, width), rows_block(tile, 1), rows_block(tile, hidden_units)]
+        + [rows_block(tile, 3 * hidden_units), rows_block(tile, width // 2)],
         split_out
-        + [out((rows, width), BF), out((rows, 1), F32)]
-        + [out((rows, hidden_units), BF)] * 3,
+        + [out((rows, width), BF), out((rows, 1), F32), out((rows, hidden_units), BF)]
+        + [out((rows, 3 * hidden_units), BF), out((rows, width // 2), BF)],
     )(offsets, *hidden_pieces, *token_pieces, *gate_parts, *up_parts, grad_product)
 
     grad_got = [shifted(p, "gx", s) for s, p in enumerate(grad_parts[1:], 1)]
-    ffn_own, ffn_got = weight_grads(
-        [(normed_two, gate_bf), (normed_two, up_bf), (cot_whole, product)], late=grad_got
-    )
     grad_normed_two = grad_parts[0]
     for part in grad_got:
         grad_normed_two = grad_normed_two + part.astype(F32)
-    (grad_low,) = after([grad_normed_two.astype(BF)], ffn_own)
-    grad_pieces = [grad_low] + pieces_of(grad_low)[1:]
-    blocks, size, total = ffn_own.shape
+    grad_pieces = pieces_of(grad_normed_two.astype(BF))
+    result_parts = split_dot(product, down_parts, *grad_got)
+    blocks = lax.axis_size("dev")
     if peers == 2:
-        row_tile = rows // blocks
-        chunk = pl.BlockSpec((1, size, total), lambda i: (i, 0, 0))
-        *result_parts, ffn_share = call(
-            functools.partial(result_share_kernel, count, halves),
-            (blocks,),
-            [SMEM, rows_block(row_tile, hidden_units)] + whole(down_parts) + [chunk, chunk],
-            [rows_block(row_tile, piece)] * count + [rows_block(size, total)],
-            split_out + [out((blocks * size, total), BF)],
-            deps=grad_got,
-        )(offsets, product, *down_parts, ffn_own, ffn_got)
+        half = pl.BlockSpec((rows, width // 4), lambda i: (0, i))
+        turned_half = pl.BlockSpec((width // 4, rows), lambda i: (i, 0))
+        ffn_share = call(
+            ffn_share_kernel,
+            (2,),
+            [half, half, turned_half, turned_half] + [same_block(deltas.shape)] * 2,
+            rows_block(width // 4, 3 * hidden_units),
+            out((width // 2, 3 * hidden_units), BF),
+        )(
+            normed_two, shifted(normed_sent, "gy", 1), cot_turned, shifted(cot_sent, "gy", 1),
+            deltas, shifted(deltas, "gy", 1),
+        )
+        (ffn_share,) = after([ffn_share], *grad_got)
     else:
-        result_parts = split_dot(product, down_parts)
-        ffn_share = ffn_own.reshape(blocks * size, total)
-    (ffn_share,) = after([ffn_share], *grad_pieces[1:])
+        ffn_share, _ = weight_grads(
+            [
+                (normed_two, [deltas[:, : 2 * hidden_units]]),
+                (cot_whole, [deltas[:, 2 * hidden_units :]]),
+            ]
+        )
+        ffn_share = ffn_share.reshape(-1, 3 * hidden_units)
     ffn_chunk = lax.psum_scatter(ffn_share, "dev", scatter_dimension=0, tiled=True)
 
+    late_parts = after(result_parts[1:], *grad_pieces[1:])
     branch, grad_mixed, inner_two = call(
         functools.partial(branch_kernel, count, halves),
         grid,
@@ -886,30 +994,32 @@
         + whole(out_w_parts),
         [rows_block(tile, width), rows_block(tile, q_cols), rows_block(tile, 1)],
         [out((rows, width), BF), out((rows, q_cols), BF), out((rows, 1), F32)],
+        deps=[late_parts[0]],
     )(
         offsets, *hidden_pieces, *grad_pieces, *token_pieces, scale_two, cot_whole, *out_w_parts
     )
 
-    late_parts = after(result_parts[1:], *grad_pieces[1:])
     result_got = [shifted(p, "gx", s) for s, p in enumerate(late_parts, 1)]
     result = hidden + result_parts[0]
     for part in result_got:
         result = result + part.astype(F32)
-    out_own, out_got = weight_grads([(branch, mixed)])
-
-    grad_query_lin, query_gain_part, *kv_parts = call(
+    out_own, out_got = weight_grads([(branch, [mixed])])
+
+    ffn_low, grad_query_lin, query_gain_part, *kv_parts = call(
         functools.partial(attend_back_kernel, head, small_tile, peers),
         None,
-        [VMEM] * (10 + 2 * len(keys)),
-        [VMEM] * (2 + 2 * len(keys)),
-        [out((rows, q_cols), BF), out((1, head), F32)]
+        [VMEM] * (10 + 2 * len(keys)) + [ANY],
+        [ANY] + [VMEM] * (2 + 2 * len(keys)),
+        [out(ffn_chunk.shape, BF), out((rows, q_cols), BF), out((1, head), F32)]
         + [out(k.shape, BF) for k in keys + values],
         [pltpu.VMEM((peers, rows, kv_cols), F32), pltpu.VMEM((peers, rows, kv_cols), F32)],
         deps=[out_own, result_got[0], result_got[-1]],
+        aliases={10 + 2 * len(keys): 0},
     )(
         grad_mixed, query_bf, query_lin, row_info, col_info, attended, logs,
-        q_scale, cosine, sine, *keys, *values,
-    )
+        q_scale, cosine, sine, *keys, *values, ffn_chunk,
+    )
+    ffn_sum = lax.all_gather(ffn_low, "dev", axis=0, tiled=True)
     if peers == 2:
         key_terms = [kv_parts[0], shifted(kv_parts[1], "gy", 1)]
         value_terms = [kv_parts[2], shifted(kv_parts[3], "gy", 1)]
@@ -927,7 +1037,6 @@
         shares
         + [out((rows + 16, piece), p.dtype) for p in split_out]
         + [out((rows, kv_cols), BF)] * 2,
-        deps=result_got[1:-1],
     )(
         offsets, grad_query_lin, query_lin, key_lin, value_bf, query_gain_part,
         *key_terms, *value_terms, k_scale, cosine, sine,
@@ -939,13 +1048,16 @@
         last_share = last_outs[0], shifted(last_outs[1], "gy", 1)
     else:
         last_share = weight_grads(
-            [(normed_turned, g) for g in (grad_query_lin, grad_key_lin, grad_value_lin)]
+            [(normed_turned, [grad_query_lin, grad_key_lin, grad_value_lin])]
         )
-    last_chunks = share_chunks([last_share, (out_own, out_got)])
-    (ffn_low,) = after([ffn_chunk], last_chunks[1])
-    ffn_sum = lax.all_gather(ffn_low, "dev", axis=0, tiled=True)
-    last_total, dev_got = dev_total(last_chunks)
-    last_others = dev_all(last_total)
+    last_shares = [last_share, (out_own, out_got)]
+    if fused and blocks == 4:
+        (last_total, last_low), dev_got = halving_total(last_shares, [], last_got)
+    else:
+        last_chunks = share_chunks(last_shares)
+        last_total, dev_got = dev_total(last_chunks)
+        last_low = last_total.astype(BF)
+    last_others = dev_all(last_low)
     gate_grad, up_grad, down_grad = widen(
         ffn_sum,
         (
@@ -971,13 +1083,13 @@
     grad_inputs, gain_part = call(
         functools.partial(final_kernel, count),
         None,
-        [VMEM] * (count + 8),
+        [VMEM] * (count + 7),
         [VMEM] * 2,
         [out((rows, piece), F32), out((8, piece), F32)],
-        deps=dev_got[:1],
+        deps=[last_low],
     )(
-        last_parts[0], *last_got, tokens, cotangent, hidden, grad_normed_two,
-        scale_one, scale_two, inner_two, below,
+        last_parts[0], *last_got, token_pieces[0], cotangent, hidden, grad_normed_two,
+        scale_one, scale_two, inner_two,
     )
     if peers == 2:
         last = small_sum(small_sum(gain_part, "gy"), "dev")

time: 314 us -> 305 us (0.971)
  waiting for transfers between devices: 125 us -> 97.6 us
  starting transfers between devices: 54.9 us -> 76.3 us
  other arithmetic: 14.1 us -> 8.25 us
  Pallas kernels: 82.8 us -> 86.9 us
    ppermute x42 -> x44, waiting for transfers between devices: 99 us -> 67.1 us  [shifted(): lax.ppermute(block, axis, [(i, (i + shift) % size) for i in range(size)])]
    ppermute x6 -> x7, waiting for transfers between devices: 0.02 us -> 30.4 us  [dev_send(): lax.ppermute(block, 'dev', [(i, i ^ m if even else (i + m) % count) for i...]
    all_gather x1, waiting for transfers between devices: 25.6 us -> 0.01 us  [per_device(): ffn_sum = lax.all_gather(ffn_low, 'dev', axis=0, tiled=True)]
    ppermute x42 -> x44, starting transfers between devices: 46.8 us -> 67.6 us  [shifted(): lax.ppermute(block, axis, [(i, (i + shift) % size) for i in range(size)])]
    convert_element_type x4 -> x1, other arithmetic: 5.75 us -> 0.96 us  [per_device(): grad_pieces = pieces_of(grad_normed_two.astype(BF))]
    pallas_call x15 -> x18, Pallas kernels: 82.8 us -> 86.9 us  [call(): return lambda *args: run(*args, *deps)]
    unnamed x105 -> x131, local copies, waits for them, and re-layouts: 14.7 us -> 16.1 us
    ppermute x6 -> x7, starting transfers between devices: 8.06 us -> 8.57 us  [dev_send(): lax.ppermute(block, 'dev', [(i, i ^ m if even else (i + m) % count) for i...]
  transfers between devices with their start and end apart: 50 -> 53, of which waited for: 17 -> 21; matrix products, arithmetic and copies ran while one was open for 7% -> 3% of each run, Pallas kernels for 22% -> 21%
where the time goes in v3:
time: 305 us; the launch traced here: 303 us
  waiting for transfers between devices  97.6 us (32%)
  Pallas kernels  86.9 us (28%)
  starting transfers between devices  76.3 us (25%)
  local copies, waits for them, and re-layouts  19.2 us (6%)
  between operations  14.5 us (5%)
  other arithmetic  8.25 us (3%)
    pallas_call x18, Pallas kernels, call(): return lambda *args: run(*args, *deps)  86.9 us
    ppermute x44, starting transfers between devices, shifted(): lax.ppermute(block, axis, [(i, (i + shift) % size) for i in range(size)])  67.6 us
    ppermute x44, waiting for transfers between devices, shifted(): lax.ppermute(block, axis, [(i, (i + shift) % size) for i in range(size)])  67.1 us
    ppermute x7, waiting for transfers between devices, dev_send(): lax.ppermute(block, 'dev', [(i, i ^ m if even else (i + m) % count) for i...  30.4 us
    unnamed x131, local copies, waits for them, and re-layouts  16.1 us
    ppermute x7, starting transfers between devices, dev_send(): lax.ppermute(block, 'dev', [(i, i ^ m if even else (i + m) % count) for i...  8.57 us
  transfers between devices with their start and end apart: 53, of which 21 were waited for; matrix products, arithmetic and copies ran while one was open for 3% of the time, Pallas kernels for 21%

profile of v3, /device:TPU:0, one launch (start us, length us, event | category | flops | bytes accessed | tf_op | source)
XLA Modules:
  0.0 302.7 jit_solution(17945512973449643346)
XLA Ops:
  8.6 1.1 maximum_maximum_fusion.refs_0_.refs_4_.refs_8_
  9.7 3.1 %collective-permute-start = (bf16[528,256]{1,0:T(8,128)(2,1)S(1)}, bf16[528,256]{1,0:T(8,128)(2,1)S(1)}, u32[]{:S(2)}, u32[]{:S(2)}) collective-permute-start(bf16[528,256]{1,0:T(8,128)(2,1)S(1)} %maximum_maximum_fusion.refs_0_.refs_4_.refs_8_), channel_id=1, source_target_pairs={{0,2},{2,4},{4,6},{6,0},{1,3},{3,5},{5,7},{7,1},{8,10},{10,12},{12... | collective-permute-start | bytes 811016 | tf_op jit(solution)/shard_map/ppermute | solution.py:42
  12.8 2.6 collective-permute-start.1
  15.4 1.3 collective-permute-start.2
  17.3 1.7 copy.34.refs_0_
  20.1 2.6 shard_map.246
  22.8 10.2 %collective-permute-done.1.refs_2_.refs_6_.refs_10_ = bf16[528,256]{1,0:T(8,128)(2,1)S(1)} collective-permute-done((bf16[528,256]{1,0:T(8,128)(2,1)S(1)}, bf16[528,256]{1,0:T(8,128)(2,1)S(1)}, u32[]{:S(2)}, u32[]{:S(2)}) %collective-permute-start.1) | collective-permute-done | bytes 270368 | tf_op jit(solution)/shard_map/ppermute | solution.py:42
  33.9 6.2 %collective-permute-start.8 = (bf16[512,256]{1,0:T(8,128)(2,1)}, bf16[512,256]{1,0:T(8,128)(2,1)S(1)}, u32[]{:S(2)}, u32[]{:S(2)}) collective-permute-start(bf16[512,256]{1,0:T(8,128)(2,1)} %shard_map.248), channel_id=1, source_target_pairs={{0,2},{2,4},{4,6},{6,0},{1,3},{3,5},{5,7},{7,1},{8,10},{10,12},{12... | collective-permute-start | bytes 786440 | tf_op jit(solution)/shard_map/ppermute | solution.py:42
  41.1 1.1 collective-permute-start.9
  43.1 5.7 %shard_map.247 = (bf16[512,1024]{1,0:T(8,128)(2,1)}, f32[512,1]{1,0:T(8,128)}, f32[512,512]{1,0:T(8,128)}, f32[512,256]{1,0:T(8,128)}, bf16[512,512]{1,0:T(8,128...) custom-call(s32[8]{0:T(128)} %stack.47.offset_ref.refs_5_, bf16[528,256]{1,0:T(8,128)(2,1)} %copy-done, ...), custom_call_target="tpu_custom_call" | custom-call | flops 1048576 | bytes 65536 | tf_op jit(solution)/shard_map/pallas_call | solution.py:639
  50.1 3.8 %collective-permute-done.9.refs_5_.refs_4_.refs_3_ = bf16[512,256]{1,0:T(8,128)(2,1)S(1)} collective-permute-done((bf16[512,256]{1,0:T(8,128)(2,1)}, bf16[512,256]{1,0:T(8,128)(2,1)S(1)}, u32[]{:S(2)}, u32[]{:S(2)}) %collective-permute-start.9) | collective-permute-done | bytes 262176 | tf_op jit(solution)/shard_map/ppermute | solution.py:42
  54.8 7.5 %shard_map.249 = (bf16[512,512]{1,0:T(8,128)(2,1)}, f32[512,512]{1,0:T(8,128)}, f32[8,512]{1,0:T(8,128)}) custom-call(bf16[512,512]{1,0:T(8,128)(2,1)} %get-tuple-element.93.q_ref.refs_1_, f32[8,512]{1,0:T(8,128)} %get-tuple-element.91.refs_18_.row_ref.refs_3_, f32[8,512]{1,0:T(8,128)} %get-tuple-element.92.refs_19_.col_ref.refs_4_, ...), custom_call_target="tpu_custom_call" | custom-call | flops 1048576 | bytes 65536 | tf_op jit(solution)/shard_map/pallas_call | solution.py:639
  62.3 2.8 collective-permute-done.11.refs_3_.refs_2_
  65.8 2.9 shard_map.250
  68.9 2.4 collective-permute-start.13
  71.3 1.3 collective-permute-start.14
  72.8 7.3 %collective-permute-done.12 = bf16[512,256]{1,0:T(8,128)(2,1)S(1)} collective-permute-done((bf16[512,256]{1,0:T(8,128)(2,1)}, bf16[512,256]{1,0:T(8,128)(2,1)S(1)}, u32[]{:S(2)}, u32[]{:S(2)}) %collective-permute-start.12) | collective-permute-done | bytes 262176 | tf_op jit(solution)/shard_map/ppermute | solution.py:42
  80.1 10.3 %collective-permute-done.13 = bf16[512,256]{1,0:T(8,128)(2,1)S(1)} collective-permute-done((bf16[512,256]{1,0:T(8,128)(2,1)}, bf16[512,256]{1,0:T(8,128)(2,1)S(1)}, u32[]{:S(2)}, u32[]{:S(2)}) %collective-permute-start.13) | collective-permute-done | bytes 262176 | tf_op jit(solution)/shard_map/ppermute | solution.py:42
  90.4 2.0 fusion.6
  92.3 5.8 %collective-permute-start.15 = (bf16[512,256]{1,0:T(8,128)(2,1)S(1)}, bf16[512,256]{1,0:T(8,128)(2,1)S(1)}, u32[]{:S(2)}, u32[]{:S(2)}) collective-permute-start(bf16[512,256]{1,0:T(8,128)(2,1)S(1)} %get-tuple-element.167.refs_0_), channel_id=1, source_target_pairs={{0,2},{2,4},{4,6},{6,0},{1,3},{3,5},{5,7},{7,1},{8,10},{10,12},{12... | collective-permute-start | bytes 786440 | tf_op jit(solution)/shard_map/ppermute | solution.py:42
  98.2 2.4 collective-permute-start.17
  100.5 4.7 %shard_map.251 = (bf16[512,1024]{1,0:T(8,128)(2,1)}, f32[512,768]{1,0:T(8,128)}, bf16[1024,512]{1,0:T(8,128)(2,1)}, bf16[512,512]{1,0:T(8,128)(2,1)}, bf16[512,512]{1,0:T(8,128)(2,1)}) custom-call(s32[8]{0:T(128)} %stack.47.offset_ref.refs_5_, bf16[512,256]{1,0:T(8,128)(2,1)} %refs_5_.3, bf16[512,256]{1,0:T(8,128)(2,1)} %copy-done.9, ...), custom_call_target="tpu_custom_call" | custom-call | flops 1048576 | bytes 65536 | tf_op jit(solution)/shard_map/pallas_call | solution.py:639
  105.2 8.4 %collective-permute-done.16.refs_2_ = bf16[512,256]{1,0:T(8,128)(2,1)S(1)} collective-permute-done((bf16[512,256]{1,0:T(8,128)(2,1)S(1)}, bf16[512,256]{1,0:T(8,128)(2,1)S(1)}, u32[]{:S(2)}, u32[]{:S(2)}) %collective-permute-start.16) | collective-permute-done | bytes 262176 | tf_op jit(solution)/shard_map/ppermute | solution.py:42
  113.6 1.3 collective-permute-done.17.refs_3_
  115.6 8.4 %shard_map.252 = (f32[512,256]{1,0:T(8,128)}, bf16[512,256]{1,0:T(8,128)(2,1)}, bf16[512,256]{1,0:T(8,128)(2,1)}, bf16[512,256]{1,0:T(8,128)(2,1)}, bf16[512,102...) custom-call(s32[8]{0:T(128)} %stack.47.offset_ref.refs_5_, ...), custom_call_target="tpu_custom_call" | custom-call | flops 1048576 | bytes 65536 | tf_op jit(solution)/shard_map/pallas_call | solution.py:639
  124.6 5.9 %collective-permute-start.21 = (bf16[512,256]{1,0:T(8,128)(2,1)}, bf16[512,256]{1,0:T(8,128)(2,1)S(1)}, u32[]{:S(2)}, u32[]{:S(2)}) collective-permute-start(bf16[512,256]{1,0:T(8,128)(2,1)} %get-tuple-element.104), channel_id=1, source_target_pairs={{0,2},{2,4},{4,6},{6,0},{1,3},{3,5},{5,7},{7,1},{8,10},{10,12},{12... | collective-permute-start | bytes 786440 | tf_op jit(solution)/shard_map/ppermute | solution.py:42
  130.6 3.4 %collective-permute-start.22 = (bf16[512,256]{1,0:T(8,128)(2,1)}, bf16[512,256]{1,0:T(8,128)(2,1)S(1)}, u32[]{:S(2)}, u32[]{:S(2)}) collective-permute-start(bf16[512,256]{1,0:T(8,128)(2,1)} %get-tuple-element.105), channel_id=1, source_target_pairs={{0,4},{2,6},{4,0},{6,2},{1,5},{3,7},{5,1},{7,3},{8,12},{10,14},{12... | collective-permute-start | bytes 786440 | tf_op jit(solution)/shard_map/ppermute | solution.py:42
  134.0 4.3 %collective-permute-start.23 = (bf16[512,256]{1,0:T(8,128)(2,1)}, bf16[512,256]{1,0:T(8,128)(2,1)S(1)}, u32[]{:S(2)}, u32[]{:S(2)}) collective-permute-start(bf16[512,256]{1,0:T(8,128)(2,1)} %get-tuple-element.106), channel_id=1, source_target_pairs={{0,6},{2,0},{4,2},{6,4},{1,7},{3,1},{5,3},{7,5},{8,14},{10,8},{12,... | collective-permute-start | bytes 786440 | tf_op jit(solution)/shard_map/ppermute | solution.py:42
  139.1 1.5 copy-done.8
  140.6 6.8 %shard_map.256.refs_0_ = bf16[512,2304]{1,0:T(8,128)(2,1)} custom-call(bf16[512,1024]{1,0:T(8,128)(2,1)} %get-tuple-element.121.own_ref, bf16[512,512]{1,0:T(8,128)(2,1)} %copy-done.44, bf16[512,512]{1,0:T(8,128)(2,1)} %get-tuple-element.123.cot_ref, bf16[512,512]{1,0:T(8,128)(2,1)} %copy-done.43, bf16[512,2304]{1,0:T(8,128)(2,1)} %get-tuple-element.125.delta_ref, ...), custom_call_target="tpu_custom_call" | custom-call | flops 1048576 | bytes 65536 | tf_op jit(solution)/shard_map/pallas_call | solution.py:639
  147.4 4.5 %collective-permute-done.22.refs_3_.refs_2_ = bf16[512,256]{1,0:T(8,128)(2,1)S(1)} collective-permute-done((bf16[512,256]{1,0:T(8,128)(2,1)}, bf16[512,256]{1,0:T(8,128)(2,1)S(1)}, u32[]{:S(2)}, u32[]{:S(2)}) %collective-permute-start.22) | collective-permute-done | bytes 262176 | tf_op jit(solution)/shard_map/ppermute | solution.py:42
  155.5 5.4 %collective-permute-start.24 = (bf16[512,256]{1,0:T(8,128)(2,1)S(1)}, bf16[512,256]{1,0:T(8,128)(2,1)S(1)}, u32[]{:S(2)}, u32[]{:S(2)}) collective-permute-start(bf16[512,256]{1,0:T(8,128)(2,1)S(1)} %get-tuple-element.165.refs_4_), channel_id=1, source_target_pairs={{0,2},{2,4},{4,6},{6,0},{1,3},{3,5},{5,7},{7,1},{8,10},{10,12},{12... | collective-permute-start | bytes 786440 | tf_op jit(solution)/shard_map/ppermute | solution.py:42
  161.1 2.2 collective-permute-start.26
  163.3 3.5 %shard_map.253 = (f32[512,256]{1,0:T(8,128)}, bf16[512,256]{1,0:T(8,128)(2,1)}, bf16[512,256]{1,0:T(8,128)(2,1)}, bf16[512,256]{1,0:T(8,128)(2,1)}) custom-call(s32[8]{0:T(128)} %stack.47.offset_ref.refs_5_, bf16[512,768]{1,0:T(8,128)(2,1)} %get-tuple-element.103.left_ref, bf16[768,512]{1,0:T(8,128)(2,1)} %refs_0_.6, bf16[768,512]{1,0:T(8,128)(2,1)} %copy-done.6, ...), custom_call_target="tpu_custom_call" | custom-call | flops 1048576 | bytes 65536 | tf_op jit(solution)/shard_map/pallas_call | solution.py:639
  167.8 10.4 %collective-permute-done.25.refs_4_.refs_6_ = bf16[512,256]{1,0:T(8,128)(2,1)S(1)} collective-permute-done((bf16[512,256]{1,0:T(8,128)(2,1)S(1)}, bf16[512,256]{1,0:T(8,128)(2,1)S(1)}, u32[]{:S(2)}, u32[]{:S(2)}) %collective-permute-start.25) | collective-permute-done | bytes 262176 | tf_op jit(solution)/shard_map/ppermute | solution.py:42
  179.1 6.0 %collective-permute-start.27 = (bf16[512,256]{1,0:T(8,128)(2,1)}, bf16[512,256]{1,0:T(8,128)(2,1)S(1)}, u32[]{:S(2)}, u32[]{:S(2)}) collective-permute-start(bf16[512,256]{1,0:T(8,128)(2,1)} %get-tuple-element.112.refs_16_), channel_id=1, source_target_pairs={{0,2},{2,4},{4,6},{6,0},{1,3},{3,5},{5,7},{7,1},{8,10},{10,12},{12... | collective-permute-start | bytes 786440 | tf_op jit(solution)/shard_map/ppermute | solution.py:42
  185.1 2.4 collective-permute-start.29
  187.5 4.8 %shard_map.255 = (bf16[512,1024]{1,0:T(8,128)(2,1)}, bf16[512,512]{1,0:T(8,128)(2,1)}, f32[512,1]{1,0:T(8,128)}) custom-call(s32[8]{0:T(128)} %stack.47.offset_ref.refs_5_, bf16[512,256]{1,0:T(8,128)(2,1)} %copy-done.7, bf16[512,256]{1,0:T(8,128)(2,1)} %copy-done.22, bf16[512,256]{1,0:T(8,128)(2,1)} %copy-done.23, bf16[512,256]{1,0:T(8,128)(2,1)} %copy-done.24, ...), custom_call_target="tpu_custom_call" | custom-call | flops 1048576 | bytes 65536 | tf_op jit(solution)/shard_map/pallas_call | solution.py:639
  192.3 4.2 %shard_map.258 = (bf16[4,128,512]{2,1,0:T(8,128)(2,1)}, bf16[4,128,512]{2,1,0:T(8,128)(2,1)}) custom-call(bf16[512,1024]{1,0:T(8,128)(2,1)} %get-tuple-element.126.refs_0_.refs_1_, bf16[512,1024]{1,0:T(8,128)(2,1)} %get-tuple-element.126.refs_0_.refs_1_, bf16[512,512]{1,0:T(8,128)(2,1)} %get-tuple-element.96.left_ref.refs_2_), custom_call_target="tpu_custom_call" | custom-call | flops 1048576 | bytes 65536 | tf_op jit(solution)/shard_map/pallas_call | solution.py:639
  196.5 2.3 collective-permute-done.29.refs_17_
  199.6 8.0 %shard_map.259 = (bf16[128,2304]{1,0:T(8,128)(2,1)}, bf16[512,512]{1,0:T(8,128)(2,1)}, f32[1,128]{1,0:T(1,128)}, bf16[512,256]{1,0:T(8,128)(2,1)}, bf16[512,256]...) custom-call(bf16[512,512]{1,0:T(8,128)(2,1)} %get-tuple-element.117.refs_, ...), custom_call_target="tpu_custom_call", output_to_operand_aliasing={{0}: (14, {})} | custom-call | flops 1048576 | bytes 65536 | tf_op jit(solution)/shard_map/pallas_call | solution.py:639
  208.2 1.2 collective-permute-done.33.refs_6_
  210.5 8.0 %shard_map.260 = (bf16[4,128,1024]{2,1,0:T(8,128)(2,1)}, bf16[4,128,1024]{2,1,0:T(8,128)(2,1)}, f32[528,256]{1,0:T(8,128)}, bf16[528,256]{1,0:T(8,128)(2,1)}, bf...) custom-call(s32[8]{0:T(128)} %stack.47.offset_ref.refs_5_, ...), custom_call_target="tpu_custom_call" | custom-call | flops 1048576 | bytes 65536 | tf_op jit(solution)/shard_map/pallas_call | solution.py:639
  219.6 2.4 collective-permute-done.39.refs_3_
  223.2 3.5 %shard_map.261 = (f32[2,128,768]{2,1,0:T(8,128)}, bf16[2,128,768]{2,1,0:T(8,128)(2,1)}, f32[2,128,768]{2,1,0:T(8,128)}, bf16[2,128,768]{2,1,0:T(8,128)(2,1)}) custom-call(s32[4]{0:T(128)} %iota_xor_fusion.chunk_ref, bf16[4,128,1024]{2,1,0:T(8,128)(2,1)} %get-tuple-element.142.refs_0_, bf16[4,128,512]{2,1,0:T(8,128)(2,1)} %get-tuple-element.127.refs_15_.refs_1_, ...), custom_call_target="tpu_custom_call" | custom-call | flops 1048576 | bytes 65536 | tf_op jit(solution)/shard_map/pallas_call | solution.py:639
  226.7 1.5 collective-permute-start.40
  228.2 1.5 collective-permute-start.41
  230.8 1.8 collective-permute-start.36
  232.6 1.1 collective-permute-start.37
  233.8 11.3 %collective-permute-done.40.got_a = bf16[2,128,768]{2,1,0:T(8,128)(2,1)S(1)} collective-permute-done((bf16[2,128,768]{2,1,0:T(8,128)(2,1)}, bf16[2,128,768]{2,1,0:T(8,128)(2,1)S(1)}, u32[]{:S(2)}, u32[]{:S(2)}) %collective-permute-start.40) | collective-permute-done | bytes 393248 | tf_op jit(solution)/shard_map/ppermute | solution.py:75
  245.0 2.5 collective-permute-done.41.got_b
  248.2 2.6 shard_map.262
  250.8 2.1 collective-permute-start.42
  253.2 4.2 %collective-permute-done.42.got_a = bf16[128,768]{1,0:T(8,128)(2,1)S(1)} collective-permute-done((bf16[128,768]{1,0:T(8,128)(2,1)}, bf16[128,768]{1,0:T(8,128)(2,1)S(1)}, u32[]{:S(2)}, u32[]{:S(2)}) %collective-permute-start.42) | collective-permute-done | bytes 196640 | tf_op jit(solution)/shard_map/ppermute | solution.py:75
  257.4 1.5 collective-permute-done.43.got_b
  259.6 2.4 shard_map.263
  261.9 3.5 %shard_map.264 = (f32[512,256]{1,0:T(8,128)}, f32[8,256]{1,0:T(8,128)}) custom-call(f32[528,256]{1,0:T(8,128)} %get-tuple-element.136.refs_0_, bf16[528,256]{1,0:T(8,128)(2,1)} %copy-done.19, bf16[528,256]{1,0:T(8,128)(2,1)} %copy-done.20, bf16[528,256]{1,0:T(8,128)(2,1)} %copy-done.21, bf16[528,256]{1,0:T(8,128)(2,1)} %copy-done, bf16[512,256]{1,0:T(8,128)(2,1)} %refs_5_.3, ...), custom_call_target="tpu_custom_call" | custom-call | flops 1048576 | bytes 65536 | tf_op jit(solution)/shard_map/pallas_call | solution.py:639
  268.1 2.7 collective-permute-start.47
  271.9 1.5 collective-permute-start.49
  273.4 1.8 collective-permute-start.50
  276.3 4.2 %shard_map.265 = (f32[512,768]{1,0:T(8,128)}, f32[512,768]{1,0:T(8,128)}, f32[768,512]{1,0:T(8,128)}) custom-call(bf16[512,2304]{1,0:T(8,128)(2,1)} %all-gather.2.cloned.1.call-done.whole_ref, f32[128,1536]{1,0:T(8,128)} %get-tuple-element.156.refs_0_), custom_call_target="tpu_custom_call" | custom-call | flops 1048576 | bytes 65536 | tf_op jit(solution)/shard_map/pallas_call | solution.py:639
  280.5 3.2 %collective-permute-done.48.refs_1_ = bf16[128,1536]{1,0:T(8,128)(2,1)S(1)} collective-permute-done((bf16[128,1536]{1,0:T(8,128)(2,1)S(1)}, bf16[128,1536]{1,0:T(8,128)(2,1)S(1)}, u32[]{:S(2)}, u32[]{:S(2)}) %collective-permute-start.48) | collective-permute-done | bytes 393248 | tf_op jit(solution)/shard_map/ppermute | solution.py:75
  283.8 7.8 %collective-permute-done.50.refs_3_ = bf16[128,1536]{1,0:T(8,128)(2,1)S(1)} collective-permute-done((bf16[128,1536]{1,0:T(8,128)(2,1)S(1)}, bf16[128,1536]{1,0:T(8,128)(2,1)S(1)}, u32[]{:S(2)}, u32[]{:S(2)}) %collective-permute-start.50) | collective-permute-done | bytes 393248 | tf_op jit(solution)/shard_map/ppermute | solution.py:75
  292.4 3.5 %shard_map.266 = (f32[512,512]{1,0:T(8,128)}, f32[512,256]{1,0:T(8,128)}, f32[512,256]{1,0:T(8,128)}, f32[512,512]{1,0:T(8,128)}) custom-call(s32[4]{0:T(128)} %pad_add_fusion.owner_ref, f32[128,1536]{1,0:T(8,128)} %get-tuple-element.156.refs_0_, bf16[128,1536]{1,0:T(8,128)(2,1)} %copy-done.50, bf16[128,1536]{1,0:T(8,128)(2,1)} %copy-done.51, ...), custom_call_target="tpu_custom_call" | custom-call | flops 1048576 | bytes 65536 | tf_op jit(solution)/shard_map/pallas_call | solution.py:639
  (214 shorter events, 30.0 us)
Async XLA Ops:
  7.2 32.8 %copy-start.63 = (bf16[128]{0:T(256)(128)(2,1)S(1)}, bf16[128]{0:T(256)(128)(2,1)}, u32[]{:S(2)}) copy-start(bf16[128]{0:T(256)(128)(2,1)} %param.21) | copy-start | bytes 772
  7.2 33.4 %copy-start.64 = (bf16[128]{0:T(256)(128)(2,1)S(1)}, bf16[128]{0:T(256)(128)(2,1)}, u32[]{:S(2)}) copy-start(bf16[128]{0:T(256)(128)(2,1)} %param.20) | copy-start | bytes 772
  7.2 191.6 %reduce-scatter.2.cloned.1.call-start = ((), (), s32[]{:S(2)}) async-start(), calls=%async_computation.1 | async-start | bytes 2949120 | tf_op jit(solution)/shard_map/reduce_scatter | solution.py:984
  9.7 32.5 %copy-start = (bf16[528,256]{1,0:T(8,128)(2,1)}, bf16[528,256]{1,0:T(8,128)(2,1)S(1)}, u32[]{:S(2)}) copy-start(bf16[528,256]{1,0:T(8,128)(2,1)S(1)} %maximum_maximum_fusion.refs_0_.refs_4_.refs_8_) | copy-start | bytes 811012
  9.7 13.0 %collective-permute-start = (bf16[528,256]{1,0:T(8,128)(2,1)S(1)}, bf16[528,256]{1,0:T(8,128)(2,1)S(1)}, u32[]{:S(2)}, u32[]{:S(2)}) collective-permute-start(bf16[528,256]{1,0:T(8,128)(2,1)S(1)} %maximum_maximum_fusion.refs_0_.refs_4_.refs_8_), channel_id=1, source_target_pairs={{0,2},{2,4},{4,6},{6,0},{1,3},{3,5},{5,7},{7,1},{8,10},{10,12},{12... | collective-permute-start | bytes 811016 | tf_op jit(solution)/shard_map/ppermute | solution.py:42
  12.8 20.2 %collective-permute-start.1 = (bf16[528,256]{1,0:T(8,128)(2,1)S(1)}, bf16[528,256]{1,0:T(8,128)(2,1)S(1)}, u32[]{:S(2)}, u32[]{:S(2)}) collective-permute-start(bf16[528,256]{1,0:T(8,128)(2,1)S(1)} %maximum_maximum_fusion.refs_0_.refs_4_.refs_8_), channel_id=1, source_target_pairs={{0,4},{2,6},{4,0},{6,2},{1,5},{3,7},{5,1},{7,3},{8,12},{10,14},{12... | collective-permute-start | bytes 811016 | tf_op jit(solution)/shard_map/ppermute | solution.py:42
  15.4 17.6 %collective-permute-start.2 = (bf16[528,256]{1,0:T(8,128)(2,1)S(1)}, bf16[528,256]{1,0:T(8,128)(2,1)S(1)}, u32[]{:S(2)}, u32[]{:S(2)}) collective-permute-start(bf16[528,256]{1,0:T(8,128)(2,1)S(1)} %maximum_maximum_fusion.refs_0_.refs_4_.refs_8_), channel_id=1, source_target_pairs={{0,6},{2,0},{4,2},{6,4},{1,7},{3,1},{5,3},{7,5},{8,14},{10,8},{12,... | collective-permute-start | bytes 811016 | tf_op jit(solution)/shard_map/ppermute | solution.py:42
  16.8 25.4 %collective-permute-start.3 = (bf16[512,512]{1,0:T(8,128)(2,1)}, bf16[512,512]{1,0:T(8,128)(2,1)S(1)}, u32[]{:S(2)}, u32[]{:S(2)}) collective-permute-start(bf16[512,512]{1,0:T(8,128)(2,1)} %refs_12_.3), channel_id=1, source_target_pairs={{0,1},{1,0},{2,3},{3,2},{4,5},{5,4},{6,7},{7,6},{8,9},{9,8},{10,11... | collective-permute-start | bytes 1572872 | tf_op jit(solution)/shard_map/ppermute | solution.py:42
  16.8 24.3 %collective-permute-start.4 = (bf16[512,256]{1,0:T(8,128)(2,1)}, bf16[512,256]{1,0:T(8,128)(2,1)S(1)}, u32[]{:S(2)}, u32[]{:S(2)}) collective-permute-start(bf16[512,256]{1,0:T(8,128)(2,1)} %refs_14_.3), channel_id=1, source_target_pairs={{0,1},{1,0},{2,3},{3,2},{4,5},{5,4},{6,7},{7,6},{8,9},{9,8},{10,11... | collective-permute-start | bytes 786440 | tf_op jit(solution)/shard_map/ppermute | solution.py:42
  22.8 19.4 %collective-permute-start.5 = (bf16[512,256]{1,0:T(8,128)(2,1)}, bf16[512,256]{1,0:T(8,128)(2,1)S(1)}, u32[]{:S(2)}, u32[]{:S(2)}) collective-permute-start(bf16[512,256]{1,0:T(8,128)(2,1)} %refs_16_.1), channel_id=1, source_target_pairs={{0,1},{1,0},{2,3},{3,2},{4,5},{5,4},{6,7},{7,6},{8,9},{9,8},{10,11... | collective-permute-start | bytes 786440 | tf_op jit(solution)/shard_map/ppermute | solution.py:42
  33.1 29.2 %collective-permute-start.10 = (bf16[512,512]{1,0:T(8,128)(2,1)}, bf16[512,512]{1,0:T(8,128)(2,1)S(1)}, u32[]{:S(2)}, u32[]{:S(2)}) collective-permute-start(bf16[512,512]{1,0:T(8,128)(2,1)} %refs_14_.2), channel_id=1, source_target_pairs={{0,1},{1,0},{2,3},{3,2},{4,5},{5,4},{6,7},{7,6},{8,9},{9,8},{10,11... | collective-permute-start | bytes 1572872 | tf_op jit(solution)/shard_map/ppermute | solution.py:42
  33.9 15.5 %collective-permute-start.8 = (bf16[512,256]{1,0:T(8,128)(2,1)}, bf16[512,256]{1,0:T(8,128)(2,1)S(1)}, u32[]{:S(2)}, u32[]{:S(2)}) collective-permute-start(bf16[512,256]{1,0:T(8,128)(2,1)} %shard_map.248), channel_id=1, source_target_pairs={{0,2},{2,4},{4,6},{6,0},{1,3},{3,5},{5,7},{7,1},{8,10},{10,12},{12... | collective-permute-start | bytes 786440 | tf_op jit(solution)/shard_map/ppermute | solution.py:42
  41.1 12.8 %collective-permute-start.9 = (bf16[512,256]{1,0:T(8,128)(2,1)}, bf16[512,256]{1,0:T(8,128)(2,1)S(1)}, u32[]{:S(2)}, u32[]{:S(2)}) collective-permute-start(bf16[512,256]{1,0:T(8,128)(2,1)} %shard_map.248), channel_id=1, source_target_pairs={{0,6},{2,0},{4,2},{6,4},{1,7},{3,1},{5,3},{7,5},{8,14},{10,8},{12,... | collective-permute-start | bytes 786440 | tf_op jit(solution)/shard_map/ppermute | solution.py:42
  48.7 20.0 %copy-start.5 = (bf16[768,512]{1,0:T(8,128)(2,1)S(1)}, bf16[768,512]{1,0:T(8,128)(2,1)}, u32[]{:S(2)}) copy-start(bf16[768,512]{1,0:T(8,128)(2,1)} %refs_0_.6) | copy-start | bytes 2359300
  48.7 23.9 %copy-start.41 = (bf16[512,768]{1,0:T(8,128)(2,1)S(1)}, bf16[512,768]{1,0:T(8,128)(2,1)}, u32[]{:S(2)}) copy-start(bf16[512,768]{1,0:T(8,128)(2,1)} %refs_8_.3) | copy-start | bytes 2359300
  48.8 41.6 %copy-start.25 = (bf16[512,256]{1,0:T(8,128)(2,1)S(1)}, bf16[512,256]{1,0:T(8,128)(2,1)}, u32[]{:S(2)}) copy-start(bf16[512,256]{1,0:T(8,128)(2,1)} %param.15) | copy-start | bytes 786436
  48.8 5.1 %collective-permute-start.6 = (bf16[512,256]{1,0:T(8,128)(2,1)}, bf16[512,256]{1,0:T(8,128)(2,1)S(1)}, u32[]{:S(2)}, u32[]{:S(2)}) collective-permute-start(bf16[512,256]{1,0:T(8,128)(2,1)} %get-tuple-element.94.refs_0_.refs_10_), channel_id=1, source_target_pairs={{0,1},{1,0},{2,3},{3,2},{4,5},{5,4},{6,7},{7,6},{8,9},{9,8},{10,11... | collective-permute-start | bytes 786440 | tf_op jit(solution)/shard_map/ppermute | solution.py:42
  49.0 4.9 %collective-permute-start.7 = (bf16[512,256]{1,0:T(8,128)(2,1)}, bf16[512,256]{1,0:T(8,128)(2,1)S(1)}, u32[]{:S(2)}, u32[]{:S(2)}) collective-permute-start(bf16[512,256]{1,0:T(8,128)(2,1)} %get-tuple-element.95.refs_2_.refs_12_.refs_3_), channel_id=1, source_target_pairs={{0,1},{1,0},{2,3},{3,2},{4,5},{5,4},{6,7},{7,6},{8,9},{9,8},{10,11... | collective-permute-start | bytes 786440 | tf_op jit(solution)/shard_map/ppermute | solution.py:42
  49.3 15.7 %collective-permute-start.11 = (bf16[512,256]{1,0:T(8,128)(2,1)S(1)}, bf16[512,256]{1,0:T(8,128)(2,1)S(1)}, u32[]{:S(2)}, u32[]{:S(2)}) collective-permute-start(bf16[512,256]{1,0:T(8,128)(2,1)S(1)} %copy-done.30), channel_id=1, source_target_pairs={{0,4},{2,6},{4,0},{6,2},{1,5},{3,7},{5,1},{7,3},{8,12},{10,14},{12... | collective-permute-start | bytes 786440 | tf_op jit(solution)/shard_map/ppermute | solution.py:42
  68.8 11.3 %collective-permute-start.12 = (bf16[512,256]{1,0:T(8,128)(2,1)}, bf16[512,256]{1,0:T(8,128)(2,1)S(1)}, u32[]{:S(2)}, u32[]{:S(2)}) collective-permute-start(bf16[512,256]{1,0:T(8,128)(2,1)} %get-tuple-element.98), channel_id=1, source_target_pairs={{0,2},{2,4},{4,6},{6,0},{1,3},{3,5},{5,7},{7,1},{8,10},{10,12},{12... | collective-permute-start | bytes 786440 | tf_op jit(solution)/shard_map/ppermute | solution.py:42
  68.8 29.4 %collective-permute-start.20 = (bf16[768,512]{1,0:T(8,128)(2,1)S(1)}, bf16[768,512]{1,0:T(8,128)(2,1)S(1)}, u32[]{:S(2)}, u32[]{:S(2)}) collective-permute-start(bf16[768,512]{1,0:T(8,128)(2,1)S(1)} %copy-done.5), channel_id=1, source_target_pairs={{0,1},{1,0},{2,3},{3,2},{4,5},{5,4},{6,7},{7,6},{8,9},{9,8},{10,11... | collective-permute-start | bytes 2359304 | tf_op jit(solution)/shard_map/ppermute | solution.py:42
  68.9 21.4 %collective-permute-start.13 = (bf16[512,256]{1,0:T(8,128)(2,1)}, bf16[512,256]{1,0:T(8,128)(2,1)S(1)}, u32[]{:S(2)}, u32[]{:S(2)}) collective-permute-start(bf16[512,256]{1,0:T(8,128)(2,1)} %get-tuple-element.99), channel_id=1, source_target_pairs={{0,4},{2,6},{4,0},{6,2},{1,5},{3,7},{5,1},{7,3},{8,12},{10,14},{12... | collective-permute-start | bytes 786440 | tf_op jit(solution)/shard_map/ppermute | solution.py:42
  71.3 19.0 %collective-permute-start.14 = (bf16[512,256]{1,0:T(8,128)(2,1)}, bf16[512,256]{1,0:T(8,128)(2,1)S(1)}, u32[]{:S(2)}, u32[]{:S(2)}) collective-permute-start(bf16[512,256]{1,0:T(8,128)(2,1)} %get-tuple-element.100), channel_id=1, source_target_pairs={{0,6},{2,0},{4,2},{6,4},{1,7},{3,1},{5,3},{7,5},{8,14},{10,8},{12,... | collective-permute-start | bytes 786440 | tf_op jit(solution)/shard_map/ppermute | solution.py:42
  72.6 32.5 %collective-permute-start.18 = (bf16[512,768]{1,0:T(8,128)(2,1)S(1)}, bf16[512,768]{1,0:T(8,128)(2,1)S(1)}, u32[]{:S(2)}, u32[]{:S(2)}) collective-permute-start(bf16[512,768]{1,0:T(8,128)(2,1)S(1)} %copy-done.41), channel_id=1, source_target_pairs={{0,1},{1,0},{2,3},{3,2},{4,5},{5,4},{6,7},{7,6},{8,9},{9,8},{10,11... | collective-permute-start | bytes 2359304 | tf_op jit(solution)/shard_map/ppermute | solution.py:42
  80.1 25.1 %collective-permute-start.19 = (bf16[512,768]{1,0:T(8,128)(2,1)}, bf16[512,768]{1,0:T(8,128)(2,1)}, u32[]{:S(2)}, u32[]{:S(2)}) collective-permute-start(bf16[512,768]{1,0:T(8,128)(2,1)} %refs_10_.3), channel_id=1, source_target_pairs={{0,1},{1,0},{2,3},{3,2},{4,5},{5,4},{6,7},{7,6},{8,9},{9,8},{10,11... | collective-permute-start | bytes 2359304 | tf_op jit(solution)/shard_map/ppermute | solution.py:42
  92.3 22.5 %copy-start.7 = (bf16[512,256]{1,0:T(8,128)(2,1)}, bf16[512,256]{1,0:T(8,128)(2,1)S(1)}, u32[]{:S(2)}) copy-start(bf16[512,256]{1,0:T(8,128)(2,1)S(1)} %get-tuple-element.167.refs_0_) | copy-start | bytes 786436
  92.3 12.9 %collective-permute-start.15 = (bf16[512,256]{1,0:T(8,128)(2,1)S(1)}, bf16[512,256]{1,0:T(8,128)(2,1)S(1)}, u32[]{:S(2)}, u32[]{:S(2)}) collective-permute-start(bf16[512,256]{1,0:T(8,128)(2,1)S(1)} %get-tuple-element.167.refs_0_), channel_id=1, source_target_pairs={{0,2},{2,4},{4,6},{6,0},{1,3},{3,5},{5,7},{7,1},{8,10},{10,12},{12... | collective-permute-start | bytes 786440 | tf_op jit(solution)/shard_map/ppermute | solution.py:42
  98.1 15.5 %collective-permute-start.16 = (bf16[512,256]{1,0:T(8,128)(2,1)S(1)}, bf16[512,256]{1,0:T(8,128)(2,1)S(1)}, u32[]{:S(2)}, u32[]{:S(2)}) collective-permute-start(bf16[512,256]{1,0:T(8,128)(2,1)S(1)} %get-tuple-element.167.refs_0_), channel_id=1, source_target_pairs={{0,4},{2,6},{4,0},{6,2},{1,5},{3,7},{5,1},{7,3},{8,12},{10,14},{12... | collective-permute-start | bytes 786440 | tf_op jit(solution)/shard_map/ppermute | solution.py:42
  98.2 16.7 %collective-permute-start.17 = (bf16[512,256]{1,0:T(8,128)(2,1)S(1)}, bf16[512,256]{1,0:T(8,128)(2,1)S(1)}, u32[]{:S(2)}, u32[]{:S(2)}) collective-permute-start(bf16[512,256]{1,0:T(8,128)(2,1)S(1)} %get-tuple-element.167.refs_0_), channel_id=1, source_target_pairs={{0,6},{2,0},{4,2},{6,4},{1,7},{3,1},{5,3},{7,5},{8,14},{10,8},{12,... | collective-permute-start | bytes 786440 | tf_op jit(solution)/shard_map/ppermute | solution.py:42
  124.0 14.3 %collective-permute-start.32 = (bf16[512,2304]{1,0:T(8,128)(2,1)}, bf16[512,2304]{1,0:T(8,128)(2,1)S(1)}, u32[]{:S(2)}, u32[]{:S(2)}) collective-permute-start(bf16[512,2304]{1,0:T(8,128)(2,1)} %get-tuple-element.125.delta_ref), channel_id=1, source_target_pairs={{0,1},{1,0},{2,3},{3,2},{4,5},{5,4},{6,7},{7,6},{8,9},{9,8},{10,11... | collective-permute-start | bytes 7077896 | tf_op jit(solution)/shard_map/ppermute | solution.py:42
  124.1 9.9 %collective-permute-start.31 = (bf16[512,512]{1,0:T(8,128)(2,1)}, bf16[512,512]{1,0:T(8,128)(2,1)S(1)}, u32[]{:S(2)}, u32[]{:S(2)}) collective-permute-start(bf16[512,512]{1,0:T(8,128)(2,1)} %get-tuple-element.124), channel_id=1, source_target_pairs={{0,1},{1,0},{2,3},{3,2},{4,5},{5,4},{6,7},{7,6},{8,9},{9,8},{10,11... | collective-permute-start | bytes 1572872 | tf_op jit(solution)/shard_map/ppermute | solution.py:42
  124.5 13.8 %collective-permute-start.30 = (bf16[512,512]{1,0:T(8,128)(2,1)}, bf16[512,512]{1,0:T(8,128)(2,1)S(1)}, u32[]{:S(2)}, u32[]{:S(2)}) collective-permute-start(bf16[512,512]{1,0:T(8,128)(2,1)} %get-tuple-element.122), channel_id=1, source_target_pairs={{0,1},{1,0},{2,3},{3,2},{4,5},{5,4},{6,7},{7,6},{8,9},{9,8},{10,11... | collective-permute-start | bytes 1572872 | tf_op jit(solution)/shard_map/ppermute | solution.py:42
  124.6 22.7 %collective-permute-start.21 = (bf16[512,256]{1,0:T(8,128)(2,1)}, bf16[512,256]{1,0:T(8,128)(2,1)S(1)}, u32[]{:S(2)}, u32[]{:S(2)}) collective-permute-start(bf16[512,256]{1,0:T(8,128)(2,1)} %get-tuple-element.104), channel_id=1, source_target_pairs={{0,2},{2,4},{4,6},{6,0},{1,3},{3,5},{5,7},{7,1},{8,10},{10,12},{12... | collective-permute-start | bytes 786440 | tf_op jit(solution)/shard_map/ppermute | solution.py:42
  130.6 21.2 %collective-permute-start.22 = (bf16[512,256]{1,0:T(8,128)(2,1)}, bf16[512,256]{1,0:T(8,128)(2,1)S(1)}, u32[]{:S(2)}, u32[]{:S(2)}) collective-permute-start(bf16[512,256]{1,0:T(8,128)(2,1)} %get-tuple-element.105), channel_id=1, source_target_pairs={{0,4},{2,6},{4,0},{6,2},{1,5},{3,7},{5,1},{7,3},{8,12},{10,14},{12... | collective-permute-start | bytes 786440 | tf_op jit(solution)/shard_map/ppermute | solution.py:42
  134.0 17.9 %collective-permute-start.23 = (bf16[512,256]{1,0:T(8,128)(2,1)}, bf16[512,256]{1,0:T(8,128)(2,1)S(1)}, u32[]{:S(2)}, u32[]{:S(2)}) collective-permute-start(bf16[512,256]{1,0:T(8,128)(2,1)} %get-tuple-element.106), channel_id=1, source_target_pairs={{0,6},{2,0},{4,2},{6,4},{1,7},{3,1},{5,3},{7,5},{8,14},{10,8},{12,... | collective-permute-start | bytes 786440 | tf_op jit(solution)/shard_map/ppermute | solution.py:42
  153.3 123.0 %all-gather.2.cloned.1.call-start = ((), (), s32[]{:S(2)}) async-start(), calls=%async_computation.2 | async-start | bytes 2949120 | tf_op jit(solution)/shard_map/all_gather | solution.py:1022
  155.5 23.6 %copy-start.38 = (bf16[512,256]{1,0:T(8,128)(2,1)}, bf16[512,256]{1,0:T(8,128)(2,1)S(1)}, u32[]{:S(2)}) copy-start(bf16[512,256]{1,0:T(8,128)(2,1)S(1)} %get-tuple-element.165.refs_4_) | copy-start | bytes 786436
  155.5 12.3 %collective-permute-start.24 = (bf16[512,256]{1,0:T(8,128)(2,1)S(1)}, bf16[512,256]{1,0:T(8,128)(2,1)S(1)}, u32[]{:S(2)}, u32[]{:S(2)}) collective-permute-start(bf16[512,256]{1,0:T(8,128)(2,1)S(1)} %get-tuple-element.165.refs_4_), channel_id=1, source_target_pairs={{0,2},{2,4},{4,6},{6,0},{1,3},{3,5},{5,7},{7,1},{8,10},{10,12},{12... | collective-permute-start | bytes 786440 | tf_op jit(solution)/shard_map/ppermute | solution.py:42
  160.9 17.3 %collective-permute-start.25 = (bf16[512,256]{1,0:T(8,128)(2,1)S(1)}, bf16[512,256]{1,0:T(8,128)(2,1)S(1)}, u32[]{:S(2)}, u32[]{:S(2)}) collective-permute-start(bf16[512,256]{1,0:T(8,128)(2,1)S(1)} %get-tuple-element.165.refs_4_), channel_id=1, source_target_pairs={{0,4},{2,6},{4,0},{6,2},{1,5},{3,7},{5,1},{7,3},{8,12},{10,14},{12... | collective-permute-start | bytes 786440 | tf_op jit(solution)/shard_map/ppermute | solution.py:42
  161.1 17.1 %collective-permute-start.26 = (bf16[512,256]{1,0:T(8,128)(2,1)S(1)}, bf16[512,256]{1,0:T(8,128)(2,1)S(1)}, u32[]{:S(2)}, u32[]{:S(2)}) collective-permute-start(bf16[512,256]{1,0:T(8,128)(2,1)S(1)} %get-tuple-element.165.refs_4_), channel_id=1, source_target_pairs={{0,6},{2,0},{4,2},{6,4},{1,7},{3,1},{5,3},{7,5},{8,14},{10,8},{12,... | collective-permute-start | bytes 786440 | tf_op jit(solution)/shard_map/ppermute | solution.py:42
  179.1 17.4 %collective-permute-start.27 = (bf16[512,256]{1,0:T(8,128)(2,1)}, bf16[512,256]{1,0:T(8,128)(2,1)S(1)}, u32[]{:S(2)}, u32[]{:S(2)}) collective-permute-start(bf16[512,256]{1,0:T(8,128)(2,1)} %get-tuple-element.112.refs_16_), channel_id=1, source_target_pairs={{0,2},{2,4},{4,6},{6,0},{1,3},{3,5},{5,7},{7,1},{8,10},{10,12},{12... | collective-permute-start | bytes 786440 | tf_op jit(solution)/shard_map/ppermute | solution.py:42
  185.1 13.8 %collective-permute-start.29 = (bf16[512,256]{1,0:T(8,128)(2,1)}, bf16[512,256]{1,0:T(8,128)(2,1)S(1)}, u32[]{:S(2)}, u32[]{:S(2)}) collective-permute-start(bf16[512,256]{1,0:T(8,128)(2,1)} %get-tuple-element.114), channel_id=1, source_target_pairs={{0,6},{2,0},{4,2},{6,4},{1,7},{3,1},{5,3},{7,5},{8,14},{10,8},{12,... | collective-permute-start | bytes 786440 | tf_op jit(solution)/shard_map/ppermute | solution.py:42
  207.6 1.8 collective-permute-start.33
  207.7 2.1 collective-permute-start.34
  218.5 12.3 %copy-start.61 = (bf16[528,256]{1,0:T(8,128)(2,1)S(1)}, bf16[528,256]{1,0:T(8,128)(2,1)}, u32[]{:S(2)}) copy-start(bf16[528,256]{1,0:T(8,128)(2,1)} %get-tuple-element.138) | copy-start | bytes 811012
  218.5 14.1 %copy-start.60 = (bf16[528,256]{1,0:T(8,128)(2,1)S(1)}, bf16[528,256]{1,0:T(8,128)(2,1)}, u32[]{:S(2)}) copy-start(bf16[528,256]{1,0:T(8,128)(2,1)} %get-tuple-element.139) | copy-start | bytes 811012
  218.5 3.5 %collective-permute-start.38 = (bf16[4,128,1024]{2,1,0:T(8,128)(2,1)}, bf16[4,128,1024]{2,1,0:T(8,128)(2,1)S(1)}, u32[]{:S(2)}, u32[]{:S(2)}) collective-permute-start(bf16[4,128,1024]{2,1,0:T(8,128)(2,1)} %get-tuple-element.143), channel_id=1, source_target_pairs={{0,1},{1,0},{2,3},{3,2},{4,5},{5,4},{6,7},{7,6},{8,9},{9,8},{10,11... | collective-permute-start | bytes 3145736 | tf_op jit(solution)/shard_map/ppermute | solution.py:42
  218.7 3.3 %collective-permute-start.39 = (bf16[4,128,512]{2,1,0:T(8,128)(2,1)S(1)}, bf16[4,128,512]{2,1,0:T(8,128)(2,1)S(1)}, u32[]{:S(2)}, u32[]{:S(2)}) collective-permute-start(bf16[4,128,512]{2,1,0:T(8,128)(2,1)S(1)} %copy-done.59), channel_id=1, source_target_pairs={{0,1},{1,0},{2,3},{3,2},{4,5},{5,4},{6,7},{7,6},{8,9},{9,8},{10,11... | collective-permute-start | bytes 1572872 | tf_op jit(solution)/shard_map/ppermute | solution.py:42
  223.2 29.8 %copy-start.54 = (bf16[512,256]{1,0:T(8,128)(2,1)S(1)}, bf16[512,256]{1,0:T(8,128)(2,1)}, u32[]{:S(2)}) copy-start(bf16[512,256]{1,0:T(8,128)(2,1)} %get-tuple-element.113) | copy-start | bytes 786436
  226.7 18.3 %collective-permute-start.40 = (bf16[2,128,768]{2,1,0:T(8,128)(2,1)}, bf16[2,128,768]{2,1,0:T(8,128)(2,1)S(1)}, u32[]{:S(2)}, u32[]{:S(2)}) collective-permute-start(bf16[2,128,768]{2,1,0:T(8,128)(2,1)} %get-tuple-element.146), channel_id=1, source_target_pairs={{0,8},{8,0},{16,24},{24,16},{1,9},{9,1},{17,25},{25,17},{2,10},{10... | collective-permute-start | bytes 1179656 | tf_op jit(solution)/shard_map/ppermute | solution.py:75
  228.2 19.3 %collective-permute-start.41 = (bf16[2,128,768]{2,1,0:T(8,128)(2,1)}, bf16[2,128,768]{2,1,0:T(8,128)(2,1)S(1)}, u32[]{:S(2)}, u32[]{:S(2)}) collective-permute-start(bf16[2,128,768]{2,1,0:T(8,128)(2,1)} %get-tuple-element.148), channel_id=1, source_target_pairs={{0,16},{8,24},{16,0},{24,8},{1,17},{9,25},{17,1},{25,9},{2,18},{10... | collective-permute-start | bytes 1179656 | tf_op jit(solution)/shard_map/ppermute | solution.py:75
  229.7 23.2 %collective-permute-start.35 = (bf16[528,256]{1,0:T(8,128)(2,1)S(1)}, bf16[528,256]{1,0:T(8,128)(2,1)S(1)}, u32[]{:S(2)}, u32[]{:S(2)}) collective-permute-start(bf16[528,256]{1,0:T(8,128)(2,1)S(1)} %copy-done.62), channel_id=1, source_target_pairs={{0,2},{2,4},{4,6},{6,0},{1,3},{3,5},{5,7},{7,1},{8,10},{10,12},{12... | collective-permute-start | bytes 811016 | tf_op jit(solution)/shard_map/ppermute | solution.py:42
  230.8 22.4 %collective-permute-start.36 = (bf16[528,256]{1,0:T(8,128)(2,1)S(1)}, bf16[528,256]{1,0:T(8,128)(2,1)S(1)}, u32[]{:S(2)}, u32[]{:S(2)}) collective-permute-start(bf16[528,256]{1,0:T(8,128)(2,1)S(1)} %copy-done.61), channel_id=1, source_target_pairs={{0,4},{2,6},{4,0},{6,2},{1,5},{3,7},{5,1},{7,3},{8,12},{10,14},{12... | collective-permute-start | bytes 811016 | tf_op jit(solution)/shard_map/ppermute | solution.py:42
  232.6 20.6 %collective-permute-start.37 = (bf16[528,256]{1,0:T(8,128)(2,1)S(1)}, bf16[528,256]{1,0:T(8,128)(2,1)S(1)}, u32[]{:S(2)}, u32[]{:S(2)}) collective-permute-start(bf16[528,256]{1,0:T(8,128)(2,1)S(1)} %copy-done.60), channel_id=1, source_target_pairs={{0,6},{2,0},{4,2},{6,4},{1,7},{3,1},{5,3},{7,5},{8,14},{10,8},{12,... | collective-permute-start | bytes 811016 | tf_op jit(solution)/shard_map/ppermute | solution.py:42
  250.8 6.6 %collective-permute-start.42 = (bf16[128,768]{1,0:T(8,128)(2,1)}, bf16[128,768]{1,0:T(8,128)(2,1)S(1)}, u32[]{:S(2)}, u32[]{:S(2)}) collective-permute-start(bf16[128,768]{1,0:T(8,128)(2,1)} %get-tuple-element.150), channel_id=1, source_target_pairs={{0,16},{8,24},{16,0},{24,8},{1,17},{9,25},{17,1},{25,9},{2,18},{10... | collective-permute-start | bytes 589832 | tf_op jit(solution)/shard_map/ppermute | solution.py:75
  252.9 5.9 %collective-permute-start.43 = (bf16[128,768]{1,0:T(8,128)(2,1)}, bf16[128,768]{1,0:T(8,128)(2,1)S(1)}, u32[]{:S(2)}, u32[]{:S(2)}) collective-permute-start(bf16[128,768]{1,0:T(8,128)(2,1)} %get-tuple-element.152), channel_id=1, source_target_pairs={{0,8},{8,0},{16,24},{24,16},{1,9},{9,1},{17,25},{25,17},{2,10},{10... | collective-permute-start | bytes 589832 | tf_op jit(solution)/shard_map/ppermute | solution.py:75
  253.0 17.9 %collective-permute-start.28 = (bf16[512,256]{1,0:T(8,128)(2,1)S(1)}, bf16[512,256]{1,0:T(8,128)(2,1)S(1)}, u32[]{:S(2)}, u32[]{:S(2)}) collective-permute-start(bf16[512,256]{1,0:T(8,128)(2,1)S(1)} %copy-done.54), channel_id=1, source_target_pairs={{0,4},{2,6},{4,0},{6,2},{1,5},{3,7},{5,1},{7,3},{8,12},{10,14},{12... | collective-permute-start | bytes 786440 | tf_op jit(solution)/shard_map/ppermute | solution.py:42
  265.5 1.4 collective-permute-start.44
  267.6 5.8 %collective-permute-start.45 = (f32[8,256]{1,0:T(8,128)S(1)}, f32[8,256]{1,0:T(8,128)S(1)}, u32[]{:S(2)}, u32[]{:S(2)}) collective-permute-start(f32[8,256]{1,0:T(8,128)S(1)} %add.182), channel_id=1, source_target_pairs={{0,8},{8,16},{16,24},{24,0},{1,9},{9,17},{17,25},{25,1},{2,10},{10... | collective-permute-start | bytes 24584 | tf_op jit(solution)/shard_map/ppermute | solution.py:42
  267.9 7.4 %collective-permute-start.46 = (f32[8,256]{1,0:T(8,128)S(1)}, f32[8,256]{1,0:T(8,128)S(1)}, u32[]{:S(2)}, u32[]{:S(2)}) collective-permute-start(f32[8,256]{1,0:T(8,128)S(1)} %add.182), channel_id=1, source_target_pairs={{0,16},{8,24},{16,0},{24,8},{1,17},{9,25},{17,1},{25,9},{2,18},{10... | collective-permute-start | bytes 24584 | tf_op jit(solution)/shard_map/ppermute | solution.py:42
  268.1 7.1 %collective-permute-start.47 = (f32[8,256]{1,0:T(8,128)S(1)}, f32[8,256]{1,0:T(8,128)S(1)}, u32[]{:S(2)}, u32[]{:S(2)}) collective-permute-start(f32[8,256]{1,0:T(8,128)S(1)} %add.182), channel_id=1, source_target_pairs={{0,24},{8,0},{16,8},{24,16},{1,25},{9,1},{17,9},{25,17},{2,26},{10... | collective-permute-start | bytes 24584 | tf_op jit(solution)/shard_map/ppermute | solution.py:42
  271.7 12.1 %collective-permute-start.48 = (bf16[128,1536]{1,0:T(8,128)(2,1)S(1)}, bf16[128,1536]{1,0:T(8,128)(2,1)S(1)}, u32[]{:S(2)}, u32[]{:S(2)}) collective-permute-start(bf16[128,1536]{1,0:T(8,128)(2,1)S(1)} %copy-done.53), channel_id=1, source_target_pairs={{0,8},{8,0},{16,24},{24,16},{1,9},{9,1},{17,25},{25,17},{2,10},{10... | collective-permute-start | bytes 1179656 | tf_op jit(solution)/shard_map/ppermute | solution.py:75
  271.9 11.8 %collective-permute-start.49 = (bf16[128,1536]{1,0:T(8,128)(2,1)S(1)}, bf16[128,1536]{1,0:T(8,128)(2,1)S(1)}, u32[]{:S(2)}, u32[]{:S(2)}) collective-permute-start(bf16[128,1536]{1,0:T(8,128)(2,1)S(1)} %copy-done.53), channel_id=1, source_target_pairs={{0,16},{8,24},{16,0},{24,8},{1,17},{9,25},{17,1},{25,9},{2,18},{10... | collective-permute-start | bytes 1179656 | tf_op jit(solution)/shard_map/ppermute | solution.py:75
  273.4 18.2 %collective-permute-start.50 = (bf16[128,1536]{1,0:T(8,128)(2,1)S(1)}, bf16[128,1536]{1,0:T(8,128)(2,1)S(1)}, u32[]{:S(2)}, u32[]{:S(2)}) collective-permute-start(bf16[128,1536]{1,0:T(8,128)(2,1)S(1)} %copy-done.53), channel_id=1, source_target_pairs={{0,24},{8,16},{16,8},{24,0},{1,25},{9,17},{17,9},{25,1},{2,26},{10... | collective-permute-start | bytes 1179656 | tf_op jit(solution)/shard_map/ppermute | solution.py:75
  (54 other events, 194.9 us)
Sparse Core Ops, SparseCore 0:
  153.4 40.4 reduce-scatter.1
  207.7 44.5 all-gather.1
